TPU v7x, 32 devices: a whole 2x2x4 slice. The times are simulated.
32 devices in a mesh: dp: 4 (over x, core), mp: 2 (over y), adp: 4 (over z).
Axes of the slice: x: 2, y: 2, z: 4, core: 2. Of those that a mesh axis runs over, the one named last changes fastest.
Arguments:
- inputs: bfloat16 [2, 16, 1024, 1024], P(None, ('dp', 'adp'), 'mp'), may hold values from -6 to 6
- memory: bfloat16 [2, 16, 1024, 1024], P(None, ('dp', 'adp'), 'mp'), may hold values from -6 to 6
- src_lengths: int32 [2, 16, 1], P(None, ('dp', 'adp')), may hold values from 1 to 1024, as said below
- self_qkv: bfloat16 [3, 1024, 1024], P(None, 'dp', 'mp'), may hold values from -0.1875 to 0.1875
- self_proj: bfloat16 [1024, 1024], P('mp', 'dp'), may hold values from -1.5 to 1.5
- cross_qkv: bfloat16 [3, 1024, 1024], P(None, 'dp', 'mp'), may hold values from -0.1875 to 0.1875
- cross_proj: bfloat16 [1024, 1024], P('mp', 'dp'), may hold values from -1.5 to 1.5
- ffn_in: bfloat16 [1024, 4096], P('dp', 'mp'), may hold values from -0.1875 to 0.1875
- ffn_out: bfloat16 [4096, 1024], P('mp', 'dp'), may hold values from -0.09375 to 0.09375
- norm_gains: bfloat16 [3, 1024], replicated, may hold values from 0.5 to 1.5
- prefix: bfloat16 [2, 30, 1024], P(None, None, 'mp'), may hold values from -6 to 6
- adapter_down: bfloat16 [1024, 512], P('dp', 'adp'), may hold values from -0.1875 to 0.1875
- adapter_up: bfloat16 [512, 1024], P('adp', 'dp'), may hold values from -0.125 to 0.125
- cotangent: bfloat16 [2, 16, 1024, 1024], P(None, ('dp', 'adp'), 'mp'), may hold values from -6 to 6
Outputs:
- result: bfloat16 [2, 16, 1024, 1024], P(None, ('dp', 'adp'), 'mp')
- input_grad: bfloat16 [2, 16, 1024, 1024], P(None, ('dp', 'adp'), 'mp')
- memory_grad: bfloat16 [2, 16, 1024, 1024], P(None, ('dp', 'adp'), 'mp')
- prefix_grad: float32 [2, 30, 1024], P(None, None, 'mp')
- adapter_down_grad: float32 [1024, 512], P(('dp', 'mp'), 'adp')
- adapter_up_grad: float32 [512, 1024], P('adp', ('dp', 'mp'))
Inputs may be any that keep to these rules, and one draw needn't show every extreme that they name: `src_lengths`: in each micro-batch one sequence of one block has all 1024 source rows valid.
All inputs are finite; a program needn't handle non-finite values.
Results may differ from a plain program's by a relative error of at most 0.028.
Values may be sent and summed in bfloat16 or wider, within the bound.
A program may use at most 448 MiB of HBM per device.

v0:
```python
import jax
import jax.numpy as jnp
from jax import lax
from jax.sharding import PartitionSpec as P

HEAD_DIM = 64
PREFIX_LEN = 30
SEQ_LEN = 1024
SRC_MAX = 1024
SEQS_BLK = 1
MICRO = 2


eps = 1e-05


def exact_gelu(values):
    return jax.nn.gelu(values, approximate=False)


def norm_forward(residual, gain_row):
    centered = residual - jnp.mean(residual, axis=-1, keepdims=True)
    inv_std = lax.rsqrt(jnp.mean(centered * centered, axis=-1, keepdims=True) + eps)
    return centered * inv_std * gain_row


def norm_backward(upstream, residual, gain_row):
    centered = residual - jnp.mean(residual, axis=-1, keepdims=True)
    inv_std = lax.rsqrt(jnp.mean(centered * centered, axis=-1, keepdims=True) + eps)
    normed = centered * inv_std
    scaled = upstream * gain_row
    inner_mean = jnp.mean(scaled * normed, axis=-1, keepdims=True)
    return inv_std * (scaled - jnp.mean(scaled, axis=-1, keepdims=True) - normed * inner_mean)


def gelu_back(pre_act, upstream):
    return jax.vjp(exact_gelu, pre_act)[1](upstream)[0]


def matmul(left_mat, right_mat):
    return jnp.dot(left_mat, right_mat, preferred_element_type=jnp.float32)


def matmul_nt(left_mat, right_mat):
    return lax.dot_general(
        left_mat, right_mat, (((1,), (1,)), ((), ())), preferred_element_type=jnp.float32
    )


def matmul_tn(left_mat, right_mat):
    return lax.dot_general(
        left_mat, right_mat, (((0,), (0,)), ((), ())), preferred_element_type=jnp.float32
    )


def to_heads(rows_mat, seq_count, length):
    heads_here = rows_mat.shape[-1] // HEAD_DIM
    return rows_mat.reshape(seq_count, length, heads_here, HEAD_DIM).transpose(0, 2, 1, 3)


def from_heads(split_mat):
    seq_count, heads_here, length, head_width = split_mat.shape
    return split_mat.transpose(0, 2, 1, 3).reshape(seq_count * length, heads_here * head_width)


def causal_allowed():
    query_pos = lax.broadcasted_iota(jnp.int32, (SEQ_LEN, PREFIX_LEN + SEQ_LEN), 0)
    key_pos = lax.broadcasted_iota(jnp.int32, (SEQ_LEN, PREFIX_LEN + SEQ_LEN), 1)
    return (key_pos < PREFIX_LEN) | (key_pos - PREFIX_LEN <= query_pos)


def source_allowed(length):
    return lax.broadcasted_iota(jnp.int32, (SEQ_LEN, SRC_MAX), 1) < length


def attend_forward(queries, keys_all, values_all, allowed):
    scores = jnp.einsum("hqd,hkd->hqk", queries, keys_all, preferred_element_type=jnp.float32)
    scores = jnp.where(allowed, scores, -1e30)
    top_score = jnp.max(scores, axis=-1, keepdims=True)
    expo_scores = jnp.exp(scores - top_score)
    row_total = jnp.sum(expo_scores, axis=-1, keepdims=True)
    weights_low = (expo_scores / row_total).astype(jnp.bfloat16)
    mixed = jnp.einsum("hqk,hkd->hqd", weights_low, values_all, preferred_element_type=jnp.float32)
    return (mixed.astype(jnp.bfloat16), top_score + jnp.log(row_total))


def attend_backward(queries, keys_all, values_all, allowed, log_total, grad_out):
    scores = jnp.einsum("hqd,hkd->hqk", queries, keys_all, preferred_element_type=jnp.float32)
    scores = jnp.where(allowed, scores, -1e30)
    soft_weights = jnp.exp(scores - log_total)
    grad_soft = jnp.einsum("hqd,hkd->hqk", grad_out, values_all, preferred_element_type=jnp.float32)
    inner_sum = jnp.sum(soft_weights * grad_soft, axis=-1, keepdims=True)
    grad_scores = (soft_weights * (grad_soft - inner_sum)).astype(jnp.bfloat16)
    grad_query = jnp.einsum(
        "hqk,hkd->hqd", grad_scores, keys_all, preferred_element_type=jnp.float32
    )
    grad_keys = jnp.einsum("hqk,hqd->hkd", grad_scores, queries, preferred_element_type=jnp.float32)
    grad_values = jnp.einsum(
        "hqk,hqd->hkd",
        soft_weights.astype(jnp.bfloat16),
        grad_out,
        preferred_element_type=jnp.float32,
    )
    return (grad_query, grad_keys, grad_values)


def gather_rows(rows_low):
    return lax.all_gather(rows_low, "mp", axis=0, tiled=True)


def reduce_rows(term_fn, own_count):
    return lax.psum_scatter(
        term_fn(jnp.int32(0), own_count * lax.axis_size("mp")).astype(jnp.bfloat16),
        "mp",
        scatter_dimension=0,
        tiled=True,
    ).astype(jnp.float32)


def gather_adapter(rows_low):
    return lax.all_gather(rows_low, "adp", axis=0, tiled=True)


def reduce_adapter(term_fn, own_count):
    return lax.psum_scatter(
        term_fn(jnp.int32(0), own_count * lax.axis_size("adp")).astype(jnp.bfloat16),
        "adp",
        scatter_dimension=0,
        tiled=True,
    ).astype(jnp.float32)


def reduce_prefix(grad_prefix):
    return lax.psum(grad_prefix, ("dp", "adp"))


def reduce_adapter_grads(grad_down, grad_up):
    return (
        lax.psum_scatter(grad_down, ("dp", "mp"), scatter_dimension=0, tiled=True),
        lax.psum_scatter(grad_up, ("dp", "mp"), scatter_dimension=1, tiled=True),
    )


def shards(
    inputs,
    memory,
    src_lengths,
    self_qkv,
    self_proj,
    cross_qkv,
    cross_proj,
    ffn_in,
    ffn_out,
    norm_gains,
    prefix,
    adapter_down,
    adapter_up,
    cotangent,
):
    scale = HEAD_DIM ** (-0.5)
    own_rows = inputs.shape[2]
    gains = norm_gains.astype(jnp.float32)
    causal = causal_allowed()
    prefix_heads = to_heads(prefix, 2, PREFIX_LEN)
    prefix_keys = prefix_heads[0]
    prefix_values = prefix_heads[1]
    results = []
    input_grads = []
    memory_grads = []
    prefix_acc = None
    down_acc = None
    up_acc = None
    for micro_index in range(MICRO):
        self_w, self_o, cross_w, cross_o, down_w, up_w = (
            lax.all_gather(self_qkv, "dp", axis=1, tiled=True),
            lax.all_gather(self_proj, "dp", axis=1, tiled=True),
            lax.all_gather(cross_qkv, "dp", axis=1, tiled=True),
            lax.all_gather(cross_proj, "dp", axis=1, tiled=True),
            lax.all_gather(adapter_down, "dp", axis=0, tiled=True),
            lax.all_gather(adapter_up, "dp", axis=1, tiled=True),
        )
        ffn_first, ffn_second = (
            lax.all_gather(ffn_in, "dp", axis=0, tiled=True),
            lax.all_gather(ffn_out, "dp", axis=1, tiled=True),
        )
        x_rows = inputs[micro_index, 0]
        lengths_here = src_lengths[micro_index, 0]
        x_full = gather_rows(x_rows)
        mem_full = lax.all_gather(memory[micro_index, 0], "mp", axis=0, tiled=True)
        projected = jnp.einsum("td,cde->cte", x_full, self_w, preferred_element_type=jnp.float32)
        query_self = to_heads((projected[0] * scale).astype(jnp.bfloat16), SEQS_BLK, SEQ_LEN)
        key_self = to_heads(projected[1].astype(jnp.bfloat16), SEQS_BLK, SEQ_LEN)
        value_self = to_heads(projected[2].astype(jnp.bfloat16), SEQS_BLK, SEQ_LEN)

        def self_forward(packed):
            query_seq, key_seq, value_seq = packed
            keys_all = jnp.concatenate([prefix_keys, key_seq], axis=1)
            values_all = jnp.concatenate([prefix_values, value_seq], axis=1)
            return attend_forward(query_seq, keys_all, values_all, causal)

        attn_self, lse_self = lax.map(self_forward, (query_self, key_self, value_self))
        attn_rows = from_heads(attn_self)

        def self_term(first_row, row_count):
            return matmul(attn_rows, self_o)

        resid_one = x_rows.astype(jnp.float32) + reduce_rows(self_term, own_rows)
        normed_one = norm_forward(resid_one, gains[0])
        one_full = gather_rows(normed_one.astype(jnp.bfloat16))
        cross_query = to_heads(
            (matmul(one_full, cross_w[0]) * scale).astype(jnp.bfloat16), SEQS_BLK, SEQ_LEN
        )
        memory_proj = jnp.einsum(
            "td,cde->cte", mem_full, cross_w[1:], preferred_element_type=jnp.float32
        )
        cross_keys = to_heads(memory_proj[0].astype(jnp.bfloat16), SEQS_BLK, SRC_MAX)
        cross_values = to_heads(memory_proj[1].astype(jnp.bfloat16), SEQS_BLK, SRC_MAX)

        def cross_forward(packed):
            query_seq, key_seq, value_seq, length = packed
            return attend_forward(query_seq, key_seq, value_seq, source_allowed(length))

        attn_cross, lse_cross = lax.map(
            cross_forward, (cross_query, cross_keys, cross_values, lengths_here)
        )
        cross_rows = from_heads(attn_cross)

        def cross_term(first_row, row_count):
            return matmul(cross_rows, cross_o)

        resid_two = normed_one + reduce_rows(cross_term, own_rows)
        normed_two = norm_forward(resid_two, gains[1])
        two_low = normed_two.astype(jnp.bfloat16)
        two_full = gather_rows(two_low)
        hidden_pre = matmul(two_full, ffn_first)
        hidden_act = exact_gelu(hidden_pre).astype(jnp.bfloat16)

        def ffn_term(first_row, row_count):
            return matmul(hidden_act, ffn_second)

        ffn_rows = reduce_rows(ffn_term, own_rows)
        adapter_in = gather_adapter(two_low)
        adapter_pre = matmul(adapter_in, down_w)
        adapter_act = exact_gelu(adapter_pre).astype(jnp.bfloat16)

        def adapter_term(first_row, row_count):
            return matmul(adapter_act, up_w)

        adapter_rows = reduce_adapter(adapter_term, own_rows)
        resid_three = normed_two + ffn_rows + 4.0 * adapter_rows
        results.append(norm_forward(resid_three, gains[2]).astype(jnp.bfloat16))
        grad_three = norm_backward(
            cotangent[micro_index, 0].astype(jnp.float32), resid_three, gains[2]
        )
        grad_branch = grad_three.astype(jnp.bfloat16)
        grad_adapter = gather_adapter(grad_branch) * 4.0
        up_term = matmul_tn(adapter_act, grad_adapter)
        grad_adapter_pre = gelu_back(adapter_pre, matmul_nt(grad_adapter, up_w)).astype(
            jnp.bfloat16
        )
        down_term = matmul_tn(adapter_in, grad_adapter_pre)

        def adapter_back_term(first_row, row_count):
            return matmul_nt(grad_adapter_pre, down_w)

        adapter_back = reduce_adapter(adapter_back_term, own_rows)
        branch_full = gather_rows(grad_branch)
        grad_pre = gelu_back(hidden_pre, matmul_nt(branch_full, ffn_second)).astype(jnp.bfloat16)

        def ffn_back_term(first_row, row_count):
            return matmul_nt(grad_pre, ffn_first)

        ffn_back = reduce_rows(ffn_back_term, own_rows)
        grad_mid = norm_backward(grad_three + ffn_back + adapter_back, resid_two, gains[1])
        mid_full = gather_rows(grad_mid.astype(jnp.bfloat16))
        grad_cross_out = to_heads(
            matmul_nt(mid_full, cross_o).astype(jnp.bfloat16), SEQS_BLK, SEQ_LEN
        )

        def cross_backward(packed):
            query_seq, key_seq, value_seq, lse_seq, grad_seq, length = packed
            return attend_backward(
                query_seq, key_seq, value_seq, source_allowed(length), lse_seq, grad_seq
            )

        cross_gq, cross_gk, cross_gv = lax.map(
            cross_backward,
            (cross_query, cross_keys, cross_values, lse_cross, grad_cross_out, lengths_here),
        )
        cross_gq_rows = from_heads(cross_gq).astype(jnp.bfloat16) * scale

        def cross_query_term(first_row, row_count):
            return matmul_nt(cross_gq_rows, cross_w[0])

        grad_one = grad_mid + reduce_rows(cross_query_term, own_rows)
        memory_stack = jnp.stack(
            [from_heads(cross_gk).astype(jnp.bfloat16), from_heads(cross_gv).astype(jnp.bfloat16)]
        )
        memory_grads.append(
            lax.psum_scatter(
                jnp.einsum(
                    "cte,cde->td", memory_stack, cross_w[1:], preferred_element_type=jnp.float32
                ).astype(jnp.bfloat16),
                "mp",
                scatter_dimension=0,
                tiled=True,
            )
        )
        grad_first = norm_backward(grad_one, resid_one, gains[0])
        first_full = gather_rows(grad_first.astype(jnp.bfloat16))
        grad_self_out = to_heads(
            matmul_nt(first_full, self_o).astype(jnp.bfloat16), SEQS_BLK, SEQ_LEN
        )

        def self_backward(packed):
            query_seq, key_seq, value_seq, lse_seq, grad_seq = packed
            keys_all = jnp.concatenate([prefix_keys, key_seq], axis=1)
            values_all = jnp.concatenate([prefix_values, value_seq], axis=1)
            return attend_backward(query_seq, keys_all, values_all, causal, lse_seq, grad_seq)

        self_gq, self_gk, self_gv = lax.map(
            self_backward, (query_self, key_self, value_self, lse_self, grad_self_out)
        )
        prefix_key_grad = from_heads(jnp.sum(self_gk[:, :, :PREFIX_LEN], axis=0)[None])
        prefix_value_grad = from_heads(jnp.sum(self_gv[:, :, :PREFIX_LEN], axis=0)[None])
        prefix_term = jnp.stack([prefix_key_grad, prefix_value_grad])
        self_stack = jnp.stack(
            [
                from_heads(self_gq).astype(jnp.bfloat16) * scale,
                from_heads(self_gk[:, :, PREFIX_LEN:]).astype(jnp.bfloat16),
                from_heads(self_gv[:, :, PREFIX_LEN:]).astype(jnp.bfloat16),
            ]
        )

        def input_term(first_row, row_count):
            return jnp.einsum("cte,cde->td", self_stack, self_w, preferred_element_type=jnp.float32)

        input_grads.append((grad_first + reduce_rows(input_term, own_rows)).astype(jnp.bfloat16))
        prefix_term = reduce_prefix(prefix_term)
        down_term, up_term = reduce_adapter_grads(down_term, up_term)
        prefix_acc = prefix_term if prefix_acc is None else prefix_acc + prefix_term
        down_acc = down_term if down_acc is None else down_acc + down_term
        up_acc = up_term if up_acc is None else up_acc + up_term
    return (
        jnp.stack(results)[:, None],
        jnp.stack(input_grads)[:, None],
        jnp.stack(memory_grads)[:, None],
        prefix_acc,
        down_acc,
        up_acc,
    )


def solution(mesh):
    return jax.shard_map(
        shards,
        mesh=mesh,
        in_specs=(
            P(None, ("dp", "adp"), "mp", None),
            P(None, ("dp", "adp"), "mp", None),
            P(None, ("dp", "adp"), None),
            P(None, "dp", "mp"),
            P("mp", "dp"),
            P(None, "dp", "mp"),
            P("mp", "dp"),
            P("dp", "mp"),
            P("mp", "dp"),
            P(),
            P(None, None, "mp"),
            P("dp", "adp"),
            P("adp", "dp"),
            P(None, ("dp", "adp"), "mp", None),
        ),
        out_specs=(
            P(None, ("dp", "adp"), "mp", None),
            P(None, ("dp", "adp"), "mp", None),
            P(None, ("dp", "adp"), "mp", None),
            P(None, None, "mp"),
            P(("dp", "mp"), "adp"),
            P("adp", ("dp", "mp")),
        ),
        check_vma=False,
    )
```

profile of v0, /device:TPU:0, one launch (start us, length us, event | category | flops | bytes accessed | tf_op | source)
XLA Modules:
  0.0 2194.2 jit_solution(3264003197662309088)
XLA Ops:
  14.4 31.9 %all-gather.69.cloned.1.call-done = bf16[1,1,1024,1024]{3,2,1,0:T(8,128)(2,1)} async-done(((bf16[1,1,512,1024]{3,2,1,0:T(8,128)(2,1)}), bf16[1,1,1024,1024]{3,2,1,0:T(8,128)(2,1)}) %all-gather.69.cloned.1.call-update) | async-done | bytes 2097168 | tf_op jit(solution)/shard_map/all_gather | solution.py:108
  46.3 31.1 %all-gather.29.cloned.1.call-done = bf16[3,1024,512]{1,2,0:T(8,128)(2,1)} async-done(((bf16[3,256,512]{1,2,0:T(8,128)(2,1)}), bf16[3,1024,512]{1,2,0:T(8,128)(2,1)}) %all-gather.29.cloned.1.call-update) | async-done | bytes 3145744 | tf_op jit(solution)/shard_map/all_gather | solution.py:175
  83.9 15.3 fusion.209
  112.6 15.7 fusion.128
  140.7 17.0 fusion.211
  195.0 25.2 %reduce-scatter.29.cloned.1.call-done = bf16[512,1024]{1,0:T(8,128)(2,1)} async-done(((bf16[1024,1024]{1,0:T(8,128)(2,1)}), bf16[512,1024]{1,0:T(8,128)(2,1)}) %reduce-scatter.29.cloned.1.call-update) | async-done | bytes 1048592 | tf_op jit(solution)/shard_map/reduce_scatter | solution.py:112
  226.6 28.9 %all-gather.71.cloned.1.call-done = bf16[1,1,1024,1024]{3,2,1,0:T(8,128)(2,1)} async-done(((bf16[1,1,512,1024]{3,2,1,0:T(8,128)(2,1)}), bf16[1,1,1024,1024]{3,2,1,0:T(8,128)(2,1)}) %all-gather.71.cloned.1.call-update) | async-done | bytes 2097168 | tf_op jit(solution)/shard_map/all_gather | solution.py:189
  255.5 30.5 %all-gather.35.cloned.1.call-done = bf16[3,1024,512]{1,2,0:T(8,128)(2,1)} async-done(((bf16[3,256,512]{1,2,0:T(8,128)(2,1)}), bf16[3,1024,512]{1,2,0:T(8,128)(2,1)}) %all-gather.35.cloned.1.call-update) | async-done | bytes 3145744 | tf_op jit(solution)/shard_map/all_gather | solution.py:177
  292.1 29.2 %all-gather.33.cloned.1.call-done = bf16[1024,1024]{1,0:T(8,128)(2,1)} async-done(((bf16[512,1024]{1,0:T(8,128)(2,1)}), bf16[1024,1024]{1,0:T(8,128)(2,1)}) %all-gather.33.cloned.1.call-update) | async-done | bytes 2097168 | tf_op jit(solution)/shard_map/all_gather | solution.py:108
  372.4 31.4 %reduce-scatter.23.cloned.1.call-done = bf16[512,1024]{1,0:T(8,128)(2,1)} async-done(((bf16[1024,1024]{1,0:T(8,128)(2,1)}), bf16[512,1024]{1,0:T(8,128)(2,1)}) %reduce-scatter.23.cloned.1.call-update) | async-done | bytes 1048592 | tf_op jit(solution)/shard_map/reduce_scatter | solution.py:112
  412.2 26.1 %all-gather.75.cloned.1.call-done = bf16[1,1,1024,1024]{3,2,1,0:T(8,128)(2,1)} async-done(((bf16[1,1,512,1024]{3,2,1,0:T(8,128)(2,1)}), bf16[1,1,1024,1024]{3,2,1,0:T(8,128)(2,1)}) %all-gather.75.cloned.1.call-update) | async-done | bytes 2097168 | tf_op jit(solution)/shard_map/all_gather | solution.py:189
  443.2 30.5 %all-gather.47.cloned.1.call-done = bf16[1024,1024]{1,0:T(8,128)(2,1)} async-done(((bf16[512,1024]{1,0:T(8,128)(2,1)}), bf16[1024,1024]{1,0:T(8,128)(2,1)}) %all-gather.47.cloned.1.call-update) | async-done | bytes 2097168 | tf_op jit(solution)/shard_map/all_gather | solution.py:108
  522.9 21.5 all-gather.39.cloned.1.call-done
  544.3 24.9 %fusion.24 = (f32[1024,2048]{1,0:T(8,128)}, f32[1024,2048]{1,0:T(8,128)}) fusion(bf16[1024,1024]{1,0:T(8,128)(2,1)} %all-gather.39.cloned.1.call-done, bf16[1024,2048]{1,0:T(8,128)(2,1)} %all-gather.41.cloned.1.call-done), kind=kOutput, calls=%fused_computation.46 | convolution fusion | flops 4424990720 | bytes 23068672 | tf_op jit(solution)/shard_map/dot_general | solution.py:41
  605.6 57.6 %all-gather.45.cloned.1.call-done = bf16[2048,1024]{1,0:T(8,128)(2,1)} async-done(((bf16[512,1024]{1,0:T(8,128)(2,1)}), bf16[2048,1024]{1,0:T(8,128)(2,1)}) %all-gather.45.cloned.1.call-update) | async-done | bytes 4194320 | tf_op jit(solution)/shard_map/all_gather | solution.py:121
  673.6 22.8 %reduce-scatter.31.cloned.1.call-done = bf16[512,1024]{1,0:T(8,128)(2,1)} async-done(((bf16[1024,1024]{1,0:T(8,128)(2,1)}), bf16[512,1024]{1,0:T(8,128)(2,1)}) %reduce-scatter.31.cloned.1.call-update) | async-done | bytes 1048592 | tf_op jit(solution)/shard_map/reduce_scatter | solution.py:112
  700.0 31.0 %reduce-scatter.25.cloned.1.call-done = bf16[512,1024]{1,0:T(8,128)(2,1)} async-done(((bf16[1024,1024]{1,0:T(8,128)(2,1)}), bf16[512,1024]{1,0:T(8,128)(2,1)}) %reduce-scatter.25.cloned.1.call-update) | async-done | bytes 1048592 | tf_op jit(solution)/shard_map/reduce_scatter | solution.py:112
  731.0 79.0 %reduce-scatter.27.cloned.1.call-done = bf16[512,1024]{1,0:T(8,128)(2,1)} async-done(((bf16[2048,1024]{1,0:T(8,128)(2,1)}), bf16[512,1024]{1,0:T(8,128)(2,1)}) %reduce-scatter.27.cloned.1.call-update) | async-done | bytes 1048592 | tf_op jit(solution)/shard_map/reduce_scatter | solution.py:125
  815.8 32.8 %all-gather.49.cloned.1.call-done = bf16[1024,1024]{1,0:T(8,128)(2,1)} async-done(((bf16[512,1024]{1,0:T(8,128)(2,1)}), bf16[1024,1024]{1,0:T(8,128)(2,1)}) %all-gather.49.cloned.1.call-update) | async-done | bytes 2097168 | tf_op jit(solution)/shard_map/all_gather | solution.py:108
  848.6 23.1 %fusion.25 = (f32[1024,2048]{1,0:T(8,128)S(1)}, f32[1024,2048]{1,0:T(8,128)S(1)}) fusion(bf16[1024,1024]{1,0:T(8,128)(2,1)} %all-gather.49.cloned.1.call-done, bf16[1024,2048]{1,0:T(8,128)(2,1)} %all-gather.41.cloned.1.call-done), kind=kOutput, calls=%fused_computation.47 | convolution fusion | flops 4424990720 | bytes 23068672 | tf_op jit(solution)/shard_map/dot_general | solution.py:41
  883.5 47.5 %all-gather.51.cloned.1.call-done = bf16[2048,1024]{1,0:T(8,128)(2,1)} async-done(((bf16[512,1024]{1,0:T(8,128)(2,1)}), bf16[2048,1024]{1,0:T(8,128)(2,1)}) %all-gather.51.cloned.1.call-update) | async-done | bytes 4194320 | tf_op jit(solution)/shard_map/all_gather | solution.py:121
  943.8 19.8 reduce-scatter.33.cloned.1.call-done
  963.6 79.0 %reduce-scatter.35.cloned.1.call-done = bf16[512,1024]{1,0:T(8,128)(2,1)} async-done(((bf16[2048,1024]{1,0:T(8,128)(2,1)}), bf16[512,1024]{1,0:T(8,128)(2,1)}) %reduce-scatter.35.cloned.1.call-update) | async-done | bytes 1048592 | tf_op jit(solution)/shard_map/reduce_scatter | solution.py:125
  1051.7 31.8 %all-gather.53.cloned.1.call-done = bf16[1024,1024]{1,0:T(8,128)(2,1)} async-done(((bf16[512,1024]{1,0:T(8,128)(2,1)}), bf16[1024,1024]{1,0:T(8,128)(2,1)}) %all-gather.53.cloned.1.call-update) | async-done | bytes 2097168 | tf_op jit(solution)/shard_map/all_gather | solution.py:108
  1083.5 17.9 fusion.104
  1101.5 64.2 %all-gather.55.cloned.1.call-done = bf16[2048,1024]{1,0:T(8,128)(2,1)} async-done(((bf16[512,1024]{1,0:T(8,128)(2,1)}), bf16[2048,1024]{1,0:T(8,128)(2,1)}) %all-gather.55.cloned.1.call-update) | async-done | bytes 4194320 | tf_op jit(solution)/shard_map/all_gather | solution.py:121
  1175.5 23.3 %all-gather.61.cloned.1.call-done = bf16[1024,1024]{1,0:T(8,128)(2,1)} async-done(((bf16[512,1024]{1,0:T(8,128)(2,1)}), bf16[1024,1024]{1,0:T(8,128)(2,1)}) %all-gather.61.cloned.1.call-update) | async-done | bytes 2097168 | tf_op jit(solution)/shard_map/all_gather | solution.py:108
  1198.8 17.9 fusion.103
  1216.8 64.4 %all-gather.63.cloned.1.call-done = bf16[2048,1024]{1,0:T(8,128)(2,1)} async-done(((bf16[512,1024]{1,0:T(8,128)(2,1)}), bf16[2048,1024]{1,0:T(8,128)(2,1)}) %all-gather.63.cloned.1.call-update) | async-done | bytes 4194320 | tf_op jit(solution)/shard_map/all_gather | solution.py:121
  1290.8 23.0 %reduce-scatter.37.cloned.1.call-done = bf16[512,1024]{1,0:T(8,128)(2,1)} async-done(((bf16[1024,1024]{1,0:T(8,128)(2,1)}), bf16[512,1024]{1,0:T(8,128)(2,1)}) %reduce-scatter.37.cloned.1.call-update) | async-done | bytes 1048592 | tf_op jit(solution)/shard_map/reduce_scatter | solution.py:112
  1313.8 79.0 %reduce-scatter.39.cloned.1.call-done = bf16[512,1024]{1,0:T(8,128)(2,1)} async-done(((bf16[2048,1024]{1,0:T(8,128)(2,1)}), bf16[512,1024]{1,0:T(8,128)(2,1)}) %reduce-scatter.39.cloned.1.call-update) | async-done | bytes 1048592 | tf_op jit(solution)/shard_map/reduce_scatter | solution.py:125
  1399.8 27.7 %reduce-scatter.45.cloned.1.call-done = bf16[512,1024]{1,0:T(8,128)(2,1)} async-done(((bf16[1024,1024]{1,0:T(8,128)(2,1)}), bf16[512,1024]{1,0:T(8,128)(2,1)}) %reduce-scatter.45.cloned.1.call-update) | async-done | bytes 1048592 | tf_op jit(solution)/shard_map/reduce_scatter | solution.py:112
  1427.5 79.2 %reduce-scatter.47.cloned.1.call-done = bf16[512,1024]{1,0:T(8,128)(2,1)} async-done(((bf16[2048,1024]{1,0:T(8,128)(2,1)}), bf16[512,1024]{1,0:T(8,128)(2,1)}) %reduce-scatter.47.cloned.1.call-update) | async-done | bytes 1048592 | tf_op jit(solution)/shard_map/reduce_scatter | solution.py:125
  1513.8 28.0 %all-gather.57.cloned.1.call-done = bf16[1024,1024]{1,0:T(8,128)(2,1)} async-done(((bf16[512,1024]{1,0:T(8,128)(2,1)}), bf16[1024,1024]{1,0:T(8,128)(2,1)}) %all-gather.57.cloned.1.call-update) | async-done | bytes 2097168 | tf_op jit(solution)/shard_map/all_gather | solution.py:108
  1544.9 23.8 %multiply_reduce_fusion.3 = (f32[8,1024]{1,0:T(8,128)S(1)}, f32[8,1024,1024]{1,2,0:T(8,128)}) fusion(f32[8,1024,1024]{1,2,0:T(8,128)} %get-tuple-element.312, f32[8,1024]{1,0:T(8,128)S(1)} %log_add_fusion.3, pred[1024]{0:T(1024)(128)(4,1)S(1)} %copy-done.107, bf16[8,1024,64]{1,2,0:T(8,128)(2,1)S(1)} %bitcast.430, bf16[8,1024,64]{1,2,0:T(8,128)(2,1)S(1)} %bitcast.413), kind=kOutput, calls=%fused_computation.14 | convolution fusion | flops 1107288064 | bytes 69272576 | tf_op jit(solution)/shard_map/while/body/eval_jaxpr/hqd,hkd->hqk/dot_general | solution.py:91
  1568.7 27.6 %multiply_convert_fusion.3 = bf16[8,1024,1024]{1,2,0:T(8,128)(2,1)} fusion(f32[8,1024,1024]{1,2,0:T(8,128)} %get-tuple-element.326, f32[8,1024,1024]{1,2,0:T(8,128)} %get-tuple-element.312, f32[8,1024]{1,0:T(8,128)S(1)} %get-tuple-element.325, f32[8,1024]{1,0:T(8,128)S(1)} %log_add_fusion.3, pred[1024]{0:T(1024)(128)(4,1)S(1)} %copy-done.107), kind=kLoop, calls=%fused_computation.13 | loop fusion | flops 41943040 | bytes 83952640 | tf_op jit(solution)/shard_map/while/body/eval_jaxpr/convert_element_type | solution.py:93
  1612.6 24.5 %multiply_reduce_fusion.2 = (f32[8,1024]{1,0:T(8,128)S(1)}, f32[8,1024,1024]{1,2,0:T(8,128)}) fusion(f32[8,1024,1024]{1,2,0:T(8,128)} %get-tuple-element.314, f32[8,1024]{1,0:T(8,128)S(1)} %log_add_fusion.1, pred[1024]{0:T(1024)(128)(4,1)S(1)} %copy-done.109, bf16[8,1024,64]{1,2,0:T(8,128)(2,1)S(1)} %bitcast.428, bf16[8,1024,64]{1,2,0:T(8,128)(2,1)S(1)} %bitcast.415), kind=kOutput, calls=%fused_computation.11 | convolution fusion | flops 1107288064 | bytes 69272576 | tf_op jit(solution)/shard_map/while/body/eval_jaxpr/hqd,hkd->hqk/dot_general | solution.py:91
  1637.0 27.7 %multiply_convert_fusion.2 = bf16[8,1024,1024]{1,2,0:T(8,128)(2,1)} fusion(f32[8,1024,1024]{1,2,0:T(8,128)} %get-tuple-element.324, f32[8,1024,1024]{1,2,0:T(8,128)} %get-tuple-element.314, f32[8,1024]{1,0:T(8,128)S(1)} %get-tuple-element.323, f32[8,1024]{1,0:T(8,128)S(1)} %log_add_fusion.1, pred[1024]{0:T(1024)(128)(4,1)S(1)} %copy-done.109), kind=kLoop, calls=%fused_computation.10 | loop fusion | flops 41943040 | bytes 83952640 | tf_op jit(solution)/shard_map/while/body/eval_jaxpr/convert_element_type | solution.py:93
  1677.6 31.8 %reduce-scatter.49.cloned.1.call-done = bf16[512,1024]{1,0:T(8,128)(2,1)} async-done(((bf16[1024,1024]{1,0:T(8,128)(2,1)}), bf16[512,1024]{1,0:T(8,128)(2,1)}) %reduce-scatter.49.cloned.1.call-update) | async-done | bytes 1048592 | tf_op jit(solution)/shard_map/reduce_scatter | solution.py:112
  1719.3 15.5 fusion.119
  1784.1 22.7 %multiply_reduce_fusion.1 = (f32[8,1024]{1,0:T(8,128)S(1)}, f32[8,1024,1054]{1,2,0:T(8,128)}) fusion(f32[8,1024,1054]{1,2,0:T(8,128)} %get-tuple-element.306, f32[8,1024]{1,0:T(8,128)S(1)} %log_add_fusion.2, bf16[8,1024,64]{1,2,0:T(8,128)(2,1)S(1)} %bitcast.406, bf16[8,30,64]{1,2,0:T(8,128)(2,1)S(1)} %copy-done.59, bf16[8,1024,64]{1,2,0:T(8,128)(2,1)S(1)} %bitcast.411), kind=kOutput, calls=%fused_computation.4 | convolution fusion | flops 1133252608 | bytes 71268352 | tf_op jit(solution)/shard_map/while/body/eval_jaxpr/hqd,hkd->hqk/dot_general | solution.py:91
  1806.7 29.6 %multiply_convert_fusion.1 = bf16[8,1024,1054]{1,2,0:T(8,128)(2,1)} fusion(f32[8,1024,1054]{1,2,0:T(8,128)} %get-tuple-element.330, f32[8,1024,1054]{1,2,0:T(8,128)} %get-tuple-element.306, f32[8,1024]{1,0:T(8,128)S(1)} %get-tuple-element.329, f32[8,1024]{1,0:T(8,128)S(1)} %log_add_fusion.2), kind=kLoop, calls=%fused_computation.3 | loop fusion | flops 34537472 | bytes 86409216 | tf_op jit(solution)/shard_map/while/body/eval_jaxpr/convert_element_type | solution.py:93
  1884.4 24.2 %multiply_reduce_fusion = (f32[8,1024]{1,0:T(8,128)S(1)}, f32[8,1024,1054]{1,2,0:T(8,128)}) fusion(f32[8,1024,1054]{1,2,0:T(8,128)} %get-tuple-element.310, f32[8,1024]{1,0:T(8,128)S(1)} %log_add_fusion, bf16[8,1024,64]{1,2,0:T(8,128)(2,1)S(1)} %bitcast.404, bf16[8,30,64]{1,2,0:T(8,128)(2,1)} %copy-done.58, bf16[8,1024,64]{1,2,0:T(8,128)(2,1)} %bitcast.409), kind=kOutput, calls=%fused_computation.1 | convolution fusion | flops 1133252608 | bytes 71268352 | tf_op jit(solution)/shard_map/while/body/eval_jaxpr/hqd,hkd->hqk/dot_general | solution.py:91
  1908.6 29.0 %multiply_convert_fusion = bf16[8,1024,1054]{1,2,0:T(8,128)(2,1)} fusion(f32[8,1024,1054]{1,2,0:T(8,128)} %get-tuple-element.328, f32[8,1024,1054]{1,2,0:T(8,128)} %get-tuple-element.310, f32[8,1024]{1,0:T(8,128)S(1)} %get-tuple-element.327, f32[8,1024]{1,0:T(8,128)S(1)} %log_add_fusion), kind=kLoop, calls=%fused_computation | loop fusion | flops 34537472 | bytes 86409216 | tf_op jit(solution)/shard_map/while/body/eval_jaxpr/convert_element_type | solution.py:93
  1937.6 15.1 fusion.54
  2022.8 34.6 %reduce-scatter.57.cloned.1.call-done = f32[128,128]{1,0:T(8,128)} async-done(((f32[1024,128]{1,0:T(8,128)}), f32[128,128]{1,0:T(8,128)}) %reduce-scatter.57.cloned.1.call-update) | async-done | bytes 65552 | tf_op jit(solution)/shard_map/reduce_scatter | solution.py:139
  2057.4 38.1 %reduce-scatter.59.cloned.1.call-done = f32[128,128]{1,0:T(8,128)} async-done(((f32[128,1024]{1,0:T(8,128)}), f32[128,128]{1,0:T(8,128)}) %reduce-scatter.59.cloned.1.call-update) | async-done | bytes 65552 | tf_op jit(solution)/shard_map/reduce_scatter | solution.py:140
  2095.5 90.3 %all-reduce.2.cloned.1.call-done = f32[2,30,512]{2,0,1:T(2,128)} async-done(((f32[2,30,512]{2,0,1:T(2,128)}), f32[2,30,512]{2,0,1:T(2,128)}) %all-reduce.2.cloned.1.call-update) | async-done | bytes 122896 | tf_op jit(solution)/shard_map/psum | solution.py:134
  (494 shorter events, 535.0 us)
Async XLA Ops:
  7.2 39.1 %all-gather.69.cloned.1.call-start = ((), (), s32[]{:S(2)}) async-start(), calls=%async_computation.58 | async-start | bytes 3145728 | tf_op jit(solution)/shard_map/all_gather | solution.py:108
  10.3 67.1 %all-gather.29.cloned.1.call-start = ((), (), s32[]{:S(2)}) async-start(), calls=%async_computation.20 | async-start | bytes 3932160 | tf_op jit(solution)/shard_map/all_gather | solution.py:175
  11.6 116.8 %all-gather.73.cloned.1.call-start = ((), (), s32[]{:S(2)}) async-start(), calls=%async_computation.60 | async-start | bytes 3145728 | tf_op jit(solution)/shard_map/all_gather | solution.py:108
  12.3 123.6 %all-gather.31.cloned.1.call-start = ((), (), s32[]{:S(2)}) async-start(), calls=%async_computation.21 | async-start | bytes 1310720 | tf_op jit(solution)/shard_map/all_gather | solution.py:176
  12.9 180.2 %reduce-scatter.21.cloned.1.call-start = ((), (), s32[]{:S(2)}) async-start(), calls=%async_computation.22 | async-start | bytes 3145728 | tf_op jit(solution)/shard_map/reduce_scatter | solution.py:112
  140.6 79.6 %reduce-scatter.29.cloned.1.call-start = ((), (), s32[]{:S(2)}) async-start(), calls=%async_computation.33 | async-start | bytes 3145728 | tf_op jit(solution)/shard_map/reduce_scatter | solution.py:112
  188.0 67.5 %all-gather.71.cloned.1.call-start = ((), (), s32[]{:S(2)}) async-start(), calls=%async_computation.59 | async-start | bytes 3145728 | tf_op jit(solution)/shard_map/all_gather | solution.py:189
  191.2 94.8 %all-gather.35.cloned.1.call-start = ((), (), s32[]{:S(2)}) async-start(), calls=%async_computation.24 | async-start | bytes 3932160 | tf_op jit(solution)/shard_map/all_gather | solution.py:177
  192.5 128.8 %all-gather.33.cloned.1.call-start = ((), (), s32[]{:S(2)}) async-start(), calls=%async_computation.23 | async-start | bytes 3145728 | tf_op jit(solution)/shard_map/all_gather | solution.py:108
  193.1 210.6 %copy-start.75 = (f32[1,1024]{1,0:T(1,128)}, f32[1,1024]{1,0:T(1,128)S(1)}, u32[]{:S(2)}) copy-start(f32[1,1024]{1,0:T(1,128)S(1)} %get-tuple-element.287) | copy-start | bytes 12292
  193.1 216.2 %copy-start.73 = (f32[1,1024]{1,0:T(1,128)}, f32[1,1024]{1,0:T(1,128)S(1)}, u32[]{:S(2)}) copy-start(f32[1,1024]{1,0:T(1,128)S(1)} %get-tuple-element.286) | copy-start | bytes 12292
  195.0 208.7 %copy-start.90 = (f32[512]{0:T(512)}, f32[512]{0:T(512)S(1)}, u32[]{:S(2)}) copy-start(f32[512]{0:T(512)S(1)} %broadcast_multiply_fusion.17) | copy-start | bytes 6148
  224.5 143.0 %all-gather.37.cloned.1.call-start = ((), (), s32[]{:S(2)}) async-start(), calls=%async_computation.25 | async-start | bytes 1310720 | tf_op jit(solution)/shard_map/all_gather | solution.py:178
  225.1 178.6 %reduce-scatter.23.cloned.1.call-start = ((), (), s32[]{:S(2)}) async-start(), calls=%async_computation.26 | async-start | bytes 3145728 | tf_op jit(solution)/shard_map/reduce_scatter | solution.py:112
  371.7 66.6 %all-gather.75.cloned.1.call-start = ((), (), s32[]{:S(2)}) async-start(), calls=%async_computation.61 | async-start | bytes 3145728 | tf_op jit(solution)/shard_map/all_gather | solution.py:189
  372.3 101.4 %all-gather.47.cloned.1.call-start = ((), (), s32[]{:S(2)}) async-start(), calls=%async_computation.34 | async-start | bytes 3145728 | tf_op jit(solution)/shard_map/all_gather | solution.py:108
  407.4 115.4 %all-gather.41.cloned.1.call-start = ((), (), s32[]{:S(2)}) async-start(), calls=%async_computation.28 | async-start | bytes 5242880 | tf_op jit(solution)/shard_map/all_gather | solution.py:183
  408.0 136.3 %all-gather.39.cloned.1.call-start = ((), (), s32[]{:S(2)}) async-start(), calls=%async_computation.27 | async-start | bytes 3145728 | tf_op jit(solution)/shard_map/all_gather | solution.py:108
  410.7 170.2 %all-gather.43.cloned.1.call-start = ((), (), s32[]{:S(2)}) async-start(), calls=%async_computation.29 | async-start | bytes 5242880 | tf_op jit(solution)/shard_map/all_gather | solution.py:184
  411.3 251.9 %all-gather.45.cloned.1.call-start = ((), (), s32[]{:S(2)}) async-start(), calls=%async_computation.31 | async-start | bytes 5242880 | tf_op jit(solution)/shard_map/all_gather | solution.py:121
  443.2 253.1 %reduce-scatter.31.cloned.1.call-start = ((), (), s32[]{:S(2)}) async-start(), calls=%async_computation.35 | async-start | bytes 3145728 | tf_op jit(solution)/shard_map/reduce_scatter | solution.py:112
  522.4 208.6 %reduce-scatter.25.cloned.1.call-start = ((), (), s32[]{:S(2)}) async-start(), calls=%async_computation.30 | async-start | bytes 3145728 | tf_op jit(solution)/shard_map/reduce_scatter | solution.py:112
  593.7 216.3 %reduce-scatter.27.cloned.1.call-start = ((), (), s32[]{:S(2)}) async-start(), calls=%async_computation.32 | async-start | bytes 5242880 | tf_op jit(solution)/shard_map/reduce_scatter | solution.py:125
  673.5 175.1 %all-gather.49.cloned.1.call-start = ((), (), s32[]{:S(2)}) async-start(), calls=%async_computation.36 | async-start | bytes 3145728 | tf_op jit(solution)/shard_map/all_gather | solution.py:108
  814.8 116.2 %all-gather.51.cloned.1.call-start = ((), (), s32[]{:S(2)}) async-start(), calls=%async_computation.38 | async-start | bytes 5242880 | tf_op jit(solution)/shard_map/all_gather | solution.py:121
  815.6 148.1 %reduce-scatter.33.cloned.1.call-start = ((), (), s32[]{:S(2)}) async-start(), calls=%async_computation.37 | async-start | bytes 3145728 | tf_op jit(solution)/shard_map/reduce_scatter | solution.py:112
  883.4 159.3 %reduce-scatter.35.cloned.1.call-start = ((), (), s32[]{:S(2)}) async-start(), calls=%async_computation.39 | async-start | bytes 5242880 | tf_op jit(solution)/shard_map/reduce_scatter | solution.py:125
  941.2 142.3 %all-gather.53.cloned.1.call-start = ((), (), s32[]{:S(2)}) async-start(), calls=%async_computation.40 | async-start | bytes 3145728 | tf_op jit(solution)/shard_map/all_gather | solution.py:108
  1049.7 116.0 %all-gather.55.cloned.1.call-start = ((), (), s32[]{:S(2)}) async-start(), calls=%async_computation.42 | async-start | bytes 5242880 | tf_op jit(solution)/shard_map/all_gather | solution.py:121
  1050.3 148.5 %all-gather.61.cloned.1.call-start = ((), (), s32[]{:S(2)}) async-start(), calls=%async_computation.48 | async-start | bytes 3145728 | tf_op jit(solution)/shard_map/all_gather | solution.py:108
  1050.9 230.3 %all-gather.63.cloned.1.call-start = ((), (), s32[]{:S(2)}) async-start(), calls=%async_computation.50 | async-start | bytes 5242880 | tf_op jit(solution)/shard_map/all_gather | solution.py:121
  1051.7 262.2 %reduce-scatter.37.cloned.1.call-start = ((), (), s32[]{:S(2)}) async-start(), calls=%async_computation.41 | async-start | bytes 3145728 | tf_op jit(solution)/shard_map/reduce_scatter | solution.py:112
  1101.5 291.4 %reduce-scatter.39.cloned.1.call-start = ((), (), s32[]{:S(2)}) async-start(), calls=%async_computation.43 | async-start | bytes 5242880 | tf_op jit(solution)/shard_map/reduce_scatter | solution.py:125
  1175.3 252.2 %reduce-scatter.45.cloned.1.call-start = ((), (), s32[]{:S(2)}) async-start(), calls=%async_computation.49 | async-start | bytes 3145728 | tf_op jit(solution)/shard_map/reduce_scatter | solution.py:112
  1216.7 290.0 %reduce-scatter.47.cloned.1.call-start = ((), (), s32[]{:S(2)}) async-start(), calls=%async_computation.51 | async-start | bytes 5242880 | tf_op jit(solution)/shard_map/reduce_scatter | solution.py:125
  1290.8 251.0 %all-gather.57.cloned.1.call-start = ((), (), s32[]{:S(2)}) async-start(), calls=%async_computation.44 | async-start | bytes 3145728 | tf_op jit(solution)/shard_map/all_gather | solution.py:108
  1399.5 210.1 %all-gather.65.cloned.1.call-start = ((), (), s32[]{:S(2)}) async-start(), calls=%async_computation.52 | async-start | bytes 3145728 | tf_op jit(solution)/shard_map/all_gather | solution.py:108
  1513.7 163.9 %reduce-scatter.41.cloned.1.call-start = ((), (), s32[]{:S(2)}) async-start(), calls=%async_computation.45 | async-start | bytes 3145728 | tf_op jit(solution)/shard_map/reduce_scatter | solution.py:112
  1609.2 100.2 %reduce-scatter.49.cloned.1.call-start = ((), (), s32[]{:S(2)}) async-start(), calls=%async_computation.53 | async-start | bytes 3145728 | tf_op jit(solution)/shard_map/reduce_scatter | solution.py:112
  1677.6 103.3 %all-gather.59.cloned.1.call-start = ((), (), s32[]{:S(2)}) async-start(), calls=%async_computation.46 | async-start | bytes 3145728 | tf_op jit(solution)/shard_map/all_gather | solution.py:108
  1718.4 162.9 %all-gather.67.cloned.1.call-start = ((), (), s32[]{:S(2)}) async-start(), calls=%async_computation.54 | async-start | bytes 3145728 | tf_op jit(solution)/shard_map/all_gather | solution.py:108
  1719.1 283.2 %reduce-scatter.53.cloned.1.call-start = ((), (), s32[]{:S(2)}) async-start(), calls=%async_computation.56 | async-start | bytes 3145728 | tf_op jit(solution)/shard_map/reduce_scatter | solution.py:300
  1750.2 252.1 %reduce-scatter.55.cloned.1.call-start = ((), (), s32[]{:S(2)}) async-start(), calls=%async_computation.57 | async-start | bytes 3145728 | tf_op jit(solution)/shard_map/reduce_scatter | solution.py:300
  1780.4 234.4 %reduce-scatter.43.cloned.1.call-start = ((), (), s32[]{:S(2)}) async-start(), calls=%async_computation.47 | async-start | bytes 3145728 | tf_op jit(solution)/shard_map/reduce_scatter | solution.py:112
  1881.2 138.6 %reduce-scatter.51.cloned.1.call-start = ((), (), s32[]{:S(2)}) async-start(), calls=%async_computation.55 | async-start | bytes 3145728 | tf_op jit(solution)/shard_map/reduce_scatter | solution.py:112
  1987.7 69.7 %reduce-scatter.57.cloned.1.call-start = ((), (), s32[]{:S(2)}) async-start(), calls=%async_computation.63 | async-start | bytes 589824 | tf_op jit(solution)/shard_map/reduce_scatter | solution.py:139
  1993.6 101.9 %reduce-scatter.59.cloned.1.call-start = ((), (), s32[]{:S(2)}) async-start(), calls=%async_computation.64 | async-start | bytes 589824 | tf_op jit(solution)/shard_map/reduce_scatter | solution.py:140
  1999.2 186.7 %all-reduce.2.cloned.1.call-start = ((), (), s32[]{:S(2)}) async-start(), calls=%async_computation.62 | async-start | bytes 245760 | tf_op jit(solution)/shard_map/psum | solution.py:134
  (117 other events, 3630.3 us)
Sparse Core Ops, SparseCore 0:
  10.5 35.8 all-gather.68
  48.4 28.9 all-gather.28
  79.5 33.1 all-gather.72
  114.1 16.8 all-gather.30
  140.7 31.9 reduce-scatter.20
  188.1 32.1 reduce-scatter.28
  222.3 33.0 all-gather.70
  257.0 28.9 all-gather.34
  288.1 33.1 all-gather.32
  322.7 16.8 all-gather.36
  371.9 31.8 reduce-scatter.22
  405.2 33.1 all-gather.74
  440.5 33.1 all-gather.46
  475.2 34.4 all-gather.40
  511.2 33.1 all-gather.38
  545.8 35.0 all-gather.42
  582.4 80.7 all-gather.44
  665.9 30.3 reduce-scatter.30
  699.1 31.8 reduce-scatter.24
  733.2 76.7 reduce-scatter.26
  815.0 33.6 all-gather.48
  850.2 80.7 all-gather.50
  933.2 30.3 reduce-scatter.32
  965.9 76.7 reduce-scatter.34
  1049.8 33.6 all-gather.52
  1084.9 80.7 all-gather.54
  1167.1 31.6 all-gather.60
  1200.4 80.7 all-gather.62
  1283.4 30.3 reduce-scatter.36
  1316.1 76.7 reduce-scatter.38
  1395.1 32.3 reduce-scatter.44
  1429.9 76.7 reduce-scatter.46
  1508.1 33.6 all-gather.56
  1543.9 33.1 all-gather.64
  1609.3 31.8 reduce-scatter.40
  1677.7 31.6 reduce-scatter.48
  1718.5 33.1 all-gather.58
  1753.2 33.1 all-gather.66
  1788.4 31.8 reduce-scatter.52
  1823.3 31.8 reduce-scatter.54
  1881.3 31.9 reduce-scatter.42
  1987.8 31.8 reduce-scatter.50
  2023.2 34.1 reduce-scatter.56
  2061.4 34.1 reduce-scatter.58
  2099.4 86.4 all-reduce.1
where the time goes:
time: 2210 us; the launch traced here: 2190 us
  waiting for transfers between devices  1290 us (58%)
  matrix products  581 us (26%)
  other arithmetic  234 us (11%)
  local copies, waits for them, and re-layouts  53.9 us (2%)
    reduce_scatter x4, waiting for transfers between devices, reduce_adapter(): lax.psum_scatter(term_fn(jnp.int32(0), own_count * lax.axis_size('adp'))....  316 us
    all_gather x4, waiting for transfers between devices, gather_adapter(): return lax.all_gather(rows_low, 'adp', axis=0, tiled=True)  234 us
    all_gather x12, waiting for transfers between devices, gather_rows(): return lax.all_gather(rows_low, 'mp', axis=0, tiled=True)  229 us
    reduce_scatter x12, waiting for transfers between devices, reduce_rows(): lax.psum_scatter(term_fn(jnp.int32(0), own_count * lax.axis_size('mp')).a...  215 us
    convert_element_type x4, other arithmetic, attend_backward(): grad_scores = (soft_weights * (grad_soft - inner_sum)).astype(jnp.bfloat16)  114 us
    dot_general x14, matrix products, matmul(): return jnp.dot(left_mat, right_mat, preferred_element_type=jnp.float32)  106 us
    dot_general x4, matrix products, attend_backward(): jnp.einsum('hqd,hkd->hqk', grad_out, values_all, preferred_element_type=j...  95.2 us
    psum x1, waiting for transfers between devices, reduce_prefix(): return lax.psum(grad_prefix, ('dp', 'adp'))  90.3 us
  transfers between devices with their start and end apart: 45, of which 33 were waited for; matrix products, arithmetic and copies ran while one was open for 37% of the time, Pallas kernels for 0%

commit v1 on v0

--- a/solution.py
+++ b/solution.py
@@ -1,6 +1,11 @@
+import functools
+import math
+
 import jax
 import jax.numpy as jnp
 from jax import lax
+from jax.experimental import pallas as pl
+from jax.experimental.pallas import tpu as pltpu
 from jax.sharding import PartitionSpec as P
 
 HEAD_DIM = 64
@@ -351,9 +356,571 @@
     )
 
 
+F32 = jnp.float32
+BF = jnp.bfloat16
+EPS = 1e-05
+LOG2E = 1.4426950408889634
+
+BQF = 512
+BQ = 512
+PRE = 32
+VMEM_BYTES = 60 * 2**20
+NEG = -1e30
+LN2 = 0.6931471805599453
+
+
+def dot_mm(a, b, ca, cb):
+    return lax.dot_general(a, b, (((ca,), (cb,)), ((), ())), preferred_element_type=jnp.float32)
+
+
+def pick_head(h, mat):
+    rows = lax.broadcasted_iota(jnp.int32, mat.shape, 0)
+    return jnp.where((rows // HEAD_DIM) == h, mat, jnp.zeros_like(mat))
+
+
+def attn_fwd_body(causal, n_ref, q_ref, k_ref, v_ref, pk_ref, pvt_ref, a_ref, p_ref, pp_ref, l_ref):
+    t = q_ref.shape[0]
+    s = k_ref.shape[0]
+    nb = t // BQF
+    qt = q_ref[...].T
+    vt = v_ref[...].T
+    ones = jnp.ones((16, s), jnp.bfloat16)
+    work = [(h, j) for h in range(2) for j in range(nb)]
+
+    def scores(h, j):
+        kk = (j + 1) * BQF if causal else s
+        qb = pick_head(h, qt[:, j * BQF:(j + 1) * BQF])
+        st = dot_mm(k_ref[:kk], qb, 1, 0)
+        return st, dot_mm(pk_ref[...], qb, 1, 0) if causal else None
+
+    res = {}
+    ahead = scores(*work[0])
+    for w, (h, j) in enumerate(work):
+        st, sp = ahead
+        if w + 1 < len(work):
+            ahead = scores(*work[w + 1])
+        kk = st.shape[0]
+        js = slice(j * BQF, (j + 1) * BQF)
+        if causal:
+            krow = lax.broadcasted_iota(jnp.int32, (BQF, BQF), 0)
+            qcol = lax.broadcasted_iota(jnp.int32, (BQF, BQF), 1)
+            diag = jnp.where(krow <= qcol, st[kk - BQF:], NEG)
+            st = jnp.concatenate([st[:kk - BQF], diag], axis=0) if kk > BQF else diag
+            prow = lax.broadcasted_iota(jnp.int32, sp.shape, 0)
+            sp = jnp.where(prow < n_ref[0], sp, NEG)
+            m = jnp.maximum(jnp.max(st, axis=0, keepdims=True), jnp.max(sp, axis=0, keepdims=True))
+            pp = jnp.exp2(sp - m).astype(jnp.bfloat16)
+            pp_ref[h, :, js] = pp
+        else:
+            krow = lax.broadcasted_iota(jnp.int32, st.shape, 0)
+            st = jnp.where(krow < n_ref[0], st, NEG)
+            m = jnp.max(st, axis=0, keepdims=True)
+        p = jnp.exp2(st - m).astype(jnp.bfloat16)
+        p_ref[h, :kk, js] = p
+        hs = slice(h * HEAD_DIM, (h + 1) * HEAD_DIM)
+        ot = dot_mm(jnp.concatenate([vt[hs, :kk], ones[:, :kk]], axis=0), p, 1, 0)
+        if causal:
+            ot += dot_mm(jnp.concatenate([pvt_ref[hs], ones[:, :PRE]], axis=0), pp, 1, 0)
+        il = 1.0 / ot[HEAD_DIM:HEAD_DIM + 1]
+        res[h, j] = (ot[:HEAD_DIM] * il, il)
+    for h in range(2):
+        l_ref[0, h:h + 1] = jnp.concatenate([res[h, j][1] for j in range(nb)], axis=1)
+    at = jnp.concatenate([jnp.concatenate([res[h, j][0] for j in range(nb)], axis=1) for h in range(2)], axis=0)
+    a_ref[...] = at.astype(jnp.bfloat16).T
+
+
+def attn_fwd(n, q, k, v, pk=None, pvt=None):
+    t, w = q.shape
+    s = k.shape[0]
+    pairs = w // 128
+    causal = pk is not None
+    if not causal:
+        pk = jnp.zeros((PRE, w), jnp.bfloat16)
+        pvt = jnp.zeros((w, PRE), jnp.bfloat16)
+    col = lambda g: (0, g)
+    lead = lambda g: (g, 0, 0)
+    bf = jnp.bfloat16
+    return pl.pallas_call(
+        functools.partial(attn_fwd_body, causal),
+        grid=(pairs,),
+        in_specs=[
+            pl.BlockSpec(memory_space=pltpu.SMEM),
+            pl.BlockSpec((t, 128), col), pl.BlockSpec((s, 128), col), pl.BlockSpec((s, 128), col),
+            pl.BlockSpec((PRE, 128), col), pl.BlockSpec((128, PRE), lambda g: (g, 0)),
+        ],
+        out_specs=[
+            pl.BlockSpec((t, 128), col), pl.BlockSpec((2, s, t), lead),
+            pl.BlockSpec((2, PRE, t), lead), pl.BlockSpec((1, 2, t), lead),
+        ],
+        out_shape=[
+            jax.ShapeDtypeStruct((t, w), bf), jax.ShapeDtypeStruct((2 * pairs, s, t), bf),
+            jax.ShapeDtypeStruct((2 * pairs, PRE, t), bf), jax.ShapeDtypeStruct((pairs, 2, t), jnp.float32),
+        ],
+        compiler_params=pltpu.CompilerParams(vmem_limit_bytes=VMEM_BYTES),
+        cost_estimate=pl.CostEstimate(
+            flops=24 * t * s * w, bytes_accessed=4 * t * s * pairs, transcendentals=t * s * 2 * pairs),
+    )(n, q, k, v, pk, pvt)
+
+
+def attn_bwd_body(causal, q_ref, k_ref, v_ref, a_ref, da_ref, l_ref, p_ref, pp_ref, pk_ref, pv_ref,
+                  dq_ref, dk_ref, dv_ref, dpk_ref, dpv_ref):
+    t = q_ref.shape[0]
+    s = k_ref.shape[0]
+    nb = t // BQ
+    qt = q_ref[...].T
+    kt = k_ref[...].T
+    dat = da_ref[...].T.astype(jnp.float32)
+    prod = dat * a_ref[...].T.astype(jnp.float32)
+    pkt = pk_ref[...].T
+    work = [(h, j) for h in range(2) for j in range(nb)]
+    head = {}
+    for h in range(2):
+        hs = slice(h * HEAD_DIM, (h + 1) * HEAD_DIM)
+        il = l_ref[0, h:h + 1]
+        head[h] = ((dat * il).astype(jnp.bfloat16), jnp.sum(prod[hs], axis=0, keepdims=True) * il)
+
+    def soft_grad(h, j):
+        js = slice(j * BQ, (j + 1) * BQ)
+        kk = (j + 1) * BQ if causal else s
+        dab = pick_head(h, head[h][0][:, js])
+        return dot_mm(v_ref[:kk], dab, 1, 0), dot_mm(pv_ref[...], dab, 1, 0) if causal else None
+
+    def add(tot, new):
+        return new if tot is None else tot + new
+
+    res = {}
+    dpk = [None, None]
+    dpv = [None, None]
+    dkb = [[None] * nb, [None] * nb]
+    dvb = [[None] * nb, [None] * nb]
+    ahead = soft_grad(*work[0])
+    for w, (h, j) in enumerate(work):
+        dp, dpp = ahead
+        if w + 1 < len(work):
+            ahead = soft_grad(*work[w + 1])
+        hs = slice(h * HEAD_DIM, (h + 1) * HEAD_DIM)
+        js = slice(j * BQ, (j + 1) * BQ)
+        kk = dp.shape[0]
+        dl = head[h][1][:, js]
+        dah = head[h][0][hs, js]
+        p = p_ref[h, :kk, js]
+        ds = (p.astype(jnp.float32) * (dp - dl)).astype(jnp.bfloat16)
+        dq = dot_mm(kt[hs, :kk], ds, 1, 0)
+        if causal:
+            pp = pp_ref[h, :, js]
+            dsp = (pp.astype(jnp.float32) * (dpp - dl)).astype(jnp.bfloat16)
+            dq += dot_mm(pkt[hs], dsp, 1, 0)
+            dpk[h] = add(dpk[h], dot_mm(qt[hs, js], dsp, 1, 1))
+            dpv[h] = add(dpv[h], dot_mm(dah, pp, 1, 1))
+        res[h, j] = dq
+        dv = dot_mm(dah, p, 1, 1)
+        dk = dot_mm(qt[hs, js], ds, 1, 1)
+        if causal:
+            for i in range(kk // BQ):
+                dvb[h][i] = add(dvb[h][i], dv[:, i * BQ:(i + 1) * BQ])
+                dkb[h][i] = add(dkb[h][i], dk[:, i * BQ:(i + 1) * BQ])
+        else:
+            dvb[h] = [add(dvb[h][0], dv)]
+            dkb[h] = [add(dkb[h][0], dk)]
+    both = lambda f: jnp.concatenate([f(0), f(1)], axis=0)
+    dq_ref[...] = (both(lambda h: jnp.concatenate([res[h, j] for j in range(nb)], axis=1))
+                   * HEAD_DIM ** -0.5).astype(jnp.bfloat16).T
+    dk_ref[...] = (both(lambda h: jnp.concatenate(dkb[h], axis=1)) * LN2).astype(jnp.bfloat16).T
+    dv_ref[...] = both(lambda h: jnp.concatenate(dvb[h], axis=1)).astype(jnp.bfloat16).T
+    if causal:
+        dpk_ref[...] = both(lambda h: dpk[h]) * LN2
+        dpv_ref[...] = both(lambda h: dpv[h])
+    else:
+        dpk_ref[...] = jnp.zeros_like(dpk_ref)
+        dpv_ref[...] = jnp.zeros_like(dpv_ref)
+
+
+def attn_bwd(q, k, v, a, da, il, p, pp, pk=None, pv=None):
+    t, w = q.shape
+    s = k.shape[0]
+    pairs = w // 128
+    causal = pk is not None
+    if not causal:
+        pk = jnp.zeros((PRE, w), jnp.bfloat16)
+        pv = pk
+    col = lambda g: (0, g)
+    lead = lambda g: (g, 0, 0)
+    f32, bf = jnp.float32, jnp.bfloat16
+    return pl.pallas_call(
+        functools.partial(attn_bwd_body, causal),
+        grid=(pairs,),
+        in_specs=[
+            pl.BlockSpec((t, 128), col), pl.BlockSpec((s, 128), col), pl.BlockSpec((s, 128), col),
+            pl.BlockSpec((t, 128), col), pl.BlockSpec((t, 128), col),
+            pl.BlockSpec((1, 2, t), lead), pl.BlockSpec((2, s, t), lead), pl.BlockSpec((2, PRE, t), lead),
+            pl.BlockSpec((PRE, 128), col), pl.BlockSpec((PRE, 128), col),
+        ],
+        out_specs=[
+            pl.BlockSpec((t, 128), col), pl.BlockSpec((s, 128), col), pl.BlockSpec((s, 128), col),
+            pl.BlockSpec((128, PRE), lambda g: (g, 0)), pl.BlockSpec((128, PRE), lambda g: (g, 0)),
+        ],
+        out_shape=[
+            jax.ShapeDtypeStruct((t, w), bf), jax.ShapeDtypeStruct((s, w), bf), jax.ShapeDtypeStruct((s, w), bf),
+            jax.ShapeDtypeStruct((w, PRE), f32), jax.ShapeDtypeStruct((w, PRE), f32),
+        ],
+        compiler_params=pltpu.CompilerParams(vmem_limit_bytes=VMEM_BYTES),
+        cost_estimate=pl.CostEstimate(flops=40 * t * s * w, bytes_accessed=4 * t * s * pairs, transcendentals=0),
+    )(q, k, v, a, da, il, p, pp, pk, pv)
+
+
+def erf_parts(v):
+    mag = jnp.abs(v)
+    expo = jnp.exp2(v * v * (-0.5 * LOG2E))
+    t = 1.0 / (1.0 + (0.3275911 * 0.5 ** 0.5) * mag)
+    poly = t * (0.254829592 + t * (-0.284496736 + t * (1.421413741 + t * (-1.453152027 + t * 1.061405429))))
+    half = 0.5 * poly * expo
+    return jnp.where(v < 0.0, half, 1.0 - half), expo * (2.0 * math.pi) ** -0.5
+
+
+def gelu_pair(v):
+    cdf, pdf = erf_parts(v)
+    return v * cdf, cdf + v * pdf
+
+
+def normalize(z):
+    centered = z - jnp.mean(z, axis=-1, keepdims=True)
+    inv = lax.rsqrt(jnp.mean(centered * centered, axis=-1, keepdims=True) + EPS)
+    return centered * inv, inv
+
+
+def norm_back(e, u, inv, gain):
+    w = e * gain
+    return inv * (w - jnp.mean(w, axis=-1, keepdims=True) - u * jnp.mean(w * u, axis=-1, keepdims=True))
+
+
+def glue(pieces):
+    rows = [jnp.concatenate(list(row), axis=1) if len(row) > 1 else row[0] for row in pieces]
+    return jnp.concatenate(rows, axis=0) if len(rows) > 1 else rows[0]
+
+
+def fused(terms, rows, consts, outs, body, tile, pick=None, dp=None, steps=None):
+    t = rows[0].shape[0]
+    steps = t // tile if steps is None else steps
+    flat, place = [], []
+    for term in terms:
+        grid_of = []
+        for row in term:
+            line = []
+            for piece in row:
+                known = [i for i, f in enumerate(flat) if f is piece]
+                if not known:
+                    flat.append(piece)
+                    known = [len(flat) - 1]
+                line.append(known[0])
+            grid_of.append(line)
+        place.append(grid_of)
+    nf, nr, nc = len(flat), len(rows), len(consts)
+
+    def kernel(sc_ref, *refs):
+        mats = [[[refs[i] for i in line] for line in grid_of] for grid_of in place]
+        body(mats, refs[nf:nf + nr], refs[nf + nr:nf + nr + nc], refs[nf + nr + nc:], sc_ref[1])
+
+    scal = jnp.stack([jnp.int32(0) if pick is None else pick, jnp.int32(0) if dp is None else dp])
+    whole = lambda a: pl.BlockSpec(a.shape, lambda i, sc: (0,) * a.ndim, pipeline_mode=pl.Buffered(1))
+    flops = 2 * sum(p.size for term in terms for row in term for p in row) * tile * steps
+    nbytes = sum(2 * f.size for f in flat) + sum(r.size * r.dtype.itemsize for r in rows)
+    return pl.pallas_call(
+        kernel,
+        grid_spec=pltpu.PrefetchScalarGridSpec(
+            num_scalar_prefetch=1,
+            grid=(steps,),
+            in_specs=[whole(f) for f in flat]
+            + [pl.BlockSpec((tile, r.shape[1]), lambda i, sc: (i + sc[0], 0)) for r in rows]
+            + [whole(c) for c in consts],
+            out_specs=[pl.BlockSpec((tile, c), lambda i, sc: (i, 0)) for _, c, _ in outs],
+        ),
+        out_shape=[jax.ShapeDtypeStruct((r, c), d) for r, c, d in outs],
+        compiler_params=pltpu.CompilerParams(vmem_limit_bytes=VMEM_BYTES),
+        cost_estimate=pl.CostEstimate(flops=flops, bytes_accessed=nbytes, transcendentals=0),
+    )(scal, *flat, *rows, *consts)
+
+
+def load(mat):
+    return glue([[ref[...] for ref in line] for line in mat])
+
+
+def project(lhs, mats, scales):
+    t = lhs.shape[0]
+
+    def body(ms, rows, consts, outs, dp):
+        x = rows[0][...]
+        for m, scale, out in zip(ms, scales, outs):
+            y = dot_mm(x, load(m), 1, 0)
+            out[...] = (y if scale == 1.0 else y * scale).astype(BF)
+
+    width = sum(p.shape[1] for p in mats[0][0])
+    return fused(mats, [lhs], [], [(t, width, BF)] * len(mats), body, min(512, t))
+
+
+def project_back(lhs, mats):
+    t = lhs.shape[0]
+
+    def body(ms, rows, consts, outs, dp):
+        x = rows[0][...]
+        for m, out in zip(ms, outs):
+            out[...] = dot_mm(x, load(m), 1, 1).astype(BF)
+
+    return fused(mats, [lhs], [], [(t, sum(line[0].shape[0] for line in m), BF) for m in mats], body, min(512, t))
+
+
+def add_norm(resid, gain_in, lhss, mats, gain):
+    t, d = resid.shape
+
+    def body(ms, rows, consts, outs, dp):
+        z = rows[0][...].astype(F32)
+        if gain_in is not None:
+            z = z * consts[1][...]
+        for lhs, m in zip(rows[1:], ms):
+            z = z + dot_mm(lhs[...], load(m), 1, 0)
+        u, inv = normalize(z)
+        outs[0][...] = u
+        outs[1][...] = inv
+        outs[2][...] = (u * consts[0][...]).astype(BF)
+
+    consts = [gain] + ([] if gain_in is None else [gain_in])
+    return fused(mats, [resid] + lhss, consts, [(t, d, F32), (t, 1, F32), (t, d, BF)], body, min(512, t))
+
+
+def hidden_forward(lhs, mat, trans):
+    t = lhs.shape[0]
+    width = sum(line[0].shape[0] for line in mat) if trans else sum(p.shape[1] for p in mat[0])
+
+    def body(ms, rows, consts, outs, dp):
+        x = rows[0][...]
+        w = load(ms[0])
+        for c in range(width // 256):
+            cs = slice(c * 256, (c + 1) * 256)
+            g = dot_mm(x, w[cs], 1, 1) if trans else dot_mm(x, w[:, cs], 1, 0)
+            act, slope = gelu_pair(g)
+            outs[0][:, cs] = act.astype(BF)
+            outs[1][:, cs] = slope.astype(BF)
+
+    return fused([mat], [lhs], [], [(t, width, BF)] * 2, body, min(512, t))
+
+
+def hidden_backward(lhs, mat, slope, scale):
+    t, width = slope.shape
+
+    def body(ms, rows, consts, outs, dp):
+        g = dot_mm(rows[0][...], load(ms[0]), 1, 1)
+        outs[0][...] = (g * scale * rows[1][...].astype(F32)).astype(BF)
+
+    return fused([mat], [lhs, slope], [], [(t, width, BF)], body, min(512, t))[0]
+
+
+def unpermute_store(out, value, dp):
+    for r in range(value.shape[1] // 256):
+        out[:, pl.ds(pl.multiple_of((dp ^ r) * 256, 256), 256)] = value[:, r * 256:(r + 1) * 256].astype(out.dtype)
+
+
+def last_norm(u2, gain2, acts, mats, adapt, up, gain3, cot, dp):
+    t, d = u2.shape
+    na = len(acts)
+
+    def body(ms, rows, consts, outs, dp):
+        z = rows[0][...] * consts[0][...]
+        for lhs, m in zip(rows[1:1 + na], ms[:na]):
+            z = z + dot_mm(lhs[...], load(m), 1, 0)
+        z = z + 4.0 * dot_mm(rows[1 + na][...], load(ms[na]), 1, 0)
+        u, inv = normalize(z)
+        unpermute_store(outs[0], u * consts[1][...], dp)
+        dz = norm_back(rows[2 + na][...].astype(F32), u, inv, consts[1][...])
+        outs[1][...] = dz
+        outs[2][...] = dz.astype(BF)
+
+    return fused(mats + [up], [u2] + acts + [adapt, cot], [gain2, gain3],
+                 [(t, d, BF), (t, d, F32), (t, d, BF)], body, min(256, t), dp=dp)
+
+
+def back_norm(resid, lhss, mats, trans, u, inv, gain):
+    t, d = resid.shape
+    nl = len(lhss)
+
+    def body(ms, rows, consts, outs, dp):
+        e = rows[0][...]
+        for lhs, m, tr in zip(rows[1:1 + nl], ms, trans):
+            e = e + dot_mm(lhs[...], load(m), 1, 1 if tr else 0)
+        dz = norm_back(e, rows[1 + nl][...], rows[2 + nl][...], consts[0][...])
+        outs[0][...] = dz
+        outs[1][...] = dz.astype(BF)
+
+    return fused(mats, [resid] + lhss + [u, inv], [gain], [(t, d, F32), (t, d, BF)], body, min(256, t))
+
+
+def half_rows(resid, lhss, mats, pick, dp, half):
+    d = sum(line[0].shape[0] for line in mats[0])
+
+    def body(ms, rows, consts, outs, dp):
+        off = 0 if resid is None else 1
+        e = rows[0][...] if off else None
+        for lhs, m in zip(rows[off:], ms):
+            y = dot_mm(lhs[...], load(m), 1, 1)
+            e = y if e is None else e + y
+        unpermute_store(outs[0], e, dp)
+
+    return fused(mats, ([] if resid is None else [resid]) + lhss, [], [(half, d, BF)], body, half,
+                 pick=pick, dp=dp, steps=1)[0]
+
+
+def whole_sequences(inputs, memory, src_lengths, self_qkv, self_proj, cross_qkv, cross_proj, ffn_in, ffn_out,
+                    norm_gains, prefix, adapter_down, adapter_up, cotangent):
+    dp, y, z = lax.axis_index("dp"), lax.axis_index("mp"), lax.axis_index("adp")
+    nz = lax.axis_size("adp")
+    half, d = inputs.shape[2], inputs.shape[3]
+    chunk = self_qkv.shape[1]
+    flip = [(i, 1 - i) for i in range(2)]
+    ring = [(i, (i + 1) % nz) for i in range(nz)]
+    pc = lambda a: lax.ppermute(a, "dp", [(i, i ^ 1) for i in range(4)])
+    px = lambda a: lax.ppermute(a, "dp", [(i, i ^ 2) for i in range(4)])
+    py = lambda a: lax.ppermute(a, "mp", flip)
+    pz = lambda a: lax.ppermute(a, "adp", ring)
+
+    def rel(a):
+        return jnp.concatenate(
+            [lax.dynamic_slice_in_dim(a, (dp ^ r) * chunk, chunk, axis=a.ndim - 1) for r in range(4)], axis=-1)
+
+    def swap_rows(a):
+        own = lax.dynamic_index_in_dim(a, y, 0, keepdims=False)[0]
+        got = py(lax.dynamic_index_in_dim(a, 1 - y, 0, keepdims=False)[0])
+        return rel(jnp.concatenate([jnp.where(y == 0, own, got), jnp.where(y == 0, got, own)], axis=0))
+
+    def plane(own):
+        across = px(own)
+        beside = py(own)
+        diagonal = px(beside)
+        return [[own, pc(own), across, pc(across)], [beside, pc(beside), diagonal, pc(diagonal)]]
+
+    x_full = swap_rows(inputs)
+    sq = plane(self_qkv)
+    quarter_h = ffn_in.shape[1] // nz
+    own_q = []
+    for k in range(nz):
+        at = ((z - k) % nz) * quarter_h
+        fi = lax.dynamic_slice_in_dim(ffn_in, at, quarter_h, axis=1)
+        fo = lax.dynamic_slice_in_dim(ffn_out, at, quarter_h, axis=0)
+        own_q.append(jnp.concatenate([fi[:, :chunk], fi[:, chunk:], fo], axis=0))
+    own_all = jnp.stack(own_q)
+    sib_all = pc(own_all)
+    fx = px(own_q[0])
+    fy = py(own_q[0])
+    fd = px(fy)
+    ad = jnp.concatenate([adapter_down.T, adapter_up], axis=0)
+    hops = [jnp.concatenate([fx, fy, fd, ad], axis=0)]
+    for k in range(1, nz):
+        hops.append(pz(hops[-1]))
+    hops_sib = [pc(h) for h in hops]
+    qrows = own_q[0].shape[0]
+    adapters = jnp.stack([h[3 * qrows:] for h in hops])
+    adapters_x = px(adapters)
+    adapters_sib = pc(jnp.stack([adapters, adapters_x]))
+    pre_own = jnp.pad(prefix, ((0, 0), (0, PRE - PREFIX_LEN), (0, 0)))
+    pre = [pre_own, py(pre_own)]
+    mem_full = swap_rows(memory)
+    so = plane(self_proj)
+    cq = plane(cross_qkv)
+    co = plane(cross_proj)
+    cot_full = swap_rows(cotangent)
+
+    def in_block(k):
+        def part(p):
+            return [p[:chunk], p[chunk:2 * chunk], p[2 * chunk:]]
+        h, hs = hops[k], hops_sib[k]
+        cut = lambda a, i: part(a[i * qrows:(i + 1) * qrows])
+        s0 = [part(own_all[k]), part(sib_all[k]), cut(h, 0), cut(hs, 0)]
+        s1 = [cut(h, 1), cut(hs, 1), cut(h, 2), cut(hs, 2)]
+        w_in = [[s0[r][0], s0[r][1], s1[r][0], s1[r][1]] for r in range(4)]
+        w_out = [[s[r][2] for r in range(4)] for s in (s0, s1)]
+        return w_in, w_out
+
+    gains = rel(norm_gains.astype(F32))
+    gain = [gains[i:i + 1] for i in range(3)]
+    pad_n = jnp.full((1,), PREFIX_LEN, jnp.int32)
+    src_n = lax.dynamic_index_in_dim(src_lengths, y, 0, keepdims=False).reshape(1)
+    qscale = HEAD_DIM ** -0.5 * LOG2E
+    w_of = lambda pieces, s, c: [[pieces[s][r][c]] for r in range(4)]
+
+    self_kept, attn_self = [], []
+    for s in range(2):
+        q, k, v = project(x_full, [w_of(sq, s, c) for c in range(3)], (qscale, 1.0, 1.0))
+        a, p, pp, il = attn_fwd(pad_n, q, k, v, pre[s][0], pre[s][1].T)
+        self_kept.append((q, k, v, a, il, p, pp))
+        attn_self.append(a)
+    so_s = [[[so[s][r] for r in range(4)]] for s in range(2)]
+    u1, inv1, h1b = add_norm(x_full, None, attn_self, so_s, gain[0])
+    cross_w = lambda c: [[cq[s][r][c] for s in range(2)] for r in range(4)]
+    (qc,) = project(h1b, [cross_w(0)], (qscale,))
+    kc, vc = project(mem_full, [cross_w(1), cross_w(2)], (1.0, 1.0))
+    ac, p_c, pp_c, il_c = attn_fwd(src_n, qc, kc, vc)
+    co_w = [[co[s][r] for r in range(4)] for s in range(2)]
+    u2, inv2, h2b = add_norm(u1, gain[0], [ac], [co_w], gain[1])
+    w_in, w_out = zip(*[in_block(k) for k in range(nz)])
+    rows_a = adapter_up.shape[0]
+    pieces_a = [adapters, adapters_sib[0], adapters_x, adapters_sib[1]]
+    down_t = [[pieces_a[r][k][:rows_a] for r in range(4)] for k in range(nz)]
+    up_w = [[pieces_a[r][k][rows_a:] for r in range(4)] for k in range(nz)]
+    acts, slopes = [], []
+    for k in range(nz):
+        act, slope = hidden_forward(h2b, w_in[k], False)
+        acts.append(act)
+        slopes.append(slope)
+    act_a, slope_a = hidden_forward(h2b, down_t, True)
+    res, dz3, b3 = last_norm(u2, gain[1], acts, list(w_out), act_a, up_w, gain[2], cot_full, dp)
+
+    def hand_back(full):
+        mine = lax.dynamic_slice_in_dim(full, y * half, half, axis=0)
+        theirs = py(lax.dynamic_slice_in_dim(full, (1 - y) * half, half, axis=0))
+        return join(mine, theirs)
+
+    def join(mine, theirs):
+        return jnp.stack([jnp.where(y == 0, mine, theirs), jnp.where(y == 0, theirs, mine)])[:, None]
+
+    result = hand_back(res)
+
+    dga = hidden_backward(b3, up_w, slope_a, 4.0)
+    tn = lambda a, b: dot_mm(a, b, 0, 0)
+    up_term = tn(act_a, b3) * 4.0
+    down_term = tn(h2b, dga)
+    order_z = lambda a, axis: jnp.concatenate(
+        [lax.dynamic_slice_in_dim(a, ((z - j) % nz) * rows_a, rows_a, axis=axis) for j in range(nz)], axis=axis)
+    down_abs = rel(order_z(down_term, 1).T)
+    up_abs = rel(order_z(up_term, 0))
+    both = jnp.stack([down_abs, up_abs])
+    both = lax.psum_scatter(both, "adp", scatter_dimension=1, tiled=True)
+    both = lax.psum_scatter(both, ("dp", "mp"), scatter_dimension=2, tiled=True)
+    down_grad, up_grad = both[0].T, both[1]
+    dgs = [hidden_backward(b3, w_out[k], slopes[k], 1.0) for k in range(nz)]
+    dz2, dz2b = back_norm(dz3, dgs + [dga], list(w_in) + [down_t], [True] * nz + [False], u2, inv2, gain[1])
+    (dac,) = project_back(dz2b, [co_w])
+    dqc, dkc, dvc, _, _ = attn_bwd(qc, kc, vc, ac, dac, il_c, p_c, pp_c)
+    mem_mats = [cross_w(1), cross_w(2)]
+    mem_send = half_rows(None, [dkc, dvc], mem_mats, 1 - y, dp, half)
+    mem_mine = half_rows(None, [dkc, dvc], mem_mats, y, dp, half)
+    memory_grad = join(mem_mine, py(mem_send))
+    dz1, dz1b = back_norm(dz2, [dqc], [cross_w(0)], [True], u1, inv1, gain[0])
+    das = project_back(dz1b, [[[so[s][r] for r in range(4)]] for s in range(2)])
+    lhss, mats, pre_terms = [], [], []
+    for s in range(2):
+        q, k, v, a, il, p, pp = self_kept[s]
+        dq, dk, dv, dpk, dpv = attn_bwd(q, k, v, a, das[s], il, p, pp, pre[s][0], pre[s][1])
+        lhss += [dq, dk, dv]
+        mats += [w_of(sq, s, c) for c in range(3)]
+        pre_terms.append(jnp.stack([dpk.T, dpv.T])[:, :PREFIX_LEN])
+    prefix_grad = lax.psum(pre_terms[0] + py(pre_terms[1]), ("dp", "adp"))
+    in_send = half_rows(dz1, lhss, mats, 1 - y, dp, half)
+    in_mine = half_rows(dz1, lhss, mats, y, dp, half)
+    input_grad = join(in_mine, py(in_send))
+    return result, input_grad, memory_grad, prefix_grad, down_grad, up_grad
+
+
 def solution(mesh):
+    by_sequence = mesh.shape["mp"] == MICRO and mesh.shape["dp"] == 4
     return jax.shard_map(
-        shards,
+        whole_sequences if by_sequence else shards,
         mesh=mesh,
         in_specs=(
             P(None, ("dp", "adp"), "mp", None),

time: 2210 us -> 706 us (0.32)
  waiting for transfers between devices: 1290 us -> 166 us
  matrix products: 581 us -> 4.04 us
  Pallas kernels: 0 us -> 349 us
  other arithmetic: 234 us -> 28.2 us
  local copies, waits for them, and re-layouts: 53.9 us -> 92.1 us
  starting transfers between devices: 4.61 us -> 39.5 us
    reduce_scatter x20 -> x2, waiting for transfers between devices: 604 us -> 0.01 us  [the longest x1 0.01 us: whole_sequences(): both = lax.psum_scatter(both, 'adp', scatter_dimension=1, tiled=True)]
    all_gather x24 -> x0, waiting for transfers between devices: 591 us -> none  [the longest x4 234 us: gather_adapter(): return lax.all_gather(rows_low, 'adp', axis=0, tiled=True)]
    dot_general x62 -> x2, matrix products: 581 us -> 4.04 us  [dot_mm(): lax.dot_general(a, b, (((ca,), (cb,)), ((), ())), preferred_element_type=...]
    pallas_call x0 -> x31, Pallas kernels: none -> 349 us  [the longest x25 218 us: fused(): pl.pallas_call(kernel, grid_spec=pltpu.PrefetchScalarGridSpec(num_scalar_...]
    convert_element_type x12 -> x1, other arithmetic: 128 us -> 0.61 us  [whole_sequences(): gains = rel(norm_gains.astype(F32))]
    ppermute x0 -> x49, waiting for transfers between devices: none -> 96.4 us  [the longest x13 63.2 us: whole_sequences(): py = lambda a: lax.ppermute(a, 'mp', flip)]
    reduce_sum x18 -> x0, other arithmetic: 90.6 us -> none  [the longest x4 55 us: attend_forward(): row_total = jnp.sum(expo_scores, axis=-1, keepdims=True)]
    ppermute x0 -> x49, starting transfers between devices: none -> 39.2 us  [the longest x11 15.9 us: whole_sequences(): px = lambda a: lax.ppermute(a, 'dp', [(i, i ^ 2) for i in range(4)])]
  transfers between devices with their start and end apart: 45 -> 52, of which waited for: 33 -> 8; matrix products, arithmetic and copies ran while one was open for 37% -> 16% of each run, Pallas kernels for 0% -> 46%
where the time goes in v1:
time: 706 us; the launch traced here: 695 us
  Pallas kernels  349 us (49%)
  waiting for transfers between devices  166 us (24%)
  local copies, waits for them, and re-layouts  92.1 us (13%)
  starting transfers between devices  39.5 us (6%)
  other arithmetic  28.2 us (4%)
  between operations  16.4 us (2%)
    pallas_call x25, Pallas kernels, fused(): pl.pallas_call(kernel, grid_spec=pltpu.PrefetchScalarGridSpec(num_scalar_...  218 us
    pallas_call x3, Pallas kernels, attn_bwd(): pl.pallas_call(functools.partial(attn_bwd_body, causal), grid=(pairs,), i...  75.6 us
    psum x1, waiting for transfers between devices, whole_sequences(): prefix_grad = lax.psum(pre_terms[0] + py(pre_terms[1]), ('dp', 'adp'))  69.4 us
    ppermute x13, waiting for transfers between devices, whole_sequences(): py = lambda a: lax.ppermute(a, 'mp', flip)  63.2 us
    pallas_call x3, Pallas kernels, attn_fwd(): pl.pallas_call(functools.partial(attn_fwd_body, causal), grid=(pairs,), i...  55.9 us
    slice x22, local copies, waits for them, and re-layouts, part(): return [p[:chunk], p[chunk:2 * chunk], p[2 * chunk:]]  36.2 us
    ppermute x3, waiting for transfers between devices, whole_sequences(): pz = lambda a: lax.ppermute(a, 'adp', ring)  28.4 us
    ppermute x11, starting transfers between devices, whole_sequences(): px = lambda a: lax.ppermute(a, 'dp', [(i, i ^ 2) for i in range(4)])  15.9 us
  transfers between devices with their start and end apart: 52, of which 8 were waited for; matrix products, arithmetic and copies ran while one was open for 16% of the time, Pallas kernels for 46%

profile of v1, /device:TPU:0, one launch (start us, length us, event | category | flops | bytes accessed | tf_op | source)
XLA Modules:
  0.0 695.4 jit_solution(8602344492427828631)
XLA Ops:
  12.3 2.9 collective-permute-start.1
  61.3 12.8 %collective-permute-done.36 = bf16[3,256,512]{2,1,0:T(8,128)(2,1)} collective-permute-done((bf16[3,256,512]{2,1,0:T(8,128)(2,1)S(1)}, bf16[3,256,512]{2,1,0:T(8,128)(2,1)}, u32[]{:S(2)}, u32[]{:S(2)}) %collective-permute-start.36) | collective-permute-done | bytes 786464 | tf_op jit(solution)/shard_map/ppermute | solution.py:780
  82.1 4.7 collective-permute-done.3
  86.8 9.6 %collective-permute-done.27 = bf16[512,1024]{1,0:T(8,128)(2,1)S(1)} collective-permute-done((bf16[512,1024]{1,0:T(8,128)(2,1)S(1)}, bf16[512,1024]{1,0:T(8,128)(2,1)S(1)}, u32[]{:S(2)}, u32[]{:S(2)}) %collective-permute-start.27) | collective-permute-done | bytes 1048608 | tf_op jit(solution)/shard_map/ppermute | solution.py:780
  96.9 22.0 %collective-permute-done.43 = bf16[512,1024]{1,0:T(8,128)(2,1)S(1)} collective-permute-done((bf16[512,1024]{1,0:T(8,128)(2,1)S(1)}, bf16[512,1024]{1,0:T(8,128)(2,1)S(1)}, u32[]{:S(2)}, u32[]{:S(2)}) %collective-permute-start.43) | collective-permute-done | bytes 1048608 | tf_op jit(solution)/shard_map/ppermute | solution.py:780
  123.0 17.7 %collective-permute-done.44 = bf16[512,1024]{1,0:T(8,128)(2,1)S(1)} collective-permute-done((bf16[512,1024]{1,0:T(8,128)(2,1)S(1)}, bf16[512,1024]{1,0:T(8,128)(2,1)S(1)}, u32[]{:S(2)}, u32[]{:S(2)}) %collective-permute-start.44) | collective-permute-done | bytes 1048608 | tf_op jit(solution)/shard_map/ppermute | solution.py:780
  149.5 7.3 %shard_map.181 = (bf16[1024,512]{1,0:T(8,128)(2,1)}, bf16[1024,512]{1,0:T(8,128)(2,1)}, bf16[1024,512]{1,0:T(8,128)(2,1)}) custom-call(s32[2]{0:T(128)} %broadcast_3_sc_ref.2.sc_ref, bf16[256,512]{1,0:T(8,128)(2,1)} %get-tuple-element.333.refs_0_, bf16[256,512]{1,0:T(8,128)(2,1)} %get-tuple-element.330.refs_1_, bf16[256,512]{1,0:T(8,128)(2,1)} %get-tuple-element.327.refs_2_, ...), custom_call_target="tpu_custom_call" | custom-call | flops 3221225472 | bytes 5242880 | tf_op jit(solution)/shard_map/pallas_call | solution.py:627
  156.8 12.7 %shard_map.182 = (bf16[1024,512]{1,0:T(8,128)(2,1)}, bf16[8,1024,1024]{2,1,0:T(8,128)(2,1)}, bf16[8,32,1024]{2,1,0:T(8,128)(2,1)}, f32[4,2,1024]{2,1,0:T(2,128)}) custom-call(s32[1]{0:T(128)} %constant.101.clone.1.n_ref, bf16[1024,512]{1,0:T(8,128)(2,1)} %get-tuple-element.64.q_ref, bf16[1024,512]{1,0:T(8,128)(2,1)} %get-tuple-element.65.k_ref, ...), custom_call_target="tpu_custom_call" | custom-call | flops 12884901888 | bytes 16777216 | tf_op jit(solution)/shard_map/pallas_call | solution.py:443
  178.2 2.2 slice_bitcast_fusion.42
  180.3 2.3 slice_bitcast_fusion.52
  183.9 7.3 %shard_map.183 = (bf16[1024,512]{1,0:T(8,128)(2,1)}, bf16[1024,512]{1,0:T(8,128)(2,1)}, bf16[1024,512]{1,0:T(8,128)(2,1)}) custom-call(s32[2]{0:T(128)} %broadcast_3_sc_ref.2.sc_ref, bf16[256,512]{1,0:T(8,128)(2,1)} %get-tuple-element.321.refs_0_.refs_12_, bf16[256,512]{1,0:T(8,128)(2,1)} %get-tuple-element.318.refs_1_.refs_13_, ...), custom_call_target="tpu_custom_call" | custom-call | flops 3221225472 | bytes 5242880 | tf_op jit(solution)/shard_map/pallas_call | solution.py:627
  193.3 2.3 collective-permute-start.5
  195.6 12.7 %shard_map.184 = (bf16[1024,512]{1,0:T(8,128)(2,1)}, bf16[8,1024,1024]{2,1,0:T(8,128)(2,1)}, bf16[8,32,1024]{2,1,0:T(8,128)(2,1)}, f32[4,2,1024]{2,1,0:T(2,128)}) custom-call(s32[1]{0:T(128)} %constant.101.clone.1.n_ref, bf16[1024,512]{1,0:T(8,128)(2,1)} %get-tuple-element.68.q_ref, bf16[1024,512]{1,0:T(8,128)(2,1)} %get-tuple-element.69.k_ref, ...), custom_call_target="tpu_custom_call" | custom-call | flops 12884901888 | bytes 16777216 | tf_op jit(solution)/shard_map/pallas_call | solution.py:443
  211.4 8.9 %shard_map.187 = (bf16[1024,1024]{1,0:T(8,128)(2,1)}, bf16[1024,1024]{1,0:T(8,128)(2,1)}) custom-call(s32[2]{0:T(128)} %broadcast_3_sc_ref.2.sc_ref, bf16[256,512]{1,0:T(8,128)(2,1)} %get-tuple-element.309.refs_0_, bf16[256,512]{1,0:T(8,128)(2,1)} %get-tuple-element.305.refs_1_, bf16[256,512]{1,0:T(8,128)(2,1)} %get-tuple-element.302.refs_2_, ...), custom_call_target="tpu_custom_call" | custom-call | flops 4294967296 | bytes 6291456 | tf_op jit(solution)/shard_map/pallas_call | solution.py:627
  221.8 8.4 %shard_map.185 = (f32[1024,1024]{1,0:T(8,128)}, f32[1024,1]{1,0:T(8,128)}, bf16[1024,1024]{1,0:T(8,128)(2,1)}) custom-call(s32[2]{0:T(128)} %broadcast_3_sc_ref.2.sc_ref, bf16[512,256]{1,0:T(8,128)(2,1)} %refs_0_.9, bf16[512,256]{1,0:T(8,128)(2,1)} %collective-permute-done.20.refs_1_, bf16[512,256]{1,0:T(8,128)(2,1)} %collective-permute-done.21.refs_2_, ...), custom_call_target="tpu_custom_call" | custom-call | flops 2147483648 | bytes 6291456 | tf_op jit(solution)/shard_map/pallas_call | solution.py:627
  230.2 6.0 shard_map.186.q_ref
  239.5 30.5 %shard_map.188 = (bf16[1024,1024]{1,0:T(8,128)(2,1)}, bf16[16,1024,1024]{2,1,0:T(8,128)(2,1)}, bf16[16,32,1024]{2,1,0:T(8,128)(2,1)}, f32[8,2,1024]{2,1,0:T(2,128)}) custom-call(s32[1]{0:T(128)} %bitcast.60.n_ref, bf16[1024,1024]{1,0:T(8,128)(2,1)} %shard_map.186.q_ref, bf16[1024,1024]{1,0:T(8,128)(2,1)} %get-tuple-element.74.k_ref, ...), custom_call_target="tpu_custom_call" | custom-call | flops 25769803776 | bytes 33554432 | tf_op jit(solution)/shard_map/pallas_call | solution.py:443
  270.0 8.6 %shard_map.189 = (f32[1024,1024]{1,0:T(8,128)}, f32[1024,1]{1,0:T(8,128)}, bf16[1024,1024]{1,0:T(8,128)(2,1)}) custom-call(s32[2]{0:T(128)} %broadcast_3_sc_ref.2.sc_ref, bf16[512,256]{1,0:T(8,128)(2,1)} %refs_0_.8, bf16[512,256]{1,0:T(8,128)(2,1)} %collective-permute-done.13.refs_1_, bf16[512,256]{1,0:T(8,128)(2,1)} %copy-done.33, ...), custom_call_target="tpu_custom_call" | custom-call | flops 2147483648 | bytes 8388608 | tf_op jit(solution)/shard_map/pallas_call | solution.py:627
  279.6 9.4 %shard_map.190 = (bf16[1024,1024]{1,0:T(8,128)(2,1)}, bf16[1024,1024]{1,0:T(8,128)(2,1)}) custom-call(s32[2]{0:T(128)} %broadcast_3_sc_ref.2.sc_ref, bf16[256,256]{1,0:T(8,128)(2,1)} %copy-done.29, bf16[256,256]{1,0:T(8,128)(2,1)} %copy-done.30, bf16[256,256]{1,0:T(8,128)(2,1)} %get-tuple-element.347.refs_2_, bf16[256,256]{1,0:T(8,128)(2,1)} %get-tuple-element.346.refs_3_, ...), custom_call_target="tpu_custom_call" | custom-call | flops 2147483648 | bytes 4194304 | tf_op jit(solution)/shard_map/pallas_call | solution.py:627
  296.9 2.1 fusion.21
  299.0 2.1 fusion.22
  303.2 28.4 %collective-permute-done.9 = bf16[3328,256]{1,0:T(8,128)(2,1)S(1)} collective-permute-done((bf16[3328,256]{1,0:T(8,128)(2,1)}, bf16[3328,256]{1,0:T(8,128)(2,1)S(1)}, u32[]{:S(2)}, u32[]{:S(2)}) %collective-permute-start.9) | collective-permute-done | bytes 1703968 | tf_op jit(solution)/shard_map/ppermute | solution.py:781
  333.2 9.4 %shard_map.191 = (bf16[1024,1024]{1,0:T(8,128)(2,1)}, bf16[1024,1024]{1,0:T(8,128)(2,1)}) custom-call(s32[2]{0:T(128)} %broadcast_3_sc_ref.2.sc_ref, bf16[256,256]{1,0:T(8,128)(2,1)} %get-tuple-element.277.refs_0_.refs_16_, bf16[256,256]{1,0:T(8,128)(2,1)} %get-tuple-element.278.refs_1_.refs_17_, bf16[256,256]{1,0:T(8,128)(2,1)} %get-tuple-element.229.refs_2_.refs_18_, ...), custom_call_target="tpu_custom_call" | custom-call | flops 2147483648 | bytes 4194304 | tf_op jit(solution)/shard_map/pallas_call | solution.py:627
  344.6 2.1 fusion.20
  348.3 9.3 %shard_map.192 = (bf16[1024,1024]{1,0:T(8,128)(2,1)}, bf16[1024,1024]{1,0:T(8,128)(2,1)}) custom-call(s32[2]{0:T(128)} %broadcast_3_sc_ref.2.sc_ref, bf16[256,256]{1,0:T(8,128)(2,1)} %get-tuple-element.276.refs_0_.refs_32_, bf16[256,256]{1,0:T(8,128)(2,1)} %get-tuple-element.281.refs_1_.refs_33_, bf16[256,256]{1,0:T(8,128)(2,1)} %get-tuple-element.216.refs_2_.refs_34_, ...), custom_call_target="tpu_custom_call" | custom-call | flops 2147483648 | bytes 4194304 | tf_op jit(solution)/shard_map/pallas_call | solution.py:627
  363.0 6.2 shard_map.194
  371.3 9.3 %shard_map.193 = (bf16[1024,1024]{1,0:T(8,128)(2,1)}, bf16[1024,1024]{1,0:T(8,128)(2,1)}) custom-call(s32[2]{0:T(128)} %broadcast_3_sc_ref.2.sc_ref, bf16[256,256]{1,0:T(8,128)(2,1)} %get-tuple-element.275.refs_0_.refs_48_, bf16[256,256]{1,0:T(8,128)(2,1)} %get-tuple-element.280.refs_1_.refs_49_, bf16[256,256]{1,0:T(8,128)(2,1)} %get-tuple-element.203.refs_2_.refs_50_, ...), custom_call_target="tpu_custom_call" | custom-call | flops 2147483648 | bytes 4194304 | tf_op jit(solution)/shard_map/pallas_call | solution.py:627
  382.7 20.9 %shard_map.195 = (bf16[1024,1024]{1,0:T(8,128)(2,1)}, f32[1024,1024]{1,0:T(8,128)}, bf16[1024,1024]{1,0:T(8,128)(2,1)}) custom-call(s32[2]{0:T(128)} %pad_add_fusion.sc_ref, bf16[512,256]{1,0:T(8,128)(2,1)} %copy-done.7, bf16[512,256]{1,0:T(8,128)(2,1)} %get-tuple-element.185.refs_1_, bf16[512,256]{1,0:T(8,128)(2,1)} %slice.1105.refs_2_, ...), custom_call_target="tpu_custom_call" | custom-call | flops 9663676416 | bytes 25165824 | tf_op jit(solution)/shard_map/pallas_call | solution.py:627
  403.6 2.4 constant_dynamic-slice_fusion.16
  407.6 2.7 convolution_multiply_fusion
  410.3 6.4 shard_map.196.refs_81_
  416.7 6.5 shard_map.197.refs_82_
  423.2 6.5 shard_map.198.refs_83_
  429.6 6.4 shard_map.199.refs_84_
  436.1 4.8 shard_map.200.refs_85_
  446.0 2.7 pad_maximum_fusion
  448.7 20.8 %shard_map.201 = (f32[1024,1024]{1,0:T(8,128)}, bf16[1024,1024]{1,0:T(8,128)(2,1)}) custom-call(s32[2]{0:T(128)} %broadcast_3_sc_ref.2.sc_ref, bf16[256,256]{1,0:T(8,128)(2,1)} %copy-done.29, bf16[256,256]{1,0:T(8,128)(2,1)} %copy-done.30, bf16[256,256]{1,0:T(8,128)(2,1)} %get-tuple-element.347.refs_2_, bf16[256,256]{1,0:T(8,128)(2,1)} %get-tuple-element.346.refs_3_, ...), custom_call_target="tpu_custom_call" | custom-call | flops 9663676416 | bytes 27267072 | tf_op jit(solution)/shard_map/pallas_call | solution.py:627
  469.5 6.2 shard_map.202.da_ref
  475.7 38.9 %shard_map.203 = (bf16[1024,1024]{1,0:T(8,128)(2,1)}, bf16[1024,1024]{1,0:T(8,128)(2,1)}, bf16[1024,1024]{1,0:T(8,128)(2,1)}, f32[1024,32]{1,0:T(8,128)}, f32[1024,32]{1,0:T(8,128)}) custom-call(bf16[1024,1024]{1,0:T(8,128)(2,1)} %shard_map.186.q_ref, bf16[1024,1024]{1,0:T(8,128)(2,1)} %get-tuple-element.74.k_ref, ...), custom_call_target="tpu_custom_call" | custom-call | flops 42949672960 | bytes 33554432 | tf_op jit(solution)/shard_map/pallas_call | solution.py:549
  514.6 10.3 %shard_map.204 = (f32[1024,1024]{1,0:T(8,128)}, bf16[1024,1024]{1,0:T(8,128)(2,1)}) custom-call(s32[2]{0:T(128)} %broadcast_3_sc_ref.2.sc_ref, bf16[256,512]{1,0:T(8,128)(2,1)} %get-tuple-element.308.refs_0_, bf16[256,512]{1,0:T(8,128)(2,1)} %get-tuple-element.306.refs_1_, bf16[256,512]{1,0:T(8,128)(2,1)} %get-tuple-element.303.refs_2_, ...), custom_call_target="tpu_custom_call" | custom-call | flops 2147483648 | bytes 12587008 | tf_op jit(solution)/shard_map/pallas_call | solution.py:627
  524.9 5.9 shard_map.205
  530.8 18.4 %shard_map.207 = (bf16[1024,512]{1,0:T(8,128)(2,1)}, bf16[1024,512]{1,0:T(8,128)(2,1)}, bf16[1024,512]{1,0:T(8,128)(2,1)}, f32[512,32]{1,0:T(8,128)}, f32[512,32]{1,0:T(8,128)}) custom-call(bf16[1024,512]{1,0:T(8,128)(2,1)} %get-tuple-element.68.q_ref, bf16[1024,512]{1,0:T(8,128)(2,1)} %get-tuple-element.69.k_ref, ...), custom_call_target="tpu_custom_call" | custom-call | flops 21474836480 | bytes 16777216 | tf_op jit(solution)/shard_map/pallas_call | solution.py:549
  551.9 18.3 %shard_map.206 = (bf16[1024,512]{1,0:T(8,128)(2,1)}, bf16[1024,512]{1,0:T(8,128)(2,1)}, bf16[1024,512]{1,0:T(8,128)(2,1)}, f32[512,32]{1,0:T(8,128)}, f32[512,32]{1,0:T(8,128)}) custom-call(bf16[1024,512]{1,0:T(8,128)(2,1)} %get-tuple-element.64.q_ref, bf16[1024,512]{1,0:T(8,128)(2,1)} %get-tuple-element.65.k_ref, ...), custom_call_target="tpu_custom_call" | custom-call | flops 21474836480 | bytes 16777216 | tf_op jit(solution)/shard_map/pallas_call | solution.py:549
  570.2 9.5 %shard_map.208 = bf16[512,1024]{1,0:T(8,128)(2,1)} custom-call(s32[2]{0:T(128)} %pad_add_fusion.1.sc_ref, bf16[256,512]{1,0:T(8,128)(2,1)} %get-tuple-element.333.refs_0_, bf16[256,512]{1,0:T(8,128)(2,1)} %get-tuple-element.330.refs_1_, bf16[256,512]{1,0:T(8,128)(2,1)} %get-tuple-element.327.refs_2_, bf16[256,512]{1,0:T(8,128)(2,1)} %get-tuple-element.324.refs_3_, ...), custom_call_target="tpu_custom_call" | custom-call | flops 3221225472 | bytes 16777216 | tf_op jit(solution)/shard_map/pallas_call | solution.py:627
  579.7 9.6 %shard_map.209 = bf16[512,1024]{1,0:T(8,128)(2,1)} custom-call(s32[2]{0:T(128)} %pad_add_fusion.2.sc_ref, bf16[256,512]{1,0:T(8,128)(2,1)} %get-tuple-element.333.refs_0_, bf16[256,512]{1,0:T(8,128)(2,1)} %get-tuple-element.330.refs_1_, bf16[256,512]{1,0:T(8,128)(2,1)} %get-tuple-element.327.refs_2_, bf16[256,512]{1,0:T(8,128)(2,1)} %get-tuple-element.324.refs_3_, ...), custom_call_target="tpu_custom_call" | custom-call | flops 3221225472 | bytes 16777216 | tf_op jit(solution)/shard_map/pallas_call | solution.py:627
  592.1 6.9 shard_map.211
  599.5 7.1 %shard_map.210 = bf16[512,1024]{1,0:T(8,128)(2,1)} custom-call(s32[2]{0:T(128)} %pad_add_fusion.1.sc_ref, bf16[256,512]{1,0:T(8,128)(2,1)} %get-tuple-element.309.refs_0_, bf16[256,512]{1,0:T(8,128)(2,1)} %get-tuple-element.305.refs_1_, bf16[256,512]{1,0:T(8,128)(2,1)} %get-tuple-element.302.refs_2_, bf16[256,512]{1,0:T(8,128)(2,1)} %get-tuple-element.299.refs_3_, ...), custom_call_target="tpu_custom_call" | custom-call | flops 2147483648 | bytes 8388608 | tf_op jit(solution)/shard_map/pallas_call | solution.py:627
  606.6 69.4 %all-reduce.3.cloned.1.call-done = f32[2,30,512]{2,1,0:T(8,128)} async-done(((f32[2,30,512]{2,1,0:T(8,128)}), f32[2,30,512]{2,1,0:T(8,128)}) %all-reduce.3.cloned.1.call-update) | async-done | bytes 122896 | tf_op jit(solution)/shard_map/psum | solution.py:913
  (293 shorter events, 141.3 us)
Async XLA Ops:
  8.0 591.5 %reduce-scatter.3.cloned.1.call-start = ((), (), s32[]{:S(2)}) async-start(), calls=%async_computation.3 | async-start | bytes 5242880 | tf_op jit(solution)/shard_map/reduce_scatter | solution.py:893
  12.3 30.1 %collective-permute-start.1 = (bf16[1024,256]{1,0:T(8,128)(2,1)}, bf16[1024,256]{1,0:T(8,128)(2,1)}, u32[]{:S(2)}, u32[]{:S(2)}) collective-permute-start(bf16[1024,256]{1,0:T(8,128)(2,1)} %get-tuple-element.350), channel_id=1, source_target_pairs={{0,16},{8,24},{16,0},{24,8},{1,17},{9,25},{17,1},{25,9},{2,18},{10... | collective-permute-start | bytes 1572872 | tf_op jit(solution)/shard_map/ppermute | solution.py:779
  15.2 25.5 %collective-permute-start.2 = (bf16[1024,256]{1,0:T(8,128)(2,1)}, bf16[1024,256]{1,0:T(8,128)(2,1)}, u32[]{:S(2)}, u32[]{:S(2)}) collective-permute-start(bf16[1024,256]{1,0:T(8,128)(2,1)} %get-tuple-element.350), channel_id=1, source_target_pairs={{0,4},{4,0},{1,5},{5,1},{2,6},{6,2},{3,7},{7,3},{8,12},{12,8},{9,1... | collective-permute-start | bytes 1572872 | tf_op jit(solution)/shard_map/ppermute | solution.py:780
  16.7 33.0 %collective-permute-start.28 = (bf16[3,256,512]{2,1,0:T(8,128)(2,1)}, bf16[3,256,512]{2,1,0:T(8,128)(2,1)}, u32[]{:S(2)}, u32[]{:S(2)}) collective-permute-start(bf16[3,256,512]{2,1,0:T(8,128)(2,1)} %param.17), channel_id=1, source_target_pairs={{0,8},{8,0},{16,24},{24,16},{1,9},{9,1},{17,25},{25,17},{2,10},{10... | collective-permute-start | bytes 2359304 | tf_op jit(solution)/shard_map/ppermute | solution.py:778
  16.7 37.0 %collective-permute-start.29 = (bf16[3,256,512]{2,1,0:T(8,128)(2,1)}, bf16[3,256,512]{2,1,0:T(8,128)(2,1)}, u32[]{:S(2)}, u32[]{:S(2)}) collective-permute-start(bf16[3,256,512]{2,1,0:T(8,128)(2,1)} %param.17), channel_id=1, source_target_pairs={{0,16},{8,24},{16,0},{24,8},{1,17},{9,25},{17,1},{25,9},{2,18},{10... | collective-permute-start | bytes 2359304 | tf_op jit(solution)/shard_map/ppermute | solution.py:779
  17.9 18.6 %collective-permute-start.35 = (bf16[2,32,512]{2,1,0:T(8,128)(2,1)}, bf16[2,32,512]{2,1,0:T(8,128)(2,1)}, u32[]{:S(2)}, u32[]{:S(2)}) collective-permute-start(bf16[2,32,512]{2,1,0:T(8,128)(2,1)} %pad.4), channel_id=1, source_target_pairs={{0,4},{4,0},{1,5},{5,1},{2,6},{6,2},{3,7},{7,3},{8,12},{12,8},{9,1... | collective-permute-start | bytes 196616 | tf_op jit(solution)/shard_map/ppermute | solution.py:780
  36.5 20.7 %collective-permute-start.31 = (bf16[3,256,512]{2,1,0:T(8,128)(2,1)}, bf16[3,256,512]{2,1,0:T(8,128)(2,1)}, u32[]{:S(2)}, u32[]{:S(2)}) collective-permute-start(bf16[3,256,512]{2,1,0:T(8,128)(2,1)} %param.17), channel_id=1, source_target_pairs={{0,4},{4,0},{1,5},{5,1},{2,6},{6,2},{3,7},{7,3},{8,12},{12,8},{9,1... | collective-permute-start | bytes 2359304 | tf_op jit(solution)/shard_map/ppermute | solution.py:780
  40.7 33.4 %collective-permute-start.36 = (bf16[3,256,512]{2,1,0:T(8,128)(2,1)S(1)}, bf16[3,256,512]{2,1,0:T(8,128)(2,1)}, u32[]{:S(2)}, u32[]{:S(2)}) collective-permute-start(bf16[3,256,512]{2,1,0:T(8,128)(2,1)S(1)} %copy-done.24), channel_id=1, source_target_pairs={{0,4},{4,0},{1,5},{5,1},{2,6},{6,2},{3,7},{7,3},{8,12},{12,8},{9,1... | collective-permute-start | bytes 2359304 | tf_op jit(solution)/shard_map/ppermute | solution.py:780
  42.4 35.7 %collective-permute-start.37 = (bf16[3,256,512]{2,1,0:T(8,128)(2,1)S(1)}, bf16[3,256,512]{2,1,0:T(8,128)(2,1)S(1)}, u32[]{:S(2)}, u32[]{:S(2)}) collective-permute-start(bf16[3,256,512]{2,1,0:T(8,128)(2,1)S(1)} %copy-done.24), channel_id=1, source_target_pairs={{0,8},{8,0},{16,24},{24,16},{1,9},{9,1},{17,25},{25,17},{2,10},{10... | collective-permute-start | bytes 2359304 | tf_op jit(solution)/shard_map/ppermute | solution.py:778
  49.7 30.9 %collective-permute-start.39 = (bf16[3,256,512]{2,1,0:T(8,128)(2,1)S(1)}, bf16[3,256,512]{2,1,0:T(8,128)(2,1)S(1)}, u32[]{:S(2)}, u32[]{:S(2)}) collective-permute-start(bf16[3,256,512]{2,1,0:T(8,128)(2,1)S(1)} %copy-done.24), channel_id=1, source_target_pairs={{0,16},{8,24},{16,0},{24,8},{1,17},{9,25},{17,1},{25,9},{2,18},{10... | collective-permute-start | bytes 2359304 | tf_op jit(solution)/shard_map/ppermute | solution.py:779
  53.7 124.4 %collective-permute-start = (bf16[4,1024,256]{2,1,0:T(8,128)(2,1)}, bf16[4,1024,256]{2,1,0:T(8,128)(2,1)}, u32[]{:S(2)}, u32[]{:S(2)}) collective-permute-start(bf16[4,1024,256]{2,1,0:T(8,128)(2,1)} %pad_maximum_fusion.1), channel_id=1, source_target_pairs={{0,8},{8,0},{16,24},{24,16},{1,9},{9,1},{17,25},{25,17},{2,10},{10... | collective-permute-start | bytes 6291464 | tf_op jit(solution)/shard_map/ppermute | solution.py:778
  57.2 39.2 %collective-permute-start.27 = (bf16[512,1024]{1,0:T(8,128)(2,1)S(1)}, bf16[512,1024]{1,0:T(8,128)(2,1)S(1)}, u32[]{:S(2)}, u32[]{:S(2)}) collective-permute-start(bf16[512,1024]{1,0:T(8,128)(2,1)S(1)} %copy-done.21), channel_id=1, source_target_pairs={{0,4},{4,0},{1,5},{5,1},{2,6},{6,2},{3,7},{7,3},{8,12},{12,8},{9,1... | collective-permute-start | bytes 3145736 | tf_op jit(solution)/shard_map/ppermute | solution.py:780
  74.1 12.7 %collective-permute-start.3 = (bf16[1024,256]{1,0:T(8,128)(2,1)}, bf16[1024,256]{1,0:T(8,128)(2,1)S(1)}, u32[]{:S(2)}, u32[]{:S(2)}) collective-permute-start(bf16[1024,256]{1,0:T(8,128)(2,1)} %collective-permute-done.2), channel_id=1, source_target_pairs={{0,16},{8,24},{16,0},{24,8},{1,17},{9,25},{17,1},{25,9},{2,18},{10... | collective-permute-start | bytes 1572872 | tf_op jit(solution)/shard_map/ppermute | solution.py:779
  78.1 40.8 %collective-permute-start.43 = (bf16[512,1024]{1,0:T(8,128)(2,1)S(1)}, bf16[512,1024]{1,0:T(8,128)(2,1)S(1)}, u32[]{:S(2)}, u32[]{:S(2)}) collective-permute-start(bf16[512,1024]{1,0:T(8,128)(2,1)S(1)} %copy-done.20), channel_id=1, source_target_pairs={{0,4},{4,0},{1,5},{5,1},{2,6},{6,2},{3,7},{7,3},{8,12},{12,8},{9,1... | collective-permute-start | bytes 3145736 | tf_op jit(solution)/shard_map/ppermute | solution.py:780
  80.6 60.1 %collective-permute-start.44 = (bf16[512,1024]{1,0:T(8,128)(2,1)S(1)}, bf16[512,1024]{1,0:T(8,128)(2,1)S(1)}, u32[]{:S(2)}, u32[]{:S(2)}) collective-permute-start(bf16[512,1024]{1,0:T(8,128)(2,1)S(1)} %copy-done.19), channel_id=1, source_target_pairs={{0,4},{4,0},{1,5},{5,1},{2,6},{6,2},{3,7},{7,3},{8,12},{12,8},{9,1... | collective-permute-start | bytes 3145736 | tf_op jit(solution)/shard_map/ppermute | solution.py:780
  86.8 59.4 %collective-permute-start.30 = (bf16[3,256,512]{2,1,0:T(8,128)(2,1)}, bf16[3,256,512]{2,1,0:T(8,128)(2,1)S(1)}, u32[]{:S(2)}, u32[]{:S(2)}) collective-permute-start(bf16[3,256,512]{2,1,0:T(8,128)(2,1)} %collective-permute-done.29), channel_id=1, source_target_pairs={{0,8},{8,0},{16,24},{24,16},{1,9},{9,1},{17,25},{25,17},{2,10},{10... | collective-permute-start | bytes 2359304 | tf_op jit(solution)/shard_map/ppermute | solution.py:778
  96.4 73.1 %collective-permute-start.32 = (bf16[3,256,512]{2,1,0:T(8,128)(2,1)}, bf16[3,256,512]{2,1,0:T(8,128)(2,1)S(1)}, u32[]{:S(2)}, u32[]{:S(2)}) collective-permute-start(bf16[3,256,512]{2,1,0:T(8,128)(2,1)} %collective-permute-done.31), channel_id=1, source_target_pairs={{0,8},{8,0},{16,24},{24,16},{1,9},{9,1},{17,25},{25,17},{2,10},{10... | collective-permute-start | bytes 2359304 | tf_op jit(solution)/shard_map/ppermute | solution.py:778
  118.9 51.8 %collective-permute-start.33 = (bf16[3,256,512]{2,1,0:T(8,128)(2,1)}, bf16[3,256,512]{2,1,0:T(8,128)(2,1)S(1)}, u32[]{:S(2)}, u32[]{:S(2)}) collective-permute-start(bf16[3,256,512]{2,1,0:T(8,128)(2,1)} %collective-permute-done.31), channel_id=1, source_target_pairs={{0,16},{8,24},{16,0},{24,8},{1,17},{9,25},{17,1},{25,9},{2,18},{10... | collective-permute-start | bytes 2359304 | tf_op jit(solution)/shard_map/ppermute | solution.py:779
  140.7 31.3 %collective-permute-start.38 = (bf16[3,256,512]{2,1,0:T(8,128)(2,1)}, bf16[3,256,512]{2,1,0:T(8,128)(2,1)}, u32[]{:S(2)}, u32[]{:S(2)}) collective-permute-start(bf16[3,256,512]{2,1,0:T(8,128)(2,1)} %collective-permute-done.36), channel_id=1, source_target_pairs={{0,8},{8,0},{16,24},{24,16},{1,9},{9,1},{17,25},{25,17},{2,10},{10... | collective-permute-start | bytes 2359304 | tf_op jit(solution)/shard_map/ppermute | solution.py:778
  146.2 29.5 %collective-permute-start.40 = (bf16[3,256,512]{2,1,0:T(8,128)(2,1)}, bf16[3,256,512]{2,1,0:T(8,128)(2,1)S(1)}, u32[]{:S(2)}, u32[]{:S(2)}) collective-permute-start(bf16[3,256,512]{2,1,0:T(8,128)(2,1)} %collective-permute-done.36), channel_id=1, source_target_pairs={{0,16},{8,24},{16,0},{24,8},{1,17},{9,25},{17,1},{25,9},{2,18},{10... | collective-permute-start | bytes 2359304 | tf_op jit(solution)/shard_map/ppermute | solution.py:779
  170.7 20.5 %collective-permute-start.14 = (bf16[512,256]{1,0:T(8,128)(2,1)S(1)}, bf16[512,256]{1,0:T(8,128)(2,1)S(1)}, u32[]{:S(2)}, u32[]{:S(2)}) collective-permute-start(bf16[512,256]{1,0:T(8,128)(2,1)S(1)} %copy-done.32), channel_id=1, source_target_pairs={{0,16},{8,24},{16,0},{24,8},{1,17},{9,25},{17,1},{25,9},{2,18},{10... | collective-permute-start | bytes 786440 | tf_op jit(solution)/shard_map/ppermute | solution.py:779
  172.0 37.3 %collective-permute-start.16 = (bf16[512,256]{1,0:T(8,128)(2,1)S(1)}, bf16[512,256]{1,0:T(8,128)(2,1)}, u32[]{:S(2)}, u32[]{:S(2)}) collective-permute-start(bf16[512,256]{1,0:T(8,128)(2,1)S(1)} %copy-done.32), channel_id=1, source_target_pairs={{0,4},{4,0},{1,5},{5,1},{2,6},{6,2},{3,7},{7,3},{8,12},{12,8},{9,1... | collective-permute-start | bytes 786440 | tf_op jit(solution)/shard_map/ppermute | solution.py:780
  176.7 32.6 %collective-permute-start.20 = (bf16[512,256]{1,0:T(8,128)(2,1)S(1)}, bf16[512,256]{1,0:T(8,128)(2,1)}, u32[]{:S(2)}, u32[]{:S(2)}) collective-permute-start(bf16[512,256]{1,0:T(8,128)(2,1)S(1)} %copy-done.41), channel_id=1, source_target_pairs={{0,8},{8,0},{16,24},{24,16},{1,9},{9,1},{17,25},{25,17},{2,10},{10... | collective-permute-start | bytes 786440 | tf_op jit(solution)/shard_map/ppermute | solution.py:778
  178.1 15.2 %collective-permute-start.42 = (bf16[3,256,512]{2,1,0:T(8,128)(2,1)S(1)}, bf16[3,256,512]{2,1,0:T(8,128)(2,1)S(1)}, u32[]{:S(2)}, u32[]{:S(2)}) collective-permute-start(bf16[3,256,512]{2,1,0:T(8,128)(2,1)S(1)} %collective-permute-done.40), channel_id=1, source_target_pairs={{0,8},{8,0},{16,24},{24,16},{1,9},{9,1},{17,25},{25,17},{2,10},{10... | collective-permute-start | bytes 2359304 | tf_op jit(solution)/shard_map/ppermute | solution.py:778
  182.7 10.4 %collective-permute-start.23 = (bf16[512,256]{1,0:T(8,128)(2,1)S(1)}, bf16[512,256]{1,0:T(8,128)(2,1)}, u32[]{:S(2)}, u32[]{:S(2)}) collective-permute-start(bf16[512,256]{1,0:T(8,128)(2,1)S(1)} %copy-done.41), channel_id=1, source_target_pairs={{0,4},{4,0},{1,5},{5,1},{2,6},{6,2},{3,7},{7,3},{8,12},{12,8},{9,1... | collective-permute-start | bytes 786440 | tf_op jit(solution)/shard_map/ppermute | solution.py:780
  191.2 19.6 %collective-permute-start.21 = (bf16[512,256]{1,0:T(8,128)(2,1)S(1)}, bf16[512,256]{1,0:T(8,128)(2,1)}, u32[]{:S(2)}, u32[]{:S(2)}) collective-permute-start(bf16[512,256]{1,0:T(8,128)(2,1)S(1)} %copy-done.41), channel_id=1, source_target_pairs={{0,16},{8,24},{16,0},{24,8},{1,17},{9,25},{17,1},{25,9},{2,18},{10... | collective-permute-start | bytes 786440 | tf_op jit(solution)/shard_map/ppermute | solution.py:779
  193.0 18.0 %collective-permute-start.25 = (bf16[512,256]{1,0:T(8,128)(2,1)}, bf16[512,256]{1,0:T(8,128)(2,1)}, u32[]{:S(2)}, u32[]{:S(2)}) collective-permute-start(bf16[512,256]{1,0:T(8,128)(2,1)} %collective-permute-done.23.refs_4_), channel_id=1, source_target_pairs={{0,16},{8,24},{16,0},{24,8},{1,17},{9,25},{17,1},{25,9},{2,18},{10... | collective-permute-start | bytes 786440 | tf_op jit(solution)/shard_map/ppermute | solution.py:779
  193.3 43.2 %collective-permute-start.5 = (bf16[3328,256]{1,0:T(8,128)(2,1)}, bf16[3328,256]{1,0:T(8,128)(2,1)S(1)}, u32[]{:S(2)}, u32[]{:S(2)}) collective-permute-start(bf16[3328,256]{1,0:T(8,128)(2,1)} %copy-done.36), channel_id=1, source_target_pairs={{0,1},{1,2},{2,3},{3,0},{4,5},{5,6},{6,7},{7,4},{8,9},{9,10},{10,1... | collective-permute-start | bytes 5111816 | tf_op jit(solution)/shard_map/ppermute | solution.py:781
  209.3 11.5 %collective-permute-start.24 = (bf16[512,256]{1,0:T(8,128)(2,1)}, bf16[512,256]{1,0:T(8,128)(2,1)S(1)}, u32[]{:S(2)}, u32[]{:S(2)}) collective-permute-start(bf16[512,256]{1,0:T(8,128)(2,1)} %collective-permute-done.23.refs_4_), channel_id=1, source_target_pairs={{0,8},{8,0},{16,24},{24,16},{1,9},{9,1},{17,25},{25,17},{2,10},{10... | collective-permute-start | bytes 786440 | tf_op jit(solution)/shard_map/ppermute | solution.py:778
  209.3 10.9 %collective-permute-start.18 = (bf16[512,256]{1,0:T(8,128)(2,1)}, bf16[512,256]{1,0:T(8,128)(2,1)}, u32[]{:S(2)}, u32[]{:S(2)}) collective-permute-start(bf16[512,256]{1,0:T(8,128)(2,1)} %collective-permute-done.16.refs_4_), channel_id=1, source_target_pairs={{0,16},{8,24},{16,0},{24,8},{1,17},{9,25},{17,1},{25,9},{2,18},{10... | collective-permute-start | bytes 786440 | tf_op jit(solution)/shard_map/ppermute | solution.py:779
  220.3 15.9 %collective-permute-start.13 = (bf16[512,256]{1,0:T(8,128)(2,1)S(1)}, bf16[512,256]{1,0:T(8,128)(2,1)}, u32[]{:S(2)}, u32[]{:S(2)}) collective-permute-start(bf16[512,256]{1,0:T(8,128)(2,1)S(1)} %copy-done.32), channel_id=1, source_target_pairs={{0,8},{8,0},{16,24},{24,16},{1,9},{9,1},{17,25},{25,17},{2,10},{10... | collective-permute-start | bytes 786440 | tf_op jit(solution)/shard_map/ppermute | solution.py:778
  220.5 49.5 %collective-permute-start.17 = (bf16[512,256]{1,0:T(8,128)(2,1)}, bf16[512,256]{1,0:T(8,128)(2,1)}, u32[]{:S(2)}, u32[]{:S(2)}) collective-permute-start(bf16[512,256]{1,0:T(8,128)(2,1)} %collective-permute-done.16.refs_4_), channel_id=1, source_target_pairs={{0,8},{8,0},{16,24},{24,16},{1,9},{9,1},{17,25},{25,17},{2,10},{10... | collective-permute-start | bytes 786440 | tf_op jit(solution)/shard_map/ppermute | solution.py:778
  220.8 49.1 %collective-permute-start.15 = (bf16[512,256]{1,0:T(8,128)(2,1)S(1)}, bf16[512,256]{1,0:T(8,128)(2,1)}, u32[]{:S(2)}, u32[]{:S(2)}) collective-permute-start(bf16[512,256]{1,0:T(8,128)(2,1)S(1)} %collective-permute-done.14.refs_2_), channel_id=1, source_target_pairs={{0,8},{8,0},{16,24},{24,16},{1,9},{9,1},{17,25},{25,17},{2,10},{10... | collective-permute-start | bytes 786440 | tf_op jit(solution)/shard_map/ppermute | solution.py:778
  221.1 48.9 %collective-permute-start.19 = (bf16[512,256]{1,0:T(8,128)(2,1)}, bf16[512,256]{1,0:T(8,128)(2,1)}, u32[]{:S(2)}, u32[]{:S(2)}) collective-permute-start(bf16[512,256]{1,0:T(8,128)(2,1)} %collective-permute-done.18.refs_6_), channel_id=1, source_target_pairs={{0,8},{8,0},{16,24},{24,16},{1,9},{9,1},{17,25},{25,17},{2,10},{10... | collective-permute-start | bytes 786440 | tf_op jit(solution)/shard_map/ppermute | solution.py:778
  236.2 42.4 %collective-permute-start.4 = (bf16[3328,256]{1,0:T(8,128)(2,1)}, bf16[3328,256]{1,0:T(8,128)(2,1)S(1)}, u32[]{:S(2)}, u32[]{:S(2)}) collective-permute-start(bf16[3328,256]{1,0:T(8,128)(2,1)} %copy-done.36), channel_id=1, source_target_pairs={{0,8},{8,0},{16,24},{24,16},{1,9},{9,1},{17,25},{25,17},{2,10},{10... | collective-permute-start | bytes 5111816 | tf_op jit(solution)/shard_map/ppermute | solution.py:778
  236.5 53.3 %collective-permute-start.7 = (bf16[3328,256]{1,0:T(8,128)(2,1)S(1)}, bf16[3328,256]{1,0:T(8,128)(2,1)}, u32[]{:S(2)}, u32[]{:S(2)}) collective-permute-start(bf16[3328,256]{1,0:T(8,128)(2,1)S(1)} %collective-permute-done.5), channel_id=1, source_target_pairs={{0,1},{1,2},{2,3},{3,0},{4,5},{5,6},{6,7},{7,4},{8,9},{9,10},{10,1... | collective-permute-start | bytes 5111816 | tf_op jit(solution)/shard_map/ppermute | solution.py:781
  278.6 20.5 %collective-permute-start.6 = (bf16[3328,256]{1,0:T(8,128)(2,1)S(1)}, bf16[3328,256]{1,0:T(8,128)(2,1)}, u32[]{:S(2)}, u32[]{:S(2)}) collective-permute-start(bf16[3328,256]{1,0:T(8,128)(2,1)S(1)} %collective-permute-done.5), channel_id=1, source_target_pairs={{0,8},{8,0},{16,24},{24,16},{1,9},{9,1},{17,25},{25,17},{2,10},{10... | collective-permute-start | bytes 5111816 | tf_op jit(solution)/shard_map/ppermute | solution.py:778
  289.8 41.8 %collective-permute-start.9 = (bf16[3328,256]{1,0:T(8,128)(2,1)}, bf16[3328,256]{1,0:T(8,128)(2,1)S(1)}, u32[]{:S(2)}, u32[]{:S(2)}) collective-permute-start(bf16[3328,256]{1,0:T(8,128)(2,1)} %collective-permute-done.7), channel_id=1, source_target_pairs={{0,1},{1,2},{2,3},{3,0},{4,5},{5,6},{6,7},{7,4},{8,9},{9,10},{10,1... | collective-permute-start | bytes 5111816 | tf_op jit(solution)/shard_map/ppermute | solution.py:781
  295.2 49.5 %collective-permute-start.8 = (bf16[3328,256]{1,0:T(8,128)(2,1)}, bf16[3328,256]{1,0:T(8,128)(2,1)}, u32[]{:S(2)}, u32[]{:S(2)}) collective-permute-start(bf16[3328,256]{1,0:T(8,128)(2,1)} %collective-permute-done.7), channel_id=1, source_target_pairs={{0,8},{8,0},{16,24},{24,16},{1,9},{9,1},{17,25},{25,17},{2,10},{10... | collective-permute-start | bytes 5111816 | tf_op jit(solution)/shard_map/ppermute | solution.py:778
  332.6 14.1 %collective-permute-start.11 = (bf16[4,256,256]{2,1,0:T(8,128)(2,1)S(1)}, bf16[4,256,256]{2,1,0:T(8,128)(2,1)S(1)}, u32[]{:S(2)}, u32[]{:S(2)}) collective-permute-start(bf16[4,256,256]{2,1,0:T(8,128)(2,1)S(1)} %get-tuple-element.349), channel_id=1, source_target_pairs={{0,16},{8,24},{16,0},{24,8},{1,17},{9,25},{17,1},{25,9},{2,18},{10... | collective-permute-start | bytes 1572872 | tf_op jit(solution)/shard_map/ppermute | solution.py:779
  344.6 24.6 %collective-permute-start.10 = (bf16[3328,256]{1,0:T(8,128)(2,1)S(1)}, bf16[3328,256]{1,0:T(8,128)(2,1)}, u32[]{:S(2)}, u32[]{:S(2)}) collective-permute-start(bf16[3328,256]{1,0:T(8,128)(2,1)S(1)} %collective-permute-done.9), channel_id=1, source_target_pairs={{0,8},{8,0},{16,24},{24,16},{1,9},{9,1},{17,25},{25,17},{2,10},{10... | collective-permute-start | bytes 5111816 | tf_op jit(solution)/shard_map/ppermute | solution.py:778
  347.8 14.3 %collective-permute-start.12 = (bf16[2,4,256,256]{3,2,1,0:T(8,128)(2,1)}, bf16[2,4,256,256]{3,2,1,0:T(8,128)(2,1)S(1)}, u32[]{:S(2)}, u32[]{:S(2)}) collective-permute-start(bf16[2,4,256,256]{3,2,1,0:T(8,128)(2,1)} %pad_maximum_fusion.7), channel_id=1, source_target_pairs={{0,8},{8,0},{16,24},{24,16},{1,9},{9,1},{17,25},{25,17},{2,10},{10... | collective-permute-start | bytes 3145736 | tf_op jit(solution)/shard_map/ppermute | solution.py:778
  406.1 271.5 %collective-permute-start.45 = (bf16[512,1024]{1,0:T(8,128)(2,1)}, bf16[512,1024]{1,0:T(8,128)(2,1)}, u32[]{:S(2)}, u32[]{:S(2)}) collective-permute-start(bf16[512,1024]{1,0:T(8,128)(2,1)} %constant_dynamic-slice_fusion.16), channel_id=1, source_target_pairs={{0,4},{4,0},{1,5},{5,1},{2,6},{6,2},{3,7},{7,3},{8,12},{12,8},{9,1... | collective-permute-start | bytes 3145736 | tf_op jit(solution)/shard_map/ppermute | solution.py:780
  448.7 227.3 %all-reduce.3.cloned.1.call-start = ((), (), s32[]{:S(2)}) async-start(), calls=%async_computation.2 | async-start | bytes 262144 | tf_op jit(solution)/shard_map/psum | solution.py:913
  551.4 39.8 %collective-permute-start.48 = (f32[2,30,512]{2,1,0:T(8,128)S(1)}, f32[2,30,512]{2,1,0:T(8,128)S(1)}, u32[]{:S(2)}, u32[]{:S(2)}) collective-permute-start(f32[2,30,512]{2,1,0:T(8,128)S(1)} %pad_maximum_fusion.10), channel_id=1, source_target_pairs={{0,4},{4,0},{1,5},{5,1},{2,6},{6,2},{3,7},{7,3},{8,12},{12,8},{9,1... | collective-permute-start | bytes 368648 | tf_op jit(solution)/shard_map/ppermute | solution.py:780
  589.3 91.7 %collective-permute-start.46 = (bf16[512,1024]{1,0:T(8,128)(2,1)}, bf16[512,1024]{1,0:T(8,128)(2,1)S(1)}, u32[]{:S(2)}, u32[]{:S(2)}) collective-permute-start(bf16[512,1024]{1,0:T(8,128)(2,1)} %shard_map.209), channel_id=1, source_target_pairs={{0,4},{4,0},{1,5},{5,1},{2,6},{6,2},{3,7},{7,3},{8,12},{12,8},{9,1... | collective-permute-start | bytes 3145736 | tf_op jit(solution)/shard_map/ppermute | solution.py:780
  591.8 93.6 %reduce-scatter.5.cloned.1.call-start = ((), (), s32[]{:S(2)}) async-start(), calls=%async_computation.4 | async-start | bytes 1179648 | tf_op jit(solution)/shard_map/reduce_scatter | solution.py:894
  599.0 83.6 %collective-permute-start.47 = (bf16[512,1024]{1,0:T(8,128)(2,1)}, bf16[512,1024]{1,0:T(8,128)(2,1)}, u32[]{:S(2)}, u32[]{:S(2)}) collective-permute-start(bf16[512,1024]{1,0:T(8,128)(2,1)} %shard_map.211), channel_id=1, source_target_pairs={{0,4},{4,0},{1,5},{5,1},{2,6},{6,2},{3,7},{7,3},{8,12},{12,8},{9,1... | collective-permute-start | bytes 3145736 | tf_op jit(solution)/shard_map/ppermute | solution.py:780
  (49 other events, 672.5 us)
Sparse Core Ops, SparseCore 0:
  448.8 74.0 reduce-scatter.2
  599.6 38.5 reduce-scatter.4
Sparse Core Ops, SparseCore 1:
  591.9 84.0 all-reduce.2

commit v2 on v0

--- a/solution.py
+++ b/solution.py
@@ -1,6 +1,11 @@
+import functools
+import math
+
 import jax
 import jax.numpy as jnp
 from jax import lax
+from jax.experimental import pallas as pl
+from jax.experimental.pallas import tpu as pltpu
 from jax.sharding import PartitionSpec as P
 
 HEAD_DIM = 64
@@ -351,9 +356,1171 @@
     )
 
 
+F32 = jnp.float32
+BF = jnp.bfloat16
+EPS = 1e-05
+LOG2E = 1.4426950408889634
+TILE = 256
+FEED_SPLIT = 2
+
+BQF = 512
+BQ = 512
+PRE = 32
+VMEM_BYTES = 60 * 2**20
+NEG = -1e30
+HBM = pl.BlockSpec(memory_space=pl.ANY)
+LN2 = 0.6931471805599453
+
+
+def dot_mm(a, b, ca, cb):
+    return lax.dot_general(a, b, (((ca,), (cb,)), ((), ())), preferred_element_type=jnp.float32)
+
+
+def pick_head(h, mat):
+    rows = lax.broadcasted_iota(jnp.int32, mat.shape, 0)
+    return jnp.where((rows // HEAD_DIM) == h, mat, jnp.zeros_like(mat))
+
+
+def attend_pair(causal, n, q, k, v, pk, pv, p_ref, pp_ref):
+    t = q.shape[0]
+    s = k.shape[0]
+    nb = t // BQF
+    qt = q.T
+    vt = v.T
+    ones = jnp.ones((16, s), jnp.bfloat16)
+    work = [(h, j) for h in range(2) for j in range(nb)]
+
+    def scores(h, j):
+        kk = (j + 1) * BQF if causal else s
+        qb = pick_head(h, qt[:, j * BQF:(j + 1) * BQF])
+        return dot_mm(k[:kk], qb, 1, 0), dot_mm(pk, qb, 1, 0) if causal else None
+
+    res = {}
+    ahead = scores(*work[0])
+    for w, (h, j) in enumerate(work):
+        st, sp = ahead
+        if w + 1 < len(work):
+            ahead = scores(*work[w + 1])
+        kk = st.shape[0]
+        js = slice(j * BQF, (j + 1) * BQF)
+        if causal:
+            krow = lax.broadcasted_iota(jnp.int32, (BQF, BQF), 0)
+            qcol = lax.broadcasted_iota(jnp.int32, (BQF, BQF), 1)
+            diag = jnp.where(krow <= qcol, st[kk - BQF:], NEG)
+            st = jnp.concatenate([st[:kk - BQF], diag], axis=0) if kk > BQF else diag
+            prow = lax.broadcasted_iota(jnp.int32, sp.shape, 0)
+            sp = jnp.where(prow < n, sp, NEG)
+            m = jnp.maximum(jnp.max(st, axis=0, keepdims=True), jnp.max(sp, axis=0, keepdims=True))
+            pp = jnp.exp2(sp - m).astype(jnp.bfloat16)
+            pp_ref[h, :, js] = pp
+        else:
+            krow = lax.broadcasted_iota(jnp.int32, st.shape, 0)
+            st = jnp.where(krow < n, st, NEG)
+            m = jnp.max(st, axis=0, keepdims=True)
+        p = jnp.exp2(st - m).astype(jnp.bfloat16)
+        p_ref[h, :kk, js] = p
+        hs = slice(h * HEAD_DIM, (h + 1) * HEAD_DIM)
+        ot = dot_mm(jnp.concatenate([vt[hs, :kk], ones[:, :kk]], axis=0), p, 1, 0)
+        if causal:
+            ot += dot_mm(jnp.concatenate([pv.T[hs], ones[:, :PRE]], axis=0), pp, 1, 0)
+        il = 1.0 / ot[HEAD_DIM:HEAD_DIM + 1]
+        res[h, j] = (ot[:HEAD_DIM] * il, il)
+    ils = [jnp.concatenate([res[h, j][1] for j in range(nb)], axis=1) for h in range(2)]
+    at = jnp.concatenate([jnp.concatenate([res[h, j][0] for j in range(nb)], axis=1) for h in range(2)], axis=0)
+    return at.astype(jnp.bfloat16).T, jnp.concatenate(ils, axis=0)
+
+
+def sum_terms(keep_hbm, give_hbm, down_ref, up_ref, keep, part, first, second, third, fourth, out2, out3, out4, near, send, recv):
+    g = pl.program_id(0)
+    last = pl.num_programs(0) - 1
+    dp, y, z, side, over, up = axes_here()
+    nz = lax.axis_size("adp")
+    rows = part.shape[1] // nz
+    wide = out3.shape[2]
+
+    def far(src, dst, peer, i):
+        return pltpu.make_async_remote_copy(src_ref=src, dst_ref=dst, send_sem=send.at[i], recv_sem=recv.at[i],
+                                            device_id=peer, device_id_type=pl.DeviceIdType.MESH)
+
+    load = pltpu.make_async_copy(keep_hbm, keep, near.at[0])
+    core = far(give_hbm, first, side, 0)
+    across = far(out2, second, over, 1)
+    beside = far(out3, third, up, 2)
+    along = [far(out4.at[k - 1], fourth.at[k - 1], {"adp": lax.rem(z + nz - k, nz)}, 2 + k) for k in range(1, nz)]
+
+    @pl.when(g == 0)
+    def _():
+        meet([side, over, up] + [{"adp": lax.rem(z + k, nz)} for k in range(1, nz)])
+        load.start()
+        core.start()
+
+    @pl.when(g == 1)
+    def _():
+        load.wait()
+        core.wait_recv()
+        out2[...] = (keep[:, 1] + first[:, 1].astype(jnp.float32)).astype(jnp.bfloat16)
+        across.start()
+
+    @pl.when(g == last // 2 + 1)
+    def _():
+        across.wait_recv()
+        keep[:, 0] = keep[:, 0] + first[:, 0].astype(jnp.float32) + second[...].astype(jnp.float32)
+        mine = pl.ds(pl.multiple_of(y * wide, wide), wide)
+        other = pl.ds(pl.multiple_of((1 - y) * wide, wide), wide)
+        out3[...] = keep[:, 0, :, other].astype(jnp.bfloat16)
+        part[...] = keep[:, 0, :, mine]
+        beside.start()
+
+    @pl.when(g == last - 1)
+    def _():
+        beside.wait_recv()
+        part[...] = part[...] + third[...].astype(jnp.float32)
+        for k in range(1, nz):
+            out4[k - 1] = part[:, k * rows:(k + 1) * rows].astype(jnp.bfloat16)
+            along[k - 1].start()
+
+    @pl.when(g == last)
+    def _():
+        total = part[:, :rows]
+        for k in range(1, nz):
+            along[k - 1].wait_recv()
+            total = total + fourth[k - 1].astype(jnp.float32)
+        down_ref[...] = total[0].T
+        up_ref[...] = total[1]
+        for c in [core, across, beside] + along:
+            c.wait_send()
+
+
+def attn_bwd_body(causal, q_ref, k_ref, v_ref, a_ref, da_ref, l_ref, p_ref, *rest):
+    if causal:
+        pp_ref, pre_ref, moved, _, dq_ref, dk_ref, dv_ref, dpre_ref, landed, sems = rest
+        y = lax.axis_index("mp")
+        carry = pltpu.make_async_remote_copy(
+            src_ref=moved, dst_ref=landed.at[y], send_sem=sems.at[0], recv_sem=sems.at[1],
+            device_id={"mp": 1 - y}, device_id_type=pl.DeviceIdType.MESH)
+
+        @pl.when(pl.program_id(0) == 0)
+        def _():
+            meet([{"mp": 1 - y}])
+            carry.start()
+    else:
+        pp_ref, pre_ref, dpre_ref = None, None, None
+        keep_ref, give_ref, dq_ref, dk_ref, dv_ref, down_ref, up_ref = rest[:7]
+        sum_terms(keep_ref, give_ref, down_ref, up_ref, *rest[7:])
+    t = q_ref.shape[0]
+    s = k_ref.shape[0]
+    nb = t // BQ
+    qt = q_ref[...].T
+    kt = k_ref[...].T
+    dat = da_ref[...].T.astype(jnp.float32)
+    prod = dat * a_ref[...].T.astype(jnp.float32)
+    pkt = pre_ref[0].T if causal else None
+    work = [(h, j) for h in range(2) for j in range(nb)]
+    head = {}
+    for h in range(2):
+        hs = slice(h * HEAD_DIM, (h + 1) * HEAD_DIM)
+        il = l_ref[0, h:h + 1]
+        head[h] = ((dat * il).astype(jnp.bfloat16), jnp.sum(prod[hs], axis=0, keepdims=True) * il)
+
+    def soft_grad(h, j):
+        js = slice(j * BQ, (j + 1) * BQ)
+        kk = (j + 1) * BQ if causal else s
+        dab = pick_head(h, head[h][0][:, js])
+        return dot_mm(v_ref[:kk], dab, 1, 0), dot_mm(pre_ref[1], dab, 1, 0) if causal else None
+
+    def add(tot, new):
+        return new if tot is None else tot + new
+
+    res = {}
+    dpk = [None, None]
+    dpv = [None, None]
+    dkb = [[None] * nb, [None] * nb]
+    dvb = [[None] * nb, [None] * nb]
+    ahead = soft_grad(*work[0])
+    for w, (h, j) in enumerate(work):
+        dp, dpp = ahead
+        if w + 1 < len(work):
+            ahead = soft_grad(*work[w + 1])
+        hs = slice(h * HEAD_DIM, (h + 1) * HEAD_DIM)
+        js = slice(j * BQ, (j + 1) * BQ)
+        kk = dp.shape[0]
+        dl = head[h][1][:, js]
+        dah = head[h][0][hs, js]
+        p = p_ref[h, :kk, js]
+        ds = (p.astype(jnp.float32) * (dp - dl)).astype(jnp.bfloat16)
+        dq = dot_mm(kt[hs, :kk], ds, 1, 0)
+        if causal:
+            pp = pp_ref[h, :, js]
+            dsp = (pp.astype(jnp.float32) * (dpp - dl)).astype(jnp.bfloat16)
+            dq += dot_mm(pkt[hs], dsp, 1, 0)
+            dpk[h] = add(dpk[h], dot_mm(qt[hs, js], dsp, 1, 1))
+            dpv[h] = add(dpv[h], dot_mm(dah, pp, 1, 1))
+        res[h, j] = dq
+        dv = dot_mm(dah, p, 1, 1)
+        dk = dot_mm(qt[hs, js], ds, 1, 1)
+        if causal:
+            for i in range(kk // BQ):
+                dvb[h][i] = add(dvb[h][i], dv[:, i * BQ:(i + 1) * BQ])
+                dkb[h][i] = add(dkb[h][i], dk[:, i * BQ:(i + 1) * BQ])
+        else:
+            dvb[h] = [add(dvb[h][0], dv)]
+            dkb[h] = [add(dkb[h][0], dk)]
+    both = lambda f: jnp.concatenate([f(0), f(1)], axis=0)
+    dq_ref[...] = (both(lambda h: jnp.concatenate([res[h, j] for j in range(nb)], axis=1))
+                   * HEAD_DIM ** -0.5).astype(jnp.bfloat16).T
+    dk_ref[...] = (both(lambda h: jnp.concatenate(dkb[h], axis=1)) * LN2).astype(jnp.bfloat16).T
+    dv_ref[...] = both(lambda h: jnp.concatenate(dvb[h], axis=1)).astype(jnp.bfloat16).T
+    if causal:
+        dpre_ref[0] = both(lambda h: dpk[h]).T * LN2
+        dpre_ref[1] = both(lambda h: dpv[h]).T
+
+        @pl.when(pl.program_id(0) == pl.num_programs(0) - 1)
+        def _():
+            carry.wait()
+
+
+def attn_bwd(q, k, v, a, da, il, p, pp=None, pre=None, moved=None, landed=None, keep=None, give=None):
+    t, w = q.shape
+    s = k.shape[0]
+    pairs = w // 128
+    causal = pre is not None
+    col = lambda g: (0, g)
+    lead = lambda g: (g, 0, 0)
+    tail = lambda g: (0, 0, g)
+    fixed = lambda g: (0, 0)
+    f32, bf = jnp.float32, jnp.bfloat16
+    vm = pltpu.VMEM
+    if not causal:
+        nz = lax.axis_size("adp")
+        bott = keep.shape[2]
+        rows, wide = bott // nz, TILE // 2
+    return pl.pallas_call(
+        functools.partial(attn_bwd_body, causal),
+        grid=(pairs,),
+        in_specs=[
+            pl.BlockSpec((t, 128), col), pl.BlockSpec((s, 128), col), pl.BlockSpec((s, 128), col),
+            pl.BlockSpec((t, 128), col), pl.BlockSpec((t, 128), col),
+            pl.BlockSpec((1, 2, t), lead), pl.BlockSpec((2, s, t), lead),
+        ] + ([pl.BlockSpec((2, PRE, t), lead), pl.BlockSpec((2, PRE, 128), tail), HBM, HBM] if causal else [HBM, HBM]),
+        out_specs=[
+            pl.BlockSpec((t, 128), col), pl.BlockSpec((s, 128), col), pl.BlockSpec((s, 128), col),
+        ] + ([pl.BlockSpec((2, PRE, 128), tail), HBM] if causal else [pl.BlockSpec((rows, wide), fixed)] * 2),
+        out_shape=[
+            jax.ShapeDtypeStruct((t, w), bf), jax.ShapeDtypeStruct((s, w), bf), jax.ShapeDtypeStruct((s, w), bf),
+        ] + ([jax.ShapeDtypeStruct((2, PRE, w), f32), jax.ShapeDtypeStruct(landed.shape, bf)] if causal
+           else [jax.ShapeDtypeStruct((rows, wide), f32)] * 2),
+        scratch_shapes=[pltpu.SemaphoreType.DMA((2,))] if causal else [
+            vm(keep.shape, f32), vm((2, bott, wide), f32), vm(keep.shape, bf), vm((2, bott, TILE), bf), vm((2, bott, wide), bf),
+            vm((nz - 1, 2, rows, wide), bf), vm((2, bott, TILE), bf), vm((2, bott, wide), bf), vm((nz - 1, 2, rows, wide), bf),
+            pltpu.SemaphoreType.DMA((1,)), pltpu.SemaphoreType.DMA((nz + 2,)), pltpu.SemaphoreType.DMA((nz + 2,))],
+        input_output_aliases={10: 4} if causal else {},
+        compiler_params=pltpu.CompilerParams(
+            vmem_limit_bytes=VMEM_BYTES, collective_id=3 if causal else 5, has_side_effects=True),
+        cost_estimate=pl.CostEstimate(flops=40 * t * s * w, bytes_accessed=4 * t * s * pairs, transcendentals=0),
+    )(q, k, v, a, da, il, p, *((pp, pre, moved, landed) if causal else (keep, give)))
+
+
+def erf_parts(v):
+    mag = jnp.abs(v)
+    expo = jnp.exp2(v * v * (-0.5 * LOG2E))
+    t = 1.0 / (1.0 + (0.3275911 * 0.5 ** 0.5) * mag)
+    poly = t * (0.254829592 + t * (-0.284496736 + t * (1.421413741 + t * (-1.453152027 + t * 1.061405429))))
+    half = 0.5 * poly * expo
+    return jnp.where(v < 0.0, half, 1.0 - half), expo * (2.0 * math.pi) ** -0.5
+
+
+def gelu_pair(v):
+    cdf, pdf = erf_parts(v)
+    return v * cdf, cdf + v * pdf
+
+
+def normalize(z):
+    centered = z - jnp.mean(z, axis=-1, keepdims=True)
+    inv = lax.rsqrt(jnp.mean(centered * centered, axis=-1, keepdims=True) + EPS)
+    return centered * inv, inv
+
+
+def norm_back(e, u, inv, gain):
+    w = e * gain
+    return inv * (w - jnp.mean(w, axis=-1, keepdims=True) - u * jnp.mean(w * u, axis=-1, keepdims=True))
+
+
+def stack_rows(refs):
+    return jnp.concatenate([r[...] for r in refs], axis=0)
+
+
+def stack_cols(refs):
+    return jnp.concatenate([r[...] for r in refs], axis=1)
+
+
+def nn(lhs, tiles):
+    return dot_mm(lhs, stack_rows(tiles), 1, 0)
+
+
+def nt(lhs, tiles):
+    return dot_mm(lhs, stack_cols(tiles), 1, 1)
+
+
+def place_cols(value_ref, dp):
+    n = value_ref.shape[1] // TILE
+    return jnp.concatenate(
+        [value_ref[:, pl.ds(pl.multiple_of((dp ^ r) * TILE, TILE), TILE)] for r in range(n)], axis=1)
+
+
+def unplace_store(out, value, dp):
+    for r in range(value.shape[1] // TILE):
+        out[:, pl.ds(pl.multiple_of((dp ^ r) * TILE, TILE), TILE)] = (
+            value[:, r * TILE:(r + 1) * TILE].astype(out.dtype))
+
+
+class Exchange:
+    def __init__(self, buf, out, local, send, recv, half):
+        self.refs = buf, out, local, send, recv
+        self.count, self.tile = buf.shape[0], buf.shape[1]
+        self.half = half
+        self.y = lax.axis_index("mp")
+
+    def copies(self, i):
+        buf, out, local, send, recv = self.refs
+        rows = pl.ds(i * self.tile % self.half, self.tile)
+        dst = out.at[self.y, rows]
+        far = pltpu.make_async_remote_copy(src_ref=buf.at[i], dst_ref=dst, send_sem=send.at[i], recv_sem=recv.at[i],
+                                           device_id={"mp": 1 - self.y}, device_id_type=pl.DeviceIdType.MESH)
+        return pltpu.make_async_copy(buf.at[i], dst, local.at[i]), far
+
+    def here(self, i):
+        return self.y == i * self.tile // self.half
+
+    def buffer(self, i):
+        return self.refs[0].at[i]
+
+    def send(self, i):
+        near, far = self.copies(i)
+
+        @pl.when(self.here(i))
+        def _():
+            near.start()
+
+        @pl.when(jnp.logical_not(self.here(i)))
+        def _():
+            far.start()
+
+    def finish(self):
+        for i in range(self.count):
+            near, far = self.copies(i)
+
+            @pl.when(self.here(i))
+            def _():
+                near.wait()
+                far.wait_recv()
+
+            @pl.when(jnp.logical_not(self.here(i)))
+            def _():
+                far.wait_send()
+
+
+def tiled(weights, rows, consts, outs, body, tile, steps, exchange=None, scratch=(), flops=0):
+    nw, nr, nc, no = len(weights), len(rows), len(consts), len(outs)
+    picks = [c for _, _, c in weights]
+    piece = [own.shape if c is None else own.shape[1:] for own, _, c in weights]
+    more = 1 if exchange else 0
+
+    def kernel(*refs):
+        srcs, refs = refs[:2 * nw], refs[2 * nw:]
+        row_refs, const_refs, out_refs = refs[:nr], refs[nr:nr + nc], refs[nr + nc:nr + nc + no]
+        refs = refs[nr + nc + no:]
+        result, refs = refs[:more], refs[more:]
+        wv, sems, refs = refs[:nw], refs[nw], refs[nw + 1:]
+        step = pl.program_id(0)
+        ex = Exchange(refs[0], result[0], *refs[1:4], exchange[1]) if exchange else None
+        own_scratch = refs[4 * more:]
+
+        def copies(i):
+            own, far, c = srcs[2 * i], srcs[2 * i + 1], picks[i]
+            own = own if c is None else own.at[c]
+            some = lambda s, rs: far.at[s, rs] if c is None else far.at[s, rs, c]
+            yield pltpu.make_async_copy(own, wv[i].at[0, 0], sems.at[i, 0])
+            yield pltpu.make_async_copy(some(0, pl.ds(1, 3)), wv[i].at[0, pl.ds(1, 3)], sems.at[i, 1])
+            yield pltpu.make_async_copy(some(1, pl.ds(0, 4)), wv[i].at[1], sems.at[i, 2])
+
+        @pl.when(step == 0)
+        def _():
+            for i in range(nw):
+                for copy in copies(i):
+                    copy.start()
+            if exchange:
+                meet([{"mp": 1 - lax.axis_index("mp")}])
+
+        def need(i):
+            @pl.when(step == 0)
+            def _():
+                for copy in copies(i):
+                    copy.wait()
+
+        def put(value):
+            dp = lax.axis_index("dp")
+            unplace_store(ex.buffer(step), value, dp)
+            for i in range(steps):
+                @pl.when(step == i)
+                def _():
+                    ex.send(i)
+
+        body(wv, need, row_refs, const_refs, out_refs, own_scratch, put)
+        if exchange:
+            @pl.when(step == steps - 1)
+            def _():
+                ex.finish()
+
+    whole = lambda a: pl.BlockSpec(a.shape, lambda i: (0,) * a.ndim, pipeline_mode=pl.Buffered(1))
+    ex_out, ex_shape, ex_scratch = [], [], []
+    if exchange:
+        _, half, cols = exchange
+        ex_out, ex_shape = [HBM], [jax.ShapeDtypeStruct((2, half, cols), BF)]
+        ex_scratch = [pltpu.VMEM((steps, tile, cols), BF)] + [pltpu.SemaphoreType.DMA((steps,))] * 3
+    return pl.pallas_call(
+        kernel,
+        grid=(steps,),
+        in_specs=[HBM] * (2 * nw) + [spec for _, spec in rows] + [whole(c) for c in consts],
+        out_specs=[pl.BlockSpec(shape, index) for _, _, shape, index in outs] + ex_out,
+        out_shape=[jax.ShapeDtypeStruct(shape, dtype) for shape, dtype, _, _ in outs] + ex_shape,
+        scratch_shapes=[pltpu.VMEM((2, 4) + tuple(p), BF) for p in piece] + [pltpu.SemaphoreType.DMA((nw, 3))]
+        + ex_scratch + list(scratch),
+        compiler_params=pltpu.CompilerParams(
+            vmem_limit_bytes=VMEM_BYTES, **(dict(collective_id=exchange[0], has_side_effects=True) if exchange else {})),
+        cost_estimate=pl.CostEstimate(flops=flops, bytes_accessed=16 * 2**20, transcendentals=0),
+    )(*[a for own, far, _ in weights for a in (own, far)], *[r[0] for r in rows], *consts)
+
+
+def last_gradient(wq, dz1, dq, dk, dv, dpre, own_w):
+    t, d = dz1.shape
+    half = t // 2
+    nz = lax.axis_size("adp")
+    tile = half // 2
+    count = t // tile
+    hw = d // 2
+
+    def kernel(wq_ref, dz_ref, dq_ref, dk_ref, dv_ref, dpre_ref, out, sum_ref,
+               wv, zv, lv, buf, pv, got, tot, zbuf, sems, local, send, recv, psend, precv):
+        dp, y, z, side, over, up = axes_here()
+        along = [{"adp": lax.rem(z + k, nz)} for k in range(1, nz)]
+
+        def rows_of(i):
+            return pl.multiple_of(jnp.where(i < count // 2, 1 - y, y) * half + (i % 2) * tile, tile)
+
+        def loads(i):
+            rows = pl.ds(rows_of(i), tile)
+            yield pltpu.make_async_copy(dz_ref.at[rows], zv.at[i], sems.at[4 * i])
+            for c, ref in enumerate((dq_ref, dk_ref, dv_ref)):
+                yield pltpu.make_async_copy(ref.at[rows], lv.at[i, :, pl.ds(c * d, d)], sems.at[4 * i + 1 + c])
+
+        weight = pltpu.make_async_copy(wq_ref, wv, sems.at[4 * count])
+        pre = pltpu.make_async_copy(dpre_ref, pv, sems.at[4 * count + 1])
+        pre.start()
+        weight.start()
+        for i in range(count):
+            for c in loads(i):
+                c.start()
+        meet([side, over, up] + along)
+
+        def far(src, dst, peer, i):
+            return pltpu.make_async_remote_copy(src_ref=src, dst_ref=dst, send_sem=psend.at[i], recv_sem=precv.at[i],
+                                                device_id=peer, device_id_type=pl.DeviceIdType.MESH)
+
+        first = far(pv.at[:, :, pl.ds(hw, hw)], got.at[0], up, 0)
+        second = far(tot.at[0], got.at[1], side, 1)
+        third = far(tot.at[1], got.at[2], over, 2)
+        ring = [far(zbuf.at[z], zbuf.at[z], peer, 3 + k) for k, peer in enumerate(along)]
+
+        def fold(k):
+            if k == 0:
+                first.wait_recv()
+                tot[0] = pv[:, :, :hw] + got[0]
+                second.start()
+            elif k == 1:
+                second.wait_recv()
+                tot[1] = tot[0] + got[1]
+                third.start()
+            elif k == 2:
+                third.wait_recv()
+                zbuf[z] = tot[1] + got[2]
+                for c in ring:
+                    c.start()
+            else:
+                for c in ring:
+                    c.wait_recv()
+                total = zbuf[0]
+                for j in range(1, nz):
+                    total = total + zbuf[j]
+                sum_ref[...] = total
+
+        pre.wait()
+        first.start()
+        weight.wait()
+        moves = []
+        for i in range(count):
+            for c in loads(i):
+                c.wait()
+            lhs = lv[i]
+            e = jnp.concatenate(
+                [dot_mm(lhs, jnp.concatenate([wv[s, r, c] for c in range(3) for s in range(2)], axis=1), 1, 1)
+                 for r in range(d // TILE)], axis=1)
+            unplace_store(buf.at[i], zv[i] + e, dp)
+            dst = out.at[y, pl.ds((i % 2) * tile, tile)]
+            if i < count // 2:
+                move = pltpu.make_async_remote_copy(
+                    src_ref=buf.at[i], dst_ref=dst, send_sem=send.at[i], recv_sem=recv.at[i],
+                    device_id=up, device_id_type=pl.DeviceIdType.MESH)
+            else:
+                move = pltpu.make_async_copy(buf.at[i], dst, local.at[i])
+            move.start()
+            moves.append(move)
+            if 1 <= i:
+                fold(i - 1)
+        fold(3)
+        for c in [first, second, third] + ring:
+            c.wait_send()
+        for c in moves:
+            c.wait()
+
+    vm = pltpu.VMEM
+    shape = jax.ShapeDtypeStruct
+    dma = pltpu.SemaphoreType.DMA
+    return pl.pallas_call(
+        kernel,
+        in_specs=[HBM] * 6,
+        out_specs=[HBM, pl.BlockSpec(memory_space=pltpu.VMEM)],
+        out_shape=[shape((2, half, d), BF), shape((2, PRE, hw), F32)],
+        scratch_shapes=[vm(wq.shape, BF), vm((count, tile, d), F32), vm((count, tile, 3 * d), BF), vm((count, tile, d), BF),
+                        vm((2, PRE, d), F32), vm((3, 2, PRE, hw), F32), vm((2, 2, PRE, hw), F32), vm((nz, 2, PRE, hw), F32),
+                        dma((4 * count + 2,)), dma((count,)), dma((count,)), dma((count,)), dma((2 + nz,)), dma((2 + nz,))],
+        compiler_params=pltpu.CompilerParams(collective_id=4, has_side_effects=True, vmem_limit_bytes=VMEM_BYTES),
+        cost_estimate=pl.CostEstimate(flops=6 * t * d * d, bytes_accessed=2**24, transcendentals=0),
+    )(wq, dz1, dq, dk, dv, dpre)
+
+
+def by_rows(ref):
+    return lambda s, r, j: ref.at[s, r, pl.ds(j * TILE, TILE)]
+
+
+def by_cols(ref):
+    return lambda s, r, j: ref.at[s, r, slice(None), pl.ds(j * TILE, TILE)]
+
+
+def meet(peers):
+    barrier = pltpu.get_barrier_semaphore()
+    for peer in peers:
+        pl.semaphore_signal(barrier, inc=1, device_id=peer, device_id_type=pl.DeviceIdType.MESH)
+    pl.semaphore_wait(barrier, len(peers))
+
+
+class Moves:
+    def __init__(self, table, send, recv, local):
+        self.table, self.send, self.recv, self.local = table, send, recv, local
+        self.place = {}
+        far = near = 0
+        for name, (src, dst, peer) in table.items():
+            if peer is None:
+                self.place[name] = near
+                near += 1
+            else:
+                self.place[name] = far
+                far += 1
+
+    def copy(self, name):
+        src, dst, peer = self.table[name]
+        i = self.place[name]
+        if peer is None:
+            return pltpu.make_async_copy(src, dst, self.local.at[i])
+        return pltpu.make_async_remote_copy(src_ref=src, dst_ref=dst, send_sem=self.send.at[i], recv_sem=self.recv.at[i],
+                                            device_id=peer, device_id_type=pl.DeviceIdType.MESH)
+
+    def start(self, *names):
+        for name in names:
+            self.copy(name).start()
+
+    def got(self, *names):
+        for name in names:
+            if self.table[name][2] is None:
+                self.copy(name).wait()
+            else:
+                self.copy(name).wait_recv()
+
+    def sent(self, *names):
+        for name in names:
+            self.copy(name).wait_send()
+
+
+def axes_here():
+    dp, y, z = lax.axis_index("dp"), lax.axis_index("mp"), lax.axis_index("adp")
+    return dp, y, z, {"dp": dp ^ 1}, {"dp": dp ^ 2}, {"mp": 1 - y}
+
+
+SPOTS = {"x": (0, 2), "y": (1, 0), "d": (1, 2)}
+
+
+def plane_moves(table, tag, own, far, part, side, over, up):
+    table[tag, "y"] = (part(own), part(far(1, 0)), up)
+    table[tag, "x"] = (part(own), part(far(0, 2)), over)
+    table[tag, "d"] = (part(far(1, 0)), part(far(1, 2)), over)
+    for spot in "xyd":
+        s, r = SPOTS[spot]
+        table[tag, spot, "side"] = (part(far(s, r)), part(far(s, r ^ 1)), side)
+
+
+def ring_moves(table, tag, own, far, quarter, z, nz, side, over, up, onward):
+    first = quarter(z)
+    table[tag, "y"] = (first(own), first(far(1, 0)), up)
+    table[tag, "x"] = (first(own), first(far(0, 2)), over)
+    table[tag, "d"] = (first(far(1, 0)), first(far(1, 2)), over)
+    for spot in "xyd":
+        s, r = SPOTS[spot]
+        for k in range(nz):
+            part = quarter(lax.rem(z + nz - k, nz))
+            table[tag, spot, k, "side"] = (part(far(s, r)), part(far(s, r ^ 1)), side)
+            if k + 1 < nz:
+                table[tag, spot, k, "on"] = (part(far(s, r)), part(far(s, r)), onward)
+
+
+def self_forward(inputs, memory, self_qkv, self_proj, cross_qkv, cross_proj, pre_own, ad_own):
+    _, _, half, d = inputs.shape
+    t = 2 * half
+    nq, wrows, hw = self_qkv.shape
+    nz = lax.axis_size("adp")
+    prow = self_proj.shape[0]
+    pairs = d // 128
+    chunks = d // TILE
+    qscale = HEAD_DIM ** -0.5 * LOG2E
+    ring_tags = ("cq12", "co")
+    plane_tags = ("so", "cq0")
+
+    def moves(refs):
+        (in_ref, mem_ref, own_ref, so_ref, cq_ref, co_ref, pre_ref, ad_ref,
+         q_out, k_out, v_out, w_out, x_out, pre_out, bso, bcq, bco, mem_out, ada_ref, wv, xv, qs, ks, vs, pv) = refs
+        dp, y, z, side, over, up = axes_here()
+        onward = {"adp": lax.rem(z + 1, nz)}
+        along = [{"adp": lax.rem(z + k, nz)} for k in range(1, nz)]
+        rows = pl.ds(pl.multiple_of(y * half, half), half)
+        table = {}
+        table["w own"] = (own_ref, wv.at[0, 0], None)
+        table["pre own"] = (pre_ref, pv.at[:, :, pl.ds(0, hw)], None)
+        for r in range(chunks):
+            cols = pl.ds(pl.multiple_of((dp ^ r) * TILE, TILE), TILE)
+            table["x own", r] = (in_ref.at[y, 0, :, cols], xv.at[rows, pl.ds(r * TILE, TILE)], None)
+            table["x up", r] = (in_ref.at[1 - y, 0, :, cols], xv.at[rows, pl.ds(r * TILE, TILE)], up)
+        table["pre up"] = (pre_ref, pv.at[:, :, pl.ds(hw, hw)], up)
+        plane_moves(table, "w", own_ref, lambda s, r: wv.at[s, r], lambda ref: ref, side, over, up)
+        table["w", "side"] = (own_ref, wv.at[0, 1], side)
+        for k in range(1, nz):
+            table["ad", k] = (ad_ref, ada_ref.at[k], along[k - 1])
+        plane_moves(table, "so", so_ref, lambda s, r: bso.at[s, r], lambda ref: ref, side, over, up)
+        plane_moves(table, "cq0", cq_ref, lambda s, r: bcq.at[s, r], lambda ref: ref.at[0], side, over, up)
+        ring_moves(table, "cq12", cq_ref, lambda s, r: bcq.at[s, r],
+                   lambda qz: lambda ref: ref.at[pl.ds(1, 2), pl.ds(pl.multiple_of(qz * (wrows // nz), wrows // nz), wrows // nz)],
+                   z, nz, side, over, up, onward)
+        ring_moves(table, "co", co_ref, lambda s, r: bco.at[s, r],
+                   lambda qz: lambda ref: ref.at[pl.ds(pl.multiple_of(qz * (prow // nz), prow // nz), prow // nz)],
+                   z, nz, side, over, up, onward)
+        table["so", "side"] = (so_ref, bso.at[0, 1], side)
+        table["cq", "side"] = (cq_ref, bcq.at[0, 1], side)
+        table["co", "side"] = (co_ref, bco.at[0, 1], side)
+        table["mem up"] = (mem_ref.at[1 - y, 0], mem_out, up)
+        for name, s_, o_ in (("q", qs, q_out), ("k", ks, k_out), ("v", vs, v_out), ("w", wv, w_out), ("x", xv, x_out), ("pre", pv, pre_out)):
+            table[name + " out"] = (s_, o_, None)
+        return table, (side, over, up), along
+
+    def count():
+        rings = len(ring_tags) * (3 + 3 * nz + 3 * (nz - 1))
+        planes = (1 + len(plane_tags)) * 6
+        return chunks + planes + rings + nz + 5, chunks + 8
+
+    def kernel(in_ref, mem_ref, own_ref, so_ref, cq_ref, co_ref, pre_ref, ad_ref,
+               a_ref, p_ref, pp_ref, l_ref, q_out, k_out, v_out, w_out, x_out, pre_out, bso, bcq, bco, mem_out, ada_ref,
+               wv, xv, qs, ks, vs, pv, send, recv, local):
+        g = pl.program_id(0)
+        table, near_peers, along = moves((in_ref, mem_ref, own_ref, so_ref, cq_ref, co_ref, pre_ref, ad_ref,
+                                          q_out, k_out, v_out, w_out, x_out, pre_out, bso, bcq, bco, mem_out, ada_ref,
+                                          wv, xv, qs, ks, vs, pv))
+        mv = Moves(table, send, recv, local)
+        done = set()
+
+        def got(*names):
+            done.update(names)
+            mv.got(*names)
+
+        xs_up = [("x up", r) for r in range(chunks)]
+        xs_own = [("x own", r) for r in range(chunks)]
+        ads = [("ad", k) for k in range(1, nz)]
+        outs = [n + " out" for n in ("q", "k", "v", "w", "x", "pre")]
+
+        def pass_on(spot, k):
+            for tag in ring_tags:
+                got((tag, spot) if k == 0 else (tag, spot, k - 1, "on"))
+                if k + 1 < nz:
+                    mv.start((tag, spot, k, "on"))
+                mv.start((tag, spot, k, "side"))
+
+        @pl.when(g == 0)
+        def _():
+            meet(list(near_peers) + along)
+            mv.start(("w", "y"), ("w", "x"), "pre up")
+            mv.start(*[(tag, spot) for tag in ring_tags for spot in "yx"])
+            mv.start(*xs_up)
+            mv.start(("w", "side"), *ads)
+            mv.start("w own", "pre own", *xs_own)
+            got(("w", "y"))
+            mv.start(("w", "d"), ("w", "y", "side"))
+            got(("w", "x"))
+            mv.start(("w", "x", "side"))
+            pass_on("y", 0)
+            mv.start(*[(tag, "d") for tag in ring_tags])
+            pass_on("x", 0)
+            mv.start(*[(tag, spot) for tag in plane_tags for spot in "xy"])
+            mv.start("mem up", ("so", "side"), ("cq", "side"), ("co", "side"))
+            for k in range(1, nz):
+                pass_on("y", k)
+                pass_on("x", k)
+            got(("w", "d"))
+            mv.start(("w", "d", "side"))
+            pass_on("d", 0)
+            got("w own", "pre own", "pre up", ("w", "side"), ("w", "y", "side"), ("w", "x", "side"), ("w", "d", "side"))
+            got(*xs_own)
+            got(*xs_up)
+            for i in range(2):
+                x = xv[i * half:(i + 1) * half]
+                for c, out in ((0, qs), (1, ks), (2, vs)):
+                    for s in range(2):
+                        w = jnp.concatenate([wv[s, r, c] for r in range(4)], axis=0)
+                        o = dot_mm(x, w, 1, 0)
+                        out[i * half:(i + 1) * half, s * hw:(s + 1) * hw] = (o * qscale if c == 0 else o).astype(BF)
+                if i + 1 < nz:
+                    pass_on("d", i + 1)
+            mv.start(*outs)
+
+        for k in range(3, nz):
+            @pl.when(g == k - 2)
+            def _():
+                pass_on("d", k)
+
+        @pl.when(g == 3)
+        def _():
+            for tag in plane_tags:
+                got((tag, "y"), (tag, "x"))
+                mv.start((tag, "d"), (tag, "y", "side"), (tag, "x", "side"))
+
+        @pl.when(g > 0)
+        def _():
+            cs = pl.ds(pl.multiple_of((g - 1) * 128, 128), 128)
+            a, il = attend_pair(True, PREFIX_LEN, qs[:, cs], ks[:, cs], vs[:, cs], pv[0, :, cs], pv[1, :, cs], p_ref, pp_ref)
+            a_ref[...] = a
+            l_ref[0] = il
+
+        @pl.when(g == pairs)
+        def _():
+            for tag in plane_tags:
+                got((tag, "d"))
+                mv.start((tag, "d", "side"))
+            far = [n for n, (_, _, peer) in table.items() if peer is not None]
+            got(*[n for n in far if n not in done])
+            got(*outs)
+            mv.sent(*far)
+
+    lead = lambda g: (jnp.maximum(g - 1, 0), 0, 0)
+    col = lambda g: (0, jnp.maximum(g - 1, 0))
+    shape = jax.ShapeDtypeStruct
+    remotes, near = count()
+    vm = pltpu.VMEM
+    return pl.pallas_call(
+        kernel,
+        grid=(pairs + 1,),
+        in_specs=[HBM] * 8,
+        out_specs=[pl.BlockSpec((t, 128), col), pl.BlockSpec((2, t, t), lead), pl.BlockSpec((2, PRE, t), lead),
+                   pl.BlockSpec((1, 2, t), lead)] + [HBM] * 11,
+        out_shape=[
+            shape((t, d), BF), shape((2 * pairs, t, t), BF), shape((2 * pairs, PRE, t), BF), shape((pairs, 2, t), F32),
+            shape((t, d), BF), shape((t, d), BF), shape((t, d), BF), shape((2, 4) + self_qkv.shape, BF),
+            shape((t, d), BF), shape((2, PRE, d), BF), shape((2, 4) + self_proj.shape, BF), shape((2, 4) + cross_qkv.shape, BF),
+            shape((2, 4) + cross_proj.shape, BF), shape((half, d), BF), shape((nz,) + ad_own.shape, BF),
+        ],
+        scratch_shapes=[vm((2, 4) + self_qkv.shape, BF), vm((t, d), BF), vm((t, d), BF), vm((t, d), BF), vm((t, d), BF),
+                        vm((2, PRE, d), BF), pltpu.SemaphoreType.DMA((remotes,)),
+                        pltpu.SemaphoreType.DMA((remotes,)), pltpu.SemaphoreType.DMA((near,))],
+        compiler_params=pltpu.CompilerParams(collective_id=0, has_side_effects=True, vmem_limit_bytes=VMEM_BYTES),
+        cost_estimate=pl.CostEstimate(flops=10**11, bytes_accessed=10**8, transcendentals=0),
+    )(inputs, memory, self_qkv, self_proj, cross_qkv, cross_proj, pre_own, ad_own)
+
+
+def cross_forward(src_n, x_full, a, mem_mine, mem_got, self_proj, b_so, cross_qkv, b_cq, ad_col, cotangent, ffn_in, ffn_out, gain):
+    t, d = x_full.shape
+    half = t // 2
+    nz = lax.axis_size("adp")
+    pairs = d // 128
+    chunks = d // TILE
+    khead = self_proj.shape[0] // TILE
+    kcol = cross_qkv.shape[2] // TILE
+    nq = cross_qkv.shape[0]
+    orow = ffn_out.shape[0]
+    icol = ffn_in.shape[1]
+    ihalf = icol // 2
+    qscale = HEAD_DIM ** -0.5 * LOG2E
+
+    def moves(refs):
+        ad_ref, cot_ref, fi_ref, fo_ref, q_out, k_out, v_out, cin, cout, ada_ref, cot_out, qs, ks, vs = refs
+        dp, y, z, side, over, up = axes_here()
+        onward = {"adp": lax.rem(z + 1, nz)}
+        before = {"adp": lax.rem(z + nz - 1, nz)}
+        table = {}
+        for name, s_, o_ in (("q", qs, q_out), ("k", ks, k_out), ("v", vs, v_out)):
+            table[name + " out"] = (s_, o_, None)
+        ring_moves(table, "o", fo_ref, lambda s, r: cout.at[s, r],
+                   lambda qz: lambda ref: ref.at[pl.ds(pl.multiple_of(qz * (orow // nz), orow // nz), orow // nz)],
+                   z, nz, side, over, up, onward)
+        table["o", "side"] = (fo_ref, cout.at[0, 1], side)
+        table["i", "side"] = (fi_ref, cin.at[0, 1], side)
+        table["i", "y"] = (fi_ref, cin.at[1, 0], up)
+        table["i", "x"] = (fi_ref, cin.at[0, 2], over)
+        one, two = pl.ds(0, ihalf), pl.ds(ihalf, ihalf)
+        table["i", "d1"] = (cin.at[1, 0, :, one], cin.at[1, 2, :, one], over)
+        table["i", "d2"] = (cin.at[0, 2, :, two], cin.at[1, 2, :, two], up)
+        table["i", "y", "side"] = (cin.at[1, 0], cin.at[1, 1], side)
+        table["i", "x", "side"] = (cin.at[0, 2], cin.at[0, 3], side)
+        table["i", "d1", "side"] = (cin.at[1, 2, :, one], cin.at[1, 3, :, one], side)
+        table["i", "d2", "side"] = (cin.at[1, 2, :, two], cin.at[1, 3, :, two], side)
+        table["ad side"] = (ad_ref, ada_ref.at[1], side)
+        table["ad over"] = (ad_ref, ada_ref.at[2], over)
+        table["ad over side"] = (ada_ref.at[2], ada_ref.at[3], side)
+        table["cot"] = (cot_ref.at[1 - y, 0], cot_out, up)
+        return table, [side, over, up, onward, before]
+
+    def kernel(n_ref, x_ref, a_in, gain_ref, memo_ref, memg_ref, so_ref, bso, cq_ref, bcq, ad_ref, cot_ref, fi_ref, fo_ref,
+               ac_ref, p_ref, l_ref, u_ref, inv_ref, q_out, k_out, v_out, cin, cout, ada_ref, cot_out,
+               sov, cqv, qs, ks, vs, send, recv, local, wsem):
+        g = pl.program_id(0)
+        dp, y = lax.axis_index("dp"), lax.axis_index("mp")
+        table, peers = moves((ad_ref, cot_ref, fi_ref, fo_ref, q_out, k_out, v_out, cin, cout, ada_ref, cot_out, qs, ks, vs))
+        mv = Moves(table, send, recv, local)
+        done = set()
+
+        def got(*names):
+            done.update(names)
+            mv.got(*names)
+
+        def pass_on(spot, k):
+            got(("o", spot) if k == 0 else ("o", spot, k - 1, "on"))
+            if k + 1 < nz:
+                mv.start(("o", spot, k, "on"))
+            mv.start(("o", spot, k, "side"))
+
+        outs = [n + " out" for n in ("q", "k", "v")]
+
+        def loads():
+            for i, (own, far, dst) in enumerate(((so_ref, bso, sov), (cq_ref, bcq, cqv))):
+                yield pltpu.make_async_copy(own, dst.at[0, 0], wsem.at[i, 0])
+                yield pltpu.make_async_copy(far.at[0, pl.ds(1, 3)], dst.at[0, pl.ds(1, 3)], wsem.at[i, 1])
+                yield pltpu.make_async_copy(far.at[1], dst.at[1], wsem.at[i, 2])
+
+        so = by_rows(sov)
+
+        def project(i):
+            rs = slice(i * half, (i + 1) * half)
+            att = a_in[rs]
+            z1 = x_ref[rs].astype(F32) + jnp.concatenate(
+                [nn(att, [so(s, r, j) for s in range(2) for j in range(khead)]) for r in range(chunks)], axis=1)
+            u, inv = normalize(z1)
+            u_ref[rs] = u
+            inv_ref[rs] = inv
+            h = (u * gain_ref[...]).astype(BF)
+            xm = jnp.where(y == i, place_cols(memo_ref, dp), place_cols(memg_ref, dp))
+            for lhs, c, out in ((h, 0, qs), (xm, 1, ks), (xm, 2, vs)):
+                for s in range(2):
+                    for j in range(kcol):
+                        o = nn(lhs, [cqv.at[s, r, c, :, pl.ds(j * TILE, TILE)] for r in range(4)])
+                        cs = slice((s * kcol + j) * TILE, (s * kcol + j + 1) * TILE)
+                        out[rs, cs] = (o * qscale if c == 0 else o).astype(BF)
+
+        @pl.when(g == 0)
+        def _():
+            for c in loads():
+                c.start()
+            meet(peers)
+            mv.start(("o", "y"), ("o", "x"), ("i", "y"), ("i", "side"), ("o", "side"), "ad side")
+            for c in loads():
+                c.wait()
+            project(0)
+            pass_on("y", 0)
+            mv.start(("o", "d"), ("i", "x"), "ad over", "cot")
+            pass_on("x", 0)
+            project(1)
+            pass_on("d", 0)
+            mv.start(*outs)
+
+        for k in range(1, nz):
+            @pl.when(g == 3 * k - 2)
+            def _():
+                pass_on("y", k)
+                pass_on("x", k)
+
+            @pl.when(g == 3 * k - 1)
+            def _():
+                pass_on("d", k)
+
+        @pl.when(g == 3)
+        def _():
+            got(("i", "y"))
+            mv.start(("i", "d1"), ("i", "y", "side"))
+
+        @pl.when(g == 6)
+        def _():
+            got(("i", "x"))
+            mv.start(("i", "d2"), ("i", "x", "side"))
+
+        @pl.when(g > 0)
+        def _():
+            cs = pl.ds(pl.multiple_of((g - 1) * 128, 128), 128)
+            av, il = attend_pair(False, n_ref[0], qs[:, cs], ks[:, cs], vs[:, cs], None, None, p_ref, None)
+            ac_ref[...] = av
+            l_ref[0] = il
+
+        @pl.when(g == pairs)
+        def _():
+            got("ad over")
+            mv.start("ad over side")
+            got(("i", "d1"))
+            mv.start(("i", "d1", "side"))
+            got(("i", "d2"))
+            mv.start(("i", "d2", "side"))
+            far = [n for n, (_, _, peer) in table.items() if peer is not None]
+            got(*[n for n in far if n not in done])
+            got(*outs)
+            mv.sent(*far)
+
+    lead = lambda g: (jnp.maximum(g - 1, 0), 0, 0)
+    col = lambda g: (0, jnp.maximum(g - 1, 0))
+    fixed = lambda g: (0, 0)
+    shape = jax.ShapeDtypeStruct
+    once = pl.Buffered(1)
+    remotes = 3 + 3 * nz + 3 * (nz - 1) + 10 + 4
+    near = 3
+    vm = pltpu.VMEM
+    whole = lambda *s: pl.BlockSpec(s, fixed, pipeline_mode=once)
+    return pl.pallas_call(
+        kernel,
+        grid=(pairs + 1,),
+        in_specs=[pl.BlockSpec(memory_space=pltpu.SMEM), whole(t, d), whole(t, d), whole(1, d), whole(half, d), whole(half, d)]
+        + [HBM] * 8,
+        out_specs=[pl.BlockSpec((t, 128), col), pl.BlockSpec((2, t, t), lead), pl.BlockSpec((1, 2, t), lead),
+                   pl.BlockSpec((t, d), fixed), pl.BlockSpec((t, 1), fixed)] + [HBM] * 7,
+        out_shape=[
+            shape((t, d), BF), shape((2 * pairs, t, t), BF), shape((pairs, 2, t), F32), shape((t, d), F32), shape((t, 1), F32),
+            shape((t, d), BF), shape((t, d), BF), shape((t, d), BF), shape((2, 4) + ffn_in.shape, BF), shape((2, 4) + ffn_out.shape, BF),
+            shape((4,) + ad_col.shape, BF), shape((half, d), BF),
+        ],
+        scratch_shapes=[vm((2, 4) + self_proj.shape, BF), vm((2, 4) + cross_qkv.shape, BF), vm((t, d), BF), vm((t, d), BF), vm((t, d), BF),
+                        pltpu.SemaphoreType.DMA((remotes,)), pltpu.SemaphoreType.DMA((remotes,)),
+                        pltpu.SemaphoreType.DMA((near,)), pltpu.SemaphoreType.DMA((2, 3))],
+        compiler_params=pltpu.CompilerParams(collective_id=1, has_side_effects=True, vmem_limit_bytes=VMEM_BYTES),
+        cost_estimate=pl.CostEstimate(flops=10**11, bytes_accessed=10**8, transcendentals=0),
+    )(src_n, x_full, a, gain, mem_mine, mem_got, self_proj, b_so, cross_qkv, b_cq, ad_col, cotangent, ffn_in, ffn_out)
+
+
+def whole_sequences(inputs, memory, src_lengths, self_qkv, self_proj, cross_qkv, cross_proj, ffn_in, ffn_out,
+                    norm_gains, prefix, adapter_down, adapter_up, cotangent):
+    dp, y, z = lax.axis_index("dp"), lax.axis_index("mp"), lax.axis_index("adp")
+    nz = lax.axis_size("adp")
+    half, d = inputs.shape[2], inputs.shape[3]
+    t = 2 * half
+    chunks = d // TILE
+    mine = lambda a: lax.dynamic_index_in_dim(a, y, 0, keepdims=False)[0]
+    rel = lambda a: jnp.concatenate(
+        [lax.dynamic_slice_in_dim(a, (dp ^ r) * TILE, TILE, axis=a.ndim - 1) for r in range(chunks)], axis=-1)
+
+    ad_own = jnp.concatenate([adapter_down.T, adapter_up], axis=0)
+    pre_own = jnp.pad(prefix, ((0, 0), (0, PRE - PREFIX_LEN), (0, 0)))
+    src_n = lax.dynamic_index_in_dim(src_lengths, y, 0, keepdims=False).reshape(1)
+    khead, kcol = self_proj.shape[0] // TILE, cross_qkv.shape[2] // TILE
+    kin = ffn_in.shape[1] // TILE
+
+    gains = rel(norm_gains.astype(F32))
+    gain = [gains[i:i + 1] for i in range(3)]
+    row = lambda i: (i, 0)
+    hw = self_qkv.shape[2]
+
+    a, p, pp, il, q, k, v, wq, x_full, pre_w, b_so, b_cq, b_co, mem_got, ad_col = self_forward(
+        inputs, memory, self_qkv, self_proj, cross_qkv, cross_proj, pre_own, ad_own)
+    ad_col = lax.dynamic_update_slice_in_dim(ad_col, ad_own[None], 0, axis=0)
+    w_so, w_co = (self_proj, b_so, None), (cross_proj, b_co, None)
+    w_cq = lambda c: (cross_qkv, b_cq, c)
+    out_rows = lambda T, r, n: [T(s, r, j) for s in range(2) for j in range(n)]
+    ac, p_c, il_c, u1, inv1, qc, kc, vc, c_in, c_out, ad_all, cot_got = cross_forward(
+        src_n, x_full, a, mine(memory), mem_got, self_proj, b_so, cross_qkv, b_cq, ad_col, cotangent, ffn_in, ffn_out, gain[0])
+    fixed = lambda i: (0, 0)
+    spec = lambda shape, index: pl.BlockSpec(shape, index)
+    held = lambda *shape: pl.BlockSpec(shape, lambda i: (0,) * len(shape), pipeline_mode=pl.Buffered(1))
+
+    n_ad = ad_own.shape[0] // 2
+    tile = half // FEED_SPLIT
+    hid = 2 * kin
+
+    def feed(W, need, rows, consts, outs, scr, put):
+        dp, y = lax.axis_index("dp"), lax.axis_index("mp")
+        ac_ref, u1_ref, cot_a, cot_b = rows
+        act_ref, slope_ref, terms = scr
+        g1, g2, g3 = consts[:3]
+        co, fi, fo = by_rows(W[0]), by_cols(W[1]), by_rows(W[2])
+        down = lambda r, kk: (consts[3].at[kk] if r == 0 else consts[4].at[r, kk]).at[pl.ds(0, n_ad)]
+        upw = lambda r, kk: (consts[3].at[kk] if r == 0 else consts[4].at[r, kk]).at[pl.ds(n_ad, n_ad)]
+        need(0)
+        att = ac_ref[...]
+        z2 = u1_ref[...] * g1[...] + jnp.concatenate(
+            [nn(att, out_rows(co, r, khead)) for r in range(chunks)], axis=1)
+        u2, inv2 = normalize(z2)
+        h2 = u2 * g2[...]
+        h2b = h2.astype(BF)
+        need(1)
+        order = [(s, j) for s in range(2) for j in range(kin)]
+        ahead = nn(h2b, [fi(0, r, 0) for r in range(4)])
+        for i in range(hid):
+            g = ahead
+            if i + 1 < hid:
+                s, j = order[i + 1]
+                ahead = nn(h2b, [fi(s, r, j) for r in range(4)])
+            act, slope = gelu_pair(g)
+            act_ref[:, i * TILE:(i + 1) * TILE] = act.astype(BF)
+            slope_ref[:, i * TILE:(i + 1) * TILE] = slope.astype(BF)
+        down_t = jnp.concatenate([stack_cols([down(r, kk) for r in range(4)]) for kk in range(nz)], axis=0)
+        up_m = jnp.concatenate([stack_cols([upw(r, kk) for r in range(4)]) for kk in range(nz)], axis=0)
+        act_a, slope_a = gelu_pair(dot_mm(h2b, down_t, 1, 1))
+        act_a = act_a.astype(BF)
+        need(2)
+        acts = act_ref[...]
+        z3 = h2 + 4.0 * dot_mm(act_a, up_m, 1, 0) + jnp.concatenate(
+            [nn(acts, out_rows(fo, r, kin)) for r in range(chunks)], axis=1)
+        u3, inv3 = normalize(z3)
+        put(u3 * g3[...])
+        in_own = pl.program_id(0) // (half // tile) == y
+        cot = jnp.where(in_own, place_cols(cot_a, dp), place_cols(cot_b, dp)).astype(F32)
+        dz3 = norm_back(cot, u3, inv3, g3[...])
+        b3 = dz3.astype(BF)
+        dga = (4.0 * dot_mm(b3, up_m, 1, 1) * slope_a).astype(BF)
+        up_term = 4.0 * dot_mm(act_a, b3, 0, 0)
+        down_term = dot_mm(dga, h2b, 0, 0)
+
+        @pl.when(pl.program_id(0) == 0)
+        def _():
+            terms[0] = down_term
+            terms[1] = up_term
+
+        @pl.when(pl.program_id(0) > 0)
+        def _():
+            terms[0] += down_term
+            terms[1] += up_term
+
+        @pl.when(pl.program_id(0) == pl.num_programs(0) - 1)
+        def _():
+            for i in range(2):
+                outs[2][:, i] = terms[:, :, 2 * i * TILE:(2 * i + 1) * TILE]
+                outs[3][:, i] = terms[:, :, (2 * i + 1) * TILE:(2 * i + 2) * TILE].astype(BF)
+
+        for i, (s, j) in enumerate(order):
+            cs = slice(i * TILE, (i + 1) * TILE)
+            df = nt(b3, [fo(s, r, j) for r in range(4)])
+            slope_ref[:, cs] = (df * slope_ref[:, cs].astype(F32)).astype(BF)
+        dg = slope_ref[...]
+        dh2 = dz3 + dot_mm(dga, down_t, 1, 0) + jnp.concatenate(
+            [nt(dg, out_rows(fi, r, kin)) for r in range(chunks)], axis=1)
+        dz2 = norm_back(dh2, u2, inv2, g2[...])
+        outs[0][...] = dz2
+        dz2b = dz2.astype(BF)
+        for s in range(2):
+            for j in range(khead):
+                i = s * khead + j
+                outs[1][:, i * TILE:(i + 1) * TILE] = nt(dz2b, [co(s, r, j) for r in range(4)]).astype(BF)
+
+    part = lambda i: (i % (half // tile), 0)
+    dz2, dac, keep, give, result = tiled(
+        [w_co, (ffn_in, c_in, None), (ffn_out, c_out, None)],
+        [(ac, spec((tile, d), row)), (u1, spec((tile, d), row)), (mine(cotangent), spec((tile, d), part)),
+         (cot_got, spec((tile, d), part))],
+        gain + [ad_col, ad_all],
+        [((t, d), F32, (tile, d), row), ((t, d), BF, (tile, d), row),
+         ((2, 2, nz * n_ad, TILE), F32, (2, 2, nz * n_ad, TILE), lambda i: (0, 0, 0, 0)),
+         ((2, 2, nz * n_ad, TILE), BF, (2, 2, nz * n_ad, TILE), lambda i: (0, 0, 0, 0))],
+        feed, tile, t // tile, exchange=(2, half, d),
+        scratch=[pltpu.VMEM((tile, hid * TILE), BF)] * 2 + [pltpu.VMEM((2, nz * n_ad, d), F32)], flops=4 * 2 * t * d * hid * TILE)
+
+    dqc, dkc, dvc, down_grad, up_grad = attn_bwd(qc, kc, vc, ac, dac, il_c, p_c, keep=keep, give=give)
+
+    def memory_back(sc, own, far, dk_ref, dv_ref, mine_ref, send_ref, wv, sems):
+        def loads():
+            yield pltpu.make_async_copy(own.at[pl.ds(1, 2)], wv.at[0, 0], sems.at[0])
+            yield pltpu.make_async_copy(far.at[0, pl.ds(1, 3), pl.ds(1, 2)], wv.at[0, pl.ds(1, 3)], sems.at[1])
+            yield pltpu.make_async_copy(far.at[1, pl.ds(0, 4), pl.ds(1, 2)], wv.at[1], sems.at[2])
+
+        step = pl.program_id(0)
+
+        @pl.when(step == 0)
+        def _():
+            for c in loads():
+                c.start()
+            for c in loads():
+                c.wait()
+
+        lhs = jnp.concatenate([dk_ref[...], dv_ref[...]], axis=1)
+        e = jnp.concatenate(
+            [dot_mm(lhs, jnp.concatenate([wv[s, r, c] for c in range(2) for s in range(2)], axis=1), 1, 1)
+             for r in range(chunks)], axis=1)
+
+        @pl.when(step == 0)
+        def _():
+            unplace_store(send_ref, e, sc[0])
+
+        @pl.when(step == 1)
+        def _():
+            unplace_store(mine_ref.at[0], e, sc[0])
+
+    turned = lambda i, sc: (jnp.where(i == 0, 1 - sc[1], sc[1]), 0)
+    mem_mine, mem_send = pl.pallas_call(
+        memory_back,
+        grid_spec=pltpu.PrefetchScalarGridSpec(
+            num_scalar_prefetch=1, grid=(2,),
+            in_specs=[HBM, HBM, pl.BlockSpec((half, d), turned), pl.BlockSpec((half, d), turned)],
+            out_specs=[pl.BlockSpec((1, half, d), lambda i, sc: (sc[1], 0, 0)), pl.BlockSpec((half, d), lambda i, sc: (0, 0))],
+            scratch_shapes=[pltpu.VMEM((2, 4, 2) + cross_qkv.shape[1:], BF), pltpu.SemaphoreType.DMA((3,))]),
+        out_shape=[jax.ShapeDtypeStruct((2, half, d), BF), jax.ShapeDtypeStruct((half, d), BF)],
+        compiler_params=pltpu.CompilerParams(vmem_limit_bytes=VMEM_BYTES),
+        cost_estimate=pl.CostEstimate(flops=4 * t * d * d, bytes_accessed=2**24, transcendentals=0),
+    )(jnp.stack([dp, y]).astype(jnp.int32), cross_qkv, b_cq, dkc, dvc)
+
+    def norm_back_self(W, need, rows, consts, outs, scr, put):
+        dz2_ref, dqc_ref, u1_ref, inv_ref = rows
+        cq, so = by_cols(W[0]), by_rows(W[1])
+        need(0)
+        dq_c = dqc_ref[...]
+        e = dz2_ref[...] + jnp.concatenate([nt(dq_c, out_rows(cq, r, kcol)) for r in range(chunks)], axis=1)
+        dz1 = norm_back(e, u1_ref[...], inv_ref[...], consts[0][...])
+        outs[0][...] = dz1
+        dz1b = dz1.astype(BF)
+        need(1)
+        for s in range(2):
+            for j in range(khead):
+                i = s * khead + j
+                outs[1][:, i * TILE:(i + 1) * TILE] = nt(dz1b, [so(s, r, j) for r in range(4)]).astype(BF)
+
+    dz1, da = tiled(
+        [w_cq(0), w_so],
+        [(dz2, spec((half, d), row)), (dqc, spec((half, d), row)), (u1, spec((half, d), row)), (inv1, spec((half, 1), row))],
+        [gain[0]],
+        [((t, d), F32, (half, d), row), ((t, d), BF, (half, d), row)], norm_back_self, half, 2,
+        flops=4 * t * d * d)
+
+    dq, dk, dv, dpre, memory_grad = attn_bwd(q, k, v, a, da, il, p, pp, pre_w, mem_send, mem_mine)
+    input_grad, pre_sum = last_gradient(wq, dz1, dq, dk, dv, dpre, self_qkv)
+    return result[:, None], input_grad[:, None], memory_grad[:, None], pre_sum[:, :PREFIX_LEN], down_grad, up_grad
+
+
 def solution(mesh):
+    by_sequence = mesh.shape["mp"] == MICRO and mesh.shape["dp"] == 4
     return jax.shard_map(
-        shards,
+        whole_sequences if by_sequence else shards,
         mesh=mesh,
         in_specs=(
             P(None, ("dp", "adp"), "mp", None),

time: 2210 us -> 418 us (0.19)
  waiting for transfers between devices: 1290 us -> 0 us
  matrix products: 581 us -> 0 us
  Pallas kernels: 0 us -> 391 us
  other arithmetic: 234 us -> 4.14 us
  local copies, waits for them, and re-layouts: 53.9 us -> 15 us
    reduce_scatter x20 -> x0, waiting for transfers between devices: 604 us -> none  [the longest x4 316 us: reduce_adapter(): lax.psum_scatter(term_fn(jnp.int32(0), own_count * lax.axis_size('adp'))....]
    all_gather x24 -> x0, waiting for transfers between devices: 591 us -> none  [the longest x4 234 us: gather_adapter(): return lax.all_gather(rows_low, 'adp', axis=0, tiled=True)]
    dot_general x62 -> x0, matrix products: 581 us -> none  [the longest x14 106 us: matmul(): return jnp.dot(left_mat, right_mat, preferred_element_type=jnp.float32)]
    pallas_call x0 -> x8, Pallas kernels: none -> 391 us  [the longest x1 97.3 us: self_forward(): pl.pallas_call(kernel, grid=(pairs + 1,), in_specs=[HBM] * 8, out_specs=[...]
    convert_element_type x12 -> x1, other arithmetic: 128 us -> 0.7 us  [whole_sequences(): gains = rel(norm_gains.astype(F32))]
    reduce_sum x18 -> x0, other arithmetic: 90.6 us -> none  [the longest x4 55 us: attend_forward(): row_total = jnp.sum(expo_scores, axis=-1, keepdims=True)]
    psum x1 -> x0, waiting for transfers between devices: 90.3 us -> none  [reduce_prefix(): return lax.psum(grad_prefix, ('dp', 'adp'))]
  transfers between devices with their start and end apart: 45 -> 0, of which waited for: 33 -> 0; matrix products, arithmetic and copies ran while one was open for 37% -> 0% of each run, Pallas kernels for 0% -> 0%
where the time goes in v2:
time: 418 us; the launch traced here: 412 us
  Pallas kernels  391 us (94%)
  local copies, waits for them, and re-layouts  15 us (4%)
    pallas_call x1, Pallas kernels, self_forward(): pl.pallas_call(kernel, grid=(pairs + 1,), in_specs=[HBM] * 8, out_specs=[...  97.3 us
    pallas_call x2, Pallas kernels, tiled(): pl.pallas_call(kernel, grid=(steps,), in_specs=[HBM] * (2 * nw) + [spec f...  96.4 us
    pallas_call x2, Pallas kernels, attn_bwd(): pl.pallas_call(functools.partial(attn_bwd_body, causal), grid=(pairs,), i...  80.7 us
    pallas_call x1, Pallas kernels, cross_forward(): pl.pallas_call(kernel, grid=(pairs + 1,), in_specs=[pl.BlockSpec(memory_s...  77.5 us
    pallas_call x1, Pallas kernels, last_gradient(): pl.pallas_call(kernel, in_specs=[HBM] * 6, out_specs=[HBM, pl.BlockSpec(m...  28.7 us
    pallas_call x1, Pallas kernels, whole_sequences(): pl.pallas_call(memory_back, grid_spec=pltpu.PrefetchScalarGridSpec(num_sc...  11 us
    unnamed x24, local copies, waits for them, and re-layouts  10.7 us

profile of v2, /device:TPU:0, one launch (start us, length us, event | category | flops | bytes accessed | tf_op | source)
XLA Modules:
  0.0 411.6 jit_solution(7750429847460997384)
XLA Ops:
  0.6 0.0 copy-start
  0.7 0.7 pad_add_fusion.sc
  1.3 0.0 copy-done
  1.3 0.6 constant_dynamic-slice_fusion.4
  1.9 0.7 convert_element_type.5
  2.6 0.6 pad_maximum_fusion.1
  3.2 0.8 copy.21
  4.1 0.6 pad.4.pre_ref
  4.7 0.9 copy.22
  5.7 1.5 pad_maximum_fusion.ad_ref
  7.2 3.0 dynamic-slice_bitcast_fusion
  10.2 0.0 copy-start.5
  10.2 97.3 %shard_map.181 = (bf16[1024,1024]{1,0:T(8,128)(2,1)}, bf16[16,1024,1024]{2,1,0:T(8,128)(2,1)}, bf16[16,32,1024]{2,1,0:T(8,128)(2,1)}, f32[8,2,1024]{2,1,0:T(2,12...) custom-call(bf16[2,1,512,1024]{3,2,1,0:T(8,128)(2,1)} %in_ref.1, ...), custom_call_target="tpu_custom_call" | custom-call | flops 99999997952 | bytes 100000000 | tf_op jit(solution)/shard_map/pallas_call | solution.py:1132
  107.5 0.0 copy-done.5
  107.5 0.7 bitcast_dynamic-update-slice_fusion.ad_ref.refs_13_
  108.2 77.5 %shard_map.182 = (bf16[1024,1024]{1,0:T(8,128)(2,1)}, bf16[16,1024,1024]{2,1,0:T(8,128)(2,1)}, f32[8,2,1024]{2,1,0:T(2,128)}, f32[1024,1024]{1,0:T(8,128)}, f32[...) custom-call(s32[1]{0:T(128)} %bitcast.1.n_ref, ...), custom_call_target="tpu_custom_call" | custom-call | flops 99999997952 | bytes 100000000 | tf_op jit(solution)/shard_map/pallas_call | solution.py:1305
  185.7 84.2 %shard_map.183 = (f32[1024,1024]{1,0:T(8,128)}, bf16[1024,1024]{1,0:T(8,128)(2,1)}, f32[2,2,512,256]{3,2,1,0:T(8,128)}, bf16[2,2,512,256]{3,2,1,0:T(8,128)(2,1)}, bf16[2,512,1024]{2,1,0:T(8,128)(2,1)}) custom-call(bf16[512,256]{1,0:T(8,128)(2,1)} %refs_0_.2, bf16[2,4,512,256]{3,2,1,0:T(8,128)(2,1)} %get-tuple-element.54.refs_1_, bf16[256,2048]{1,0:T(8,128)(2,1)} %refs_2_.2, ...), custom_call_target="tpu_custom_call" | custom-call | flops 34359738368 | bytes 16777216 | tf_op jit(solution)/shard_map/pallas_call | solution.py:780
  269.8 44.4 %shard_map.184 = (bf16[1024,1024]{1,0:T(8,128)(2,1)}, bf16[1024,1024]{1,0:T(8,128)(2,1)}, bf16[1024,1024]{1,0:T(8,128)(2,1)}, f32[128,128]{1,0:T(8,128)}, f32[128,128]{1,0:T(8,128)}) custom-call(bf16[1024,1024]{1,0:T(8,128)(2,1)} %get-tuple-element.70.q_ref, bf16[1024,1024]{1,0:T(8,128)(2,1)} %get-tuple-element.71.k_ref, ...), custom_call_target="tpu_custom_call" | custom-call | flops 42949672960 | bytes 33554432 | tf_op jit(solution)/shard_map/pallas_call | solution.py:597
  314.3 12.2 %shard_map.185 = (f32[1024,1024]{1,0:T(8,128)}, bf16[1024,1024]{1,0:T(8,128)(2,1)}) custom-call(bf16[3,256,512]{2,1,0:T(8,128)(2,1)} %own.1, bf16[2,4,3,256,512]{4,3,2,1,0:T(8,128)(2,1)} %get-tuple-element.59.bcq.refs_1_.far, bf16[512,256]{1,0:T(8,128)(2,1)} %refs_2_.3, bf16[2,4,512,256]{3,2,1,0:T(8,128)(2,1)} %get-tuple-element.58.bso.refs_3_, ...), custom_call_target="tpu_custom_call" | custom-call | flops 4294967296 | bytes 16777216 | tf_op jit(solution)/shard_map/pallas_call | solution.py:780
  326.5 11.0 %shard_map.186 = (bf16[2,512,1024]{2,1,0:T(8,128)(2,1)}, bf16[512,1024]{1,0:T(8,128)(2,1)}) custom-call(s32[2]{0:T(128)} %pad_add_fusion.sc, bf16[3,256,512]{2,1,0:T(8,128)(2,1)} %own.1, bf16[2,4,3,256,512]{4,3,2,1,0:T(8,128)(2,1)} %get-tuple-element.59.bcq.refs_1_.far, bf16[1024,1024]{1,0:T(8,128)(2,1)} %get-tuple-element.89.dk_ref, ...), custom_call_target="tpu_custom_call" | custom-call | flops 4294967296 | bytes 16777216 | tf_op jit(solution)/shard_map/pallas_call | solution.py:1481
  337.5 36.2 %shard_map.187 = (bf16[1024,1024]{1,0:T(8,128)(2,1)}, bf16[1024,1024]{1,0:T(8,128)(2,1)}, bf16[1024,1024]{1,0:T(8,128)(2,1)}, f32[2,32,1024]{2,1,0:T(8,128)}, bf16[2,512,1024]{2,1,0:T(8,128)(2,1)}) custom-call(bf16[1024,1024]{1,0:T(8,128)(2,1)} %get-tuple-element.81.q_ref, ...), custom_call_target="tpu_custom_call", output_to_operand_aliasing={{4}: (10, {})} | custom-call | flops 42949672960 | bytes 33554432 | tf_op jit(solution)/shard_map/pallas_call | solution.py:597
  373.7 0.0 copy-start.2
  373.7 28.7 %shard_map.188 = (bf16[2,512,1024]{2,1,0:T(8,128)(2,1)}, f32[2,32,512]{2,1,0:T(8,128)}) custom-call(bf16[2,4,3,256,512]{4,3,2,1,0:T(8,128)(2,1)} %get-tuple-element.68.wq_ref, f32[1024,1024]{1,0:T(8,128)} %get-tuple-element.80.dz_ref, bf16[1024,1024]{1,0:T(8,128)(2,1)} %get-tuple-element.93.dq_ref, bf16[1024,1024]{1,0:T(8,128)(2,1)} %get-tuple-element.94.dk_ref, ...), custom_call_target="tpu_custom_call" | custom-call | flops 6442450944 | bytes 16777216 | tf_op jit(solution)/shard_map/pallas_call | solution.py:888
  402.4 1.6 copy.26
  404.1 0.0 copy-done.2
  404.1 0.0 copy-start.4
  404.1 1.3 copy.34
  405.4 1.0 copy-done.4
  406.4 0.0 copy-start.3
  406.4 0.0 copy-start.1
  406.4 1.3 copy.35
  407.7 1.0 copy-done.3
  408.8 0.0 copy-start.7
  408.8 0.0 copy-start.6
  408.8 1.3 copy.36
  410.1 0.0 copy-done.7
  410.1 0.6 copy.37
  410.7 0.0 copy-done.6
  410.7 0.6 copy.38
  411.3 0.0 copy-done.1
  (1 shorter events, 0.0 us)
Async XLA Ops:
  0.6 0.7 copy-start
  10.2 97.3 %copy-start.5 = (bf16[128,256]{1,0:T(8,128)(2,1)S(1)}, bf16[128,256]{1,0:T(8,128)(2,1)}, u32[]{:S(2)}) copy-start(bf16[128,256]{1,0:T(8,128)(2,1)} %param.26) | copy-start | bytes 196612
  373.7 30.3 %copy-start.2 = (bf16[2,512,1024]{2,1,0:T(8,128)(2,1)S(1)}, bf16[2,512,1024]{2,1,0:T(8,128)(2,1)}, u32[]{:S(2)}) copy-start(bf16[2,512,1024]{2,1,0:T(8,128)(2,1)} %get-tuple-element.67) | copy-start | bytes 6291460
  404.1 2.3 copy-start.4
  406.4 2.3 copy-start.3
  406.4 4.9 %copy-start.1 = (s32[2,1,1]{0,2,1:T(1,128)S(1)}, s32[2,1,1]{0,2,1:T(1,128)}, u32[]{:S(2)}) copy-start(s32[2,1,1]{0,2,1:T(1,128)} %param.16) | copy-start | bytes 28
  408.8 1.3 copy-start.7
  408.8 2.0 copy-start.6

commit v3 on v2

--- a/solution.py
+++ b/solution.py
@@ -620,18 +620,15 @@
     )(q, k, v, a, da, il, p, *((pp, pre, moved, landed) if causal else (keep, give)))
 
 
-def erf_parts(v):
-    mag = jnp.abs(v)
+def gelu_pair(v):
+    x = 1.0 + (0.3275911 * 0.5 ** 0.5) * jnp.abs(v)
+    t = pl.reciprocal(x, approx=True)
+    t = t * (2.0 - x * t)
     expo = jnp.exp2(v * v * (-0.5 * LOG2E))
-    t = 1.0 / (1.0 + (0.3275911 * 0.5 ** 0.5) * mag)
-    poly = t * (0.254829592 + t * (-0.284496736 + t * (1.421413741 + t * (-1.453152027 + t * 1.061405429))))
-    half = 0.5 * poly * expo
-    return jnp.where(v < 0.0, half, 1.0 - half), expo * (2.0 * math.pi) ** -0.5
-
-
-def gelu_pair(v):
-    cdf, pdf = erf_parts(v)
-    return v * cdf, cdf + v * pdf
+    poly = 0.127414796 + t * (-0.142248368 + t * (0.7107068705 + t * (-0.7265760135 + t * 0.5307027145)))
+    half = poly * t * expo
+    cdf = jnp.where(v < 0.0, half, 1.0 - half)
+    return v * cdf, cdf + v * expo * (2.0 * math.pi) ** -0.5
 
 
 def normalize(z):
@@ -1003,13 +1000,21 @@
         table = {}
         table["w own"] = (own_ref, wv.at[0, 0], None)
         table["pre own"] = (pre_ref, pv.at[:, :, pl.ds(0, hw)], None)
-        for r in range(chunks):
-            cols = pl.ds(pl.multiple_of((dp ^ r) * TILE, TILE), TILE)
-            table["x own", r] = (in_ref.at[y, 0, :, cols], xv.at[rows, pl.ds(r * TILE, TILE)], None)
-            table["x up", r] = (in_ref.at[1 - y, 0, :, cols], xv.at[rows, pl.ds(r * TILE, TILE)], up)
+        table["x own"] = (in_ref.at[y, 0], xv.at[rows], None)
+        table["x up"] = (in_ref.at[1 - y, 0], xv.at[rows], up)
         table["pre up"] = (pre_ref, pv.at[:, :, pl.ds(hw, hw)], up)
-        plane_moves(table, "w", own_ref, lambda s, r: wv.at[s, r], lambda ref: ref, side, over, up)
         table["w", "side"] = (own_ref, wv.at[0, 1], side)
+        table["w", "x"] = (own_ref, wv.at[0, 2], over)
+        table["w", "x", "side"] = (wv.at[0, 2], wv.at[0, 3], side)
+        quarter = lambda k: (slice(None), pl.ds(pl.multiple_of(lax.rem(z + nz - k, nz) * (wrows // nz), wrows // nz), wrows // nz))
+        table["w", "y"] = (own_ref.at[quarter(0)], wv.at[(1, 0) + quarter(0)], up)
+        for k in range(nz):
+            beside, diagonal = wv.at[(1, 0) + quarter(k)], wv.at[(1, 2) + quarter(k)]
+            table["w", "y", k, "side"] = (beside, wv.at[(1, 1) + quarter(k)], side)
+            table["w", "d", k] = (beside, diagonal, over)
+            table["w", "d", k, "side"] = (diagonal, wv.at[(1, 3) + quarter(k)], side)
+            if k + 1 < nz:
+                table["w", "y", k, "on"] = (beside, beside, onward)
         for k in range(1, nz):
             table["ad", k] = (ad_ref, ada_ref.at[k], along[k - 1])
         plane_moves(table, "so", so_ref, lambda s, r: bso.at[s, r], lambda ref: ref, side, over, up)
@@ -1030,8 +1035,8 @@
 
     def count():
         rings = len(ring_tags) * (3 + 3 * nz + 3 * (nz - 1))
-        planes = (1 + len(plane_tags)) * 6
-        return chunks + planes + rings + nz + 5, chunks + 8
+        planes = len(plane_tags) * 6
+        return 1 + 1 + 4 + 4 * nz - 1 + planes + rings + (nz - 1) + 3 + 1, 9
 
     def kernel(in_ref, mem_ref, own_ref, so_ref, cq_ref, co_ref, pre_ref, ad_ref,
                a_ref, p_ref, pp_ref, l_ref, q_out, k_out, v_out, w_out, x_out, pre_out, bso, bcq, bco, mem_out, ada_ref,
@@ -1047,12 +1052,12 @@
             done.update(names)
             mv.got(*names)
 
-        xs_up = [("x up", r) for r in range(chunks)]
-        xs_own = [("x own", r) for r in range(chunks)]
         ads = [("ad", k) for k in range(1, nz)]
         outs = [n + " out" for n in ("q", "k", "v", "w", "x", "pre")]
 
         def pass_on(spot, k):
+            if k >= nz:
+                return
             for tag in ring_tags:
                 got((tag, spot) if k == 0 else (tag, spot, k - 1, "on"))
                 if k + 1 < nz:
@@ -1064,42 +1069,49 @@
             meet(list(near_peers) + along)
             mv.start(("w", "y"), ("w", "x"), "pre up")
             mv.start(*[(tag, spot) for tag in ring_tags for spot in "yx"])
-            mv.start(*xs_up)
-            mv.start(("w", "side"), *ads)
-            mv.start("w own", "pre own", *xs_own)
-            got(("w", "y"))
-            mv.start(("w", "d"), ("w", "y", "side"))
+            mv.start("x up", *[(tag, "y") for tag in plane_tags])
+            mv.start("mem up", ("w", "side"), "w own", "pre own", "x own")
+            for k in range(nz):
+                got(("w", "y") if k == 0 else ("w", "y", k - 1, "on"))
+                if k + 1 < nz:
+                    mv.start(("w", "y", k, "on"))
+                mv.start(("w", "d", k), ("w", "y", k, "side"))
+            pass_on("y", 0)
+            pass_on("x", 0)
+            mv.start(*[(tag, "d") for tag in ring_tags])
+            mv.start(*[(tag, "x") for tag in plane_tags])
             got(("w", "x"))
-            mv.start(("w", "x", "side"))
-            pass_on("y", 0)
-            mv.start(*[(tag, "d") for tag in ring_tags])
-            pass_on("x", 0)
-            mv.start(*[(tag, spot) for tag in plane_tags for spot in "xy"])
-            mv.start("mem up", ("so", "side"), ("cq", "side"), ("co", "side"))
-            for k in range(1, nz):
-                pass_on("y", k)
-                pass_on("x", k)
-            got(("w", "d"))
-            mv.start(("w", "d", "side"))
-            pass_on("d", 0)
-            got("w own", "pre own", "pre up", ("w", "side"), ("w", "y", "side"), ("w", "x", "side"), ("w", "d", "side"))
-            got(*xs_own)
-            got(*xs_up)
+            mv.start(("w", "x", "side"), ("so", "side"), ("cq", "side"), ("co", "side"))
+            for k in range(nz):
+                if 0 < k < nz - 1:
+                    pass_on("y", k)
+                    pass_on("x", k)
+                got(("w", "d", k))
+                mv.start(("w", "d", k, "side"))
+            got("w own", "pre own", "pre up", "x own", "x up", ("w", "side"), ("w", "x", "side"))
+            for k in range(nz):
+                got(("w", "y", k, "side"), ("w", "d", k, "side"))
             for i in range(2):
-                x = xv[i * half:(i + 1) * half]
+                x = place_cols(xv.at[pl.ds(i * half, half)], lax.axis_index("dp"))
                 for c, out in ((0, qs), (1, ks), (2, vs)):
                     for s in range(2):
                         w = jnp.concatenate([wv[s, r, c] for r in range(4)], axis=0)
                         o = dot_mm(x, w, 1, 0)
                         out[i * half:(i + 1) * half, s * hw:(s + 1) * hw] = (o * qscale if c == 0 else o).astype(BF)
-                if i + 1 < nz:
-                    pass_on("d", i + 1)
+                if i == 0:
+                    pass_on("d", 0)
+            if nz > 1:
+                pass_on("y", nz - 1)
+                pass_on("x", nz - 1)
+            pass_on("d", 1)
             mv.start(*outs)
 
-        for k in range(3, nz):
-            @pl.when(g == k - 2)
+        for k in range(2, nz):
+            @pl.when(g == 2 * (k - 1))
             def _():
                 pass_on("d", k)
+                if k == 2:
+                    mv.start(*ads)
 
         @pl.when(g == 3)
         def _():
@@ -1159,8 +1171,7 @@
     kcol = cross_qkv.shape[2] // TILE
     nq = cross_qkv.shape[0]
     orow = ffn_out.shape[0]
-    icol = ffn_in.shape[1]
-    ihalf = icol // 2
+    ihalf = ffn_in.shape[0] // 2
     qscale = HEAD_DIM ** -0.5 * LOG2E
 
     def moves(refs):
@@ -1179,12 +1190,12 @@
         table["i", "y"] = (fi_ref, cin.at[1, 0], up)
         table["i", "x"] = (fi_ref, cin.at[0, 2], over)
         one, two = pl.ds(0, ihalf), pl.ds(ihalf, ihalf)
-        table["i", "d1"] = (cin.at[1, 0, :, one], cin.at[1, 2, :, one], over)
-        table["i", "d2"] = (cin.at[0, 2, :, two], cin.at[1, 2, :, two], up)
+        table["i", "d1"] = (cin.at[1, 0, one], cin.at[1, 2, one], over)
+        table["i", "d2"] = (cin.at[0, 2, two], cin.at[1, 2, two], up)
         table["i", "y", "side"] = (cin.at[1, 0], cin.at[1, 1], side)
         table["i", "x", "side"] = (cin.at[0, 2], cin.at[0, 3], side)
-        table["i", "d1", "side"] = (cin.at[1, 2, :, one], cin.at[1, 3, :, one], side)
-        table["i", "d2", "side"] = (cin.at[1, 2, :, two], cin.at[1, 3, :, two], side)
+        table["i", "d1", "side"] = (cin.at[1, 2, one], cin.at[1, 3, one], side)
+        table["i", "d2", "side"] = (cin.at[1, 2, two], cin.at[1, 3, two], side)
         table["ad side"] = (ad_ref, ada_ref.at[1], side)
         table["ad over"] = (ad_ref, ada_ref.at[2], over)
         table["ad over side"] = (ada_ref.at[2], ada_ref.at[3], side)
@@ -1205,6 +1216,8 @@
             mv.got(*names)
 
         def pass_on(spot, k):
+            if k >= nz:
+                return
             got(("o", spot) if k == 0 else ("o", spot, k - 1, "on"))
             if k + 1 < nz:
                 mv.start(("o", spot, k, "on"))
@@ -1223,7 +1236,7 @@
         def project(i):
             rs = slice(i * half, (i + 1) * half)
             att = a_in[rs]
-            z1 = x_ref[rs].astype(F32) + jnp.concatenate(
+            z1 = place_cols(x_ref.at[pl.ds(i * half, half)], dp).astype(F32) + jnp.concatenate(
                 [nn(att, [so(s, r, j) for s in range(2) for j in range(khead)]) for r in range(chunks)], axis=1)
             u, inv = normalize(z1)
             u_ref[rs] = u
@@ -1242,33 +1255,33 @@
             for c in loads():
                 c.start()
             meet(peers)
-            mv.start(("o", "y"), ("o", "x"), ("i", "y"), ("i", "side"), ("o", "side"), "ad side")
+            mv.start(("o", "y"), ("o", "x"), ("i", "y"), "cot", ("o", "side"), ("i", "side"), "ad side")
+            pass_on("y", 0)
+            mv.start(("o", "d"), ("i", "x"))
+            pass_on("x", 0)
             for c in loads():
                 c.wait()
             project(0)
-            pass_on("y", 0)
-            mv.start(("o", "d"), ("i", "x"), "ad over", "cot")
-            pass_on("x", 0)
+            pass_on("d", 0)
+            pass_on("y", 1)
+            pass_on("x", 1)
             project(1)
-            pass_on("d", 0)
+            pass_on("d", 1)
+            got(("i", "y"))
+            mv.start(("i", "d1"), ("i", "y", "side"), "ad over")
             mv.start(*outs)
 
-        for k in range(1, nz):
-            @pl.when(g == 3 * k - 2)
+        for k in range(2, nz):
+            @pl.when(g == 5 * k - 8)
             def _():
                 pass_on("y", k)
                 pass_on("x", k)
 
-            @pl.when(g == 3 * k - 1)
+            @pl.when(g == 4 * k - 4)
             def _():
                 pass_on("d", k)
 
         @pl.when(g == 3)
-        def _():
-            got(("i", "y"))
-            mv.start(("i", "d1"), ("i", "y", "side"))
-
-        @pl.when(g == 6)
         def _():
             got(("i", "x"))
             mv.start(("i", "d2"), ("i", "x", "side"))
@@ -1377,23 +1390,41 @@
         h2b = h2.astype(BF)
         need(1)
         order = [(s, j) for s in range(2) for j in range(kin)]
-        ahead = nn(h2b, [fi(0, r, 0) for r in range(4)])
-        for i in range(hid):
-            g = ahead
-            if i + 1 < hid:
-                s, j = order[i + 1]
-                ahead = nn(h2b, [fi(s, r, j) for r in range(4)])
-            act, slope = gelu_pair(g)
-            act_ref[:, i * TILE:(i + 1) * TILE] = act.astype(BF)
-            slope_ref[:, i * TILE:(i + 1) * TILE] = slope.astype(BF)
+        acc = outs[0]
         down_t = jnp.concatenate([stack_cols([down(r, kk) for r in range(4)]) for kk in range(nz)], axis=0)
         up_m = jnp.concatenate([stack_cols([upw(r, kk) for r in range(4)]) for kk in range(nz)], axis=0)
-        act_a, slope_a = gelu_pair(dot_mm(h2b, down_t, 1, 1))
+        span = 256
+        spans = [(s, j) for s in range(2) for j in range(kin * TILE // span)]
+
+        def grow(i):
+            s, j = spans[i]
+            return nn(h2b, [W[1].at[s, r, slice(None), pl.ds(j * span, span)] for r in range(4)])
+
+        def fall(i):
+            s, j = spans[i]
+            w = jnp.concatenate([W[2][s, r, j * span:(j + 1) * span] for r in range(4)], axis=1)
+            return dot_mm(act_ref[:, i * span:(i + 1) * span], w, 1, 0)
+
+        def bend(i, g):
+            act, slope = gelu_pair(g)
+            act_ref[:, i * span:(i + 1) * span] = act.astype(BF)
+            slope_ref[:, i * span:(i + 1) * span] = slope.astype(BF)
+
+        ahead = grow(0)
+        g_a = dot_mm(h2b, down_t, 1, 1)
+        act_a, slope_a = gelu_pair(g_a)
         act_a = act_a.astype(BF)
         need(2)
-        acts = act_ref[...]
-        z3 = h2 + 4.0 * dot_mm(act_a, up_m, 1, 0) + jnp.concatenate(
-            [nn(acts, out_rows(fo, r, kin)) for r in range(chunks)], axis=1)
+        for i in range(len(spans)):
+            g = ahead
+            if i + 1 < len(spans):
+                ahead = grow(i + 1)
+            if i == 1:
+                acc[...] = h2 + fall(0)
+            elif i > 1:
+                acc[...] += fall(i - 1)
+            bend(i, g)
+        z3 = acc[...] + fall(len(spans) - 1) + 4.0 * dot_mm(act_a, up_m, 1, 0)
         u3, inv3 = normalize(z3)
         put(u3 * g3[...])
         in_own = pl.program_id(0) // (half // tile) == y

time: 418 us -> 404 us (0.967)
  Pallas kernels: 391 us -> 378 us
    pallas_call x1, Pallas kernels: 97.3 us -> 90 us  [self_forward(): pl.pallas_call(kernel, grid=(pairs + 1,), in_specs=[HBM] * 8, out_specs=[...]
    pallas_call x2, Pallas kernels: 96.4 us -> 89.9 us  [tiled(): pl.pallas_call(kernel, grid=(steps,), in_specs=[HBM] * (2 * nw) + [spec f...]
where the time goes in v3:
time: 404 us; the launch traced here: 398 us
  Pallas kernels  378 us (94%)
  local copies, waits for them, and re-layouts  15 us (4%)
  other arithmetic  4.14 us (1%)
    pallas_call x1, Pallas kernels, self_forward(): pl.pallas_call(kernel, grid=(pairs + 1,), in_specs=[HBM] * 8, out_specs=[...  90 us
    pallas_call x2, Pallas kernels, tiled(): pl.pallas_call(kernel, grid=(steps,), in_specs=[HBM] * (2 * nw) + [spec f...  89.9 us
    pallas_call x2, Pallas kernels, attn_bwd(): pl.pallas_call(functools.partial(attn_bwd_body, causal), grid=(pairs,), i...  80.6 us
    pallas_call x1, Pallas kernels, cross_forward(): pl.pallas_call(kernel, grid=(pairs + 1,), in_specs=[pl.BlockSpec(memory_s...  77.4 us
    pallas_call x1, Pallas kernels, last_gradient(): pl.pallas_call(kernel, in_specs=[HBM] * 6, out_specs=[HBM, pl.BlockSpec(m...  28.7 us
    pallas_call x1, Pallas kernels, whole_sequences(): pl.pallas_call(memory_back, grid_spec=pltpu.PrefetchScalarGridSpec(num_sc...  11 us
    unnamed x24, local copies, waits for them, and re-layouts  10.7 us

profile of v3, /device:TPU:0, one launch (start us, length us, event | category | flops | bytes accessed | tf_op | source)
XLA Modules:
  0.0 397.6 jit_solution(13659014129950225484)
XLA Ops:
  0.6 0.0 copy-start
  0.7 0.7 pad_add_fusion.sc
  1.3 0.0 copy-done
  1.3 0.6 constant_dynamic-slice_fusion.4
  1.9 0.7 convert_element_type.5
  2.6 0.6 pad_maximum_fusion.1
  3.2 0.8 copy.21
  4.1 0.6 pad.4.pre_ref
  4.7 0.9 copy.22
  5.7 1.5 pad_maximum_fusion.ad_ref
  7.2 3.0 dynamic-slice_bitcast_fusion
  10.2 0.0 copy-start.5
  10.2 90.0 %shard_map.181 = (bf16[1024,1024]{1,0:T(8,128)(2,1)}, bf16[16,1024,1024]{2,1,0:T(8,128)(2,1)}, bf16[16,32,1024]{2,1,0:T(8,128)(2,1)}, f32[8,2,1024]{2,1,0:T(2,12...) custom-call(bf16[2,1,512,1024]{3,2,1,0:T(8,128)(2,1)} %in_ref.1, ...), custom_call_target="tpu_custom_call" | custom-call | flops 99999997952 | bytes 100000000 | tf_op jit(solution)/shard_map/pallas_call | solution.py:1144
  100.2 0.0 copy-done.5
  100.2 0.7 bitcast_dynamic-update-slice_fusion.ad_ref.refs_13_
  100.9 77.4 %shard_map.182 = (bf16[1024,1024]{1,0:T(8,128)(2,1)}, bf16[16,1024,1024]{2,1,0:T(8,128)(2,1)}, f32[8,2,1024]{2,1,0:T(2,128)}, f32[1024,1024]{1,0:T(8,128)}, f32[...) custom-call(s32[1]{0:T(128)} %bitcast.1.n_ref, ...), custom_call_target="tpu_custom_call" | custom-call | flops 99999997952 | bytes 100000000 | tf_op jit(solution)/shard_map/pallas_call | solution.py:1318
  178.3 77.6 %shard_map.183 = (f32[1024,1024]{1,0:T(8,128)}, bf16[1024,1024]{1,0:T(8,128)(2,1)}, f32[2,2,512,256]{3,2,1,0:T(8,128)}, bf16[2,2,512,256]{3,2,1,0:T(8,128)(2,1)}, bf16[2,512,1024]{2,1,0:T(8,128)(2,1)}) custom-call(bf16[512,256]{1,0:T(8,128)(2,1)} %refs_0_.2, bf16[2,4,512,256]{3,2,1,0:T(8,128)(2,1)} %get-tuple-element.54.refs_1_, bf16[256,2048]{1,0:T(8,128)(2,1)} %refs_2_.2, ...), custom_call_target="tpu_custom_call" | custom-call | flops 34359738368 | bytes 16777216 | tf_op jit(solution)/shard_map/pallas_call | solution.py:777
  255.9 44.4 %shard_map.184 = (bf16[1024,1024]{1,0:T(8,128)(2,1)}, bf16[1024,1024]{1,0:T(8,128)(2,1)}, bf16[1024,1024]{1,0:T(8,128)(2,1)}, f32[128,128]{1,0:T(8,128)}, f32[128,128]{1,0:T(8,128)}) custom-call(bf16[1024,1024]{1,0:T(8,128)(2,1)} %get-tuple-element.70.q_ref, bf16[1024,1024]{1,0:T(8,128)(2,1)} %get-tuple-element.71.k_ref, ...), custom_call_target="tpu_custom_call" | custom-call | flops 42949672960 | bytes 33554432 | tf_op jit(solution)/shard_map/pallas_call | solution.py:597
  300.3 12.2 %shard_map.185 = (f32[1024,1024]{1,0:T(8,128)}, bf16[1024,1024]{1,0:T(8,128)(2,1)}) custom-call(bf16[3,256,512]{2,1,0:T(8,128)(2,1)} %own.1, bf16[2,4,3,256,512]{4,3,2,1,0:T(8,128)(2,1)} %get-tuple-element.59.bcq.refs_1_.far, bf16[512,256]{1,0:T(8,128)(2,1)} %refs_2_.3, bf16[2,4,512,256]{3,2,1,0:T(8,128)(2,1)} %get-tuple-element.58.bso.refs_3_, ...), custom_call_target="tpu_custom_call" | custom-call | flops 4294967296 | bytes 16777216 | tf_op jit(solution)/shard_map/pallas_call | solution.py:777
  312.6 11.0 %shard_map.186 = (bf16[2,512,1024]{2,1,0:T(8,128)(2,1)}, bf16[512,1024]{1,0:T(8,128)(2,1)}) custom-call(s32[2]{0:T(128)} %pad_add_fusion.sc, bf16[3,256,512]{2,1,0:T(8,128)(2,1)} %own.1, bf16[2,4,3,256,512]{4,3,2,1,0:T(8,128)(2,1)} %get-tuple-element.59.bcq.refs_1_.far, bf16[1024,1024]{1,0:T(8,128)(2,1)} %get-tuple-element.89.dk_ref, ...), custom_call_target="tpu_custom_call" | custom-call | flops 4294967296 | bytes 16777216 | tf_op jit(solution)/shard_map/pallas_call | solution.py:1512
  323.5 36.2 %shard_map.187 = (bf16[1024,1024]{1,0:T(8,128)(2,1)}, bf16[1024,1024]{1,0:T(8,128)(2,1)}, bf16[1024,1024]{1,0:T(8,128)(2,1)}, f32[2,32,1024]{2,1,0:T(8,128)}, bf16[2,512,1024]{2,1,0:T(8,128)(2,1)}) custom-call(bf16[1024,1024]{1,0:T(8,128)(2,1)} %get-tuple-element.81.q_ref, ...), custom_call_target="tpu_custom_call", output_to_operand_aliasing={{4}: (10, {})} | custom-call | flops 42949672960 | bytes 33554432 | tf_op jit(solution)/shard_map/pallas_call | solution.py:597
  359.8 0.0 copy-start.2
  359.8 28.7 %shard_map.188 = (bf16[2,512,1024]{2,1,0:T(8,128)(2,1)}, f32[2,32,512]{2,1,0:T(8,128)}) custom-call(bf16[2,4,3,256,512]{4,3,2,1,0:T(8,128)(2,1)} %get-tuple-element.68.wq_ref, f32[1024,1024]{1,0:T(8,128)} %get-tuple-element.80.dz_ref, bf16[1024,1024]{1,0:T(8,128)(2,1)} %get-tuple-element.93.dq_ref, bf16[1024,1024]{1,0:T(8,128)(2,1)} %get-tuple-element.94.dk_ref, ...), custom_call_target="tpu_custom_call" | custom-call | flops 6442450944 | bytes 16777216 | tf_op jit(solution)/shard_map/pallas_call | solution.py:885
  388.5 1.6 copy.26
  390.1 0.0 copy-done.2
  390.1 0.0 copy-start.4
  390.1 1.3 copy.34
  391.4 1.0 copy-done.4
  392.5 0.0 copy-start.3
  392.5 0.0 copy-start.1
  392.5 1.3 copy.35
  393.8 1.0 copy-done.3
  394.8 0.0 copy-start.7
  394.8 0.0 copy-start.6
  394.8 1.3 copy.36
  396.1 0.0 copy-done.7
  396.1 0.6 copy.37
  396.8 0.0 copy-done.6
  396.8 0.6 copy.38
  397.4 0.0 copy-done.1
  (1 shorter events, 0.0 us)
Async XLA Ops:
  0.6 0.7 copy-start
  10.2 90.0 %copy-start.5 = (bf16[128,256]{1,0:T(8,128)(2,1)S(1)}, bf16[128,256]{1,0:T(8,128)(2,1)}, u32[]{:S(2)}) copy-start(bf16[128,256]{1,0:T(8,128)(2,1)} %param.26) | copy-start | bytes 196612
  359.8 30.3 %copy-start.2 = (bf16[2,512,1024]{2,1,0:T(8,128)(2,1)S(1)}, bf16[2,512,1024]{2,1,0:T(8,128)(2,1)}, u32[]{:S(2)}) copy-start(bf16[2,512,1024]{2,1,0:T(8,128)(2,1)} %get-tuple-element.67) | copy-start | bytes 6291460
  390.1 2.3 copy-start.4
  392.5 2.3 copy-start.3
  392.5 4.9 %copy-start.1 = (s32[2,1,1]{0,2,1:T(1,128)S(1)}, s32[2,1,1]{0,2,1:T(1,128)}, u32[]{:S(2)}) copy-start(s32[2,1,1]{0,2,1:T(1,128)} %param.16) | copy-start | bytes 28
  394.8 1.3 copy-start.7
  394.8 2.0 copy-start.6

commit v4 on v3

--- a/solution.py
+++ b/solution.py
@@ -1161,7 +1161,7 @@
     )(inputs, memory, self_qkv, self_proj, cross_qkv, cross_proj, pre_own, ad_own)
 
 
-def cross_forward(src_n, x_full, a, mem_mine, mem_got, self_proj, b_so, cross_qkv, b_cq, ad_col, cotangent, ffn_in, ffn_out, gain):
+def cross_forward(src_n, x_full, a, memory, mem_got, self_proj, b_so, cross_qkv, b_cq, ad_col, cotangent, ffn_in, ffn_out, gain):
     t, d = x_full.shape
     half = t // 2
     nz = lax.axis_size("adp")
@@ -1202,9 +1202,9 @@
         table["cot"] = (cot_ref.at[1 - y, 0], cot_out, up)
         return table, [side, over, up, onward, before]
 
-    def kernel(n_ref, x_ref, a_in, gain_ref, memo_ref, memg_ref, so_ref, bso, cq_ref, bcq, ad_ref, cot_ref, fi_ref, fo_ref,
+    def kernel(n_ref, x_ref, a_in, gain_ref, memg_ref, mem_ref, so_ref, bso, cq_ref, bcq, ad_ref, cot_ref, fi_ref, fo_ref,
                ac_ref, p_ref, l_ref, u_ref, inv_ref, q_out, k_out, v_out, cin, cout, ada_ref, cot_out,
-               sov, cqv, qs, ks, vs, send, recv, local, wsem):
+               sov, cqv, memo_ref, qs, ks, vs, send, recv, local, wsem):
         g = pl.program_id(0)
         dp, y = lax.axis_index("dp"), lax.axis_index("mp")
         table, peers = moves((ad_ref, cot_ref, fi_ref, fo_ref, q_out, k_out, v_out, cin, cout, ada_ref, cot_out, qs, ks, vs))
@@ -1226,6 +1226,7 @@
         outs = [n + " out" for n in ("q", "k", "v")]
 
         def loads():
+            yield pltpu.make_async_copy(mem_ref.at[y, 0], memo_ref, wsem.at[2, 0])
             for i, (own, far, dst) in enumerate(((so_ref, bso, sov), (cq_ref, bcq, cqv))):
                 yield pltpu.make_async_copy(own, dst.at[0, 0], wsem.at[i, 0])
                 yield pltpu.make_async_copy(far.at[0, pl.ds(1, 3)], dst.at[0, pl.ds(1, 3)], wsem.at[i, 1])
@@ -1318,8 +1319,8 @@
     return pl.pallas_call(
         kernel,
         grid=(pairs + 1,),
-        in_specs=[pl.BlockSpec(memory_space=pltpu.SMEM), whole(t, d), whole(t, d), whole(1, d), whole(half, d), whole(half, d)]
-        + [HBM] * 8,
+        in_specs=[pl.BlockSpec(memory_space=pltpu.SMEM), whole(t, d), whole(t, d), whole(1, d), whole(half, d)]
+        + [HBM] * 9,
         out_specs=[pl.BlockSpec((t, 128), col), pl.BlockSpec((2, t, t), lead), pl.BlockSpec((1, 2, t), lead),
                    pl.BlockSpec((t, d), fixed), pl.BlockSpec((t, 1), fixed)] + [HBM] * 7,
         out_shape=[
@@ -1327,12 +1328,12 @@
             shape((t, d), BF), shape((t, d), BF), shape((t, d), BF), shape((2, 4) + ffn_in.shape, BF), shape((2, 4) + ffn_out.shape, BF),
             shape((4,) + ad_col.shape, BF), shape((half, d), BF),
         ],
-        scratch_shapes=[vm((2, 4) + self_proj.shape, BF), vm((2, 4) + cross_qkv.shape, BF), vm((t, d), BF), vm((t, d), BF), vm((t, d), BF),
+        scratch_shapes=[vm((2, 4) + self_proj.shape, BF), vm((2, 4) + cross_qkv.shape, BF), vm((half, d), BF), vm((t, d), BF), vm((t, d), BF), vm((t, d), BF),
                         pltpu.SemaphoreType.DMA((remotes,)), pltpu.SemaphoreType.DMA((remotes,)),
-                        pltpu.SemaphoreType.DMA((near,)), pltpu.SemaphoreType.DMA((2, 3))],
+                        pltpu.SemaphoreType.DMA((near,)), pltpu.SemaphoreType.DMA((3, 3))],
         compiler_params=pltpu.CompilerParams(collective_id=1, has_side_effects=True, vmem_limit_bytes=VMEM_BYTES),
         cost_estimate=pl.CostEstimate(flops=10**11, bytes_accessed=10**8, transcendentals=0),
-    )(src_n, x_full, a, gain, mem_mine, mem_got, self_proj, b_so, cross_qkv, b_cq, ad_col, cotangent, ffn_in, ffn_out)
+    )(src_n, x_full, a, gain, mem_got, memory, self_proj, b_so, cross_qkv, b_cq, ad_col, cotangent, ffn_in, ffn_out)
 
 
 def whole_sequences(inputs, memory, src_lengths, self_qkv, self_proj, cross_qkv, cross_proj, ffn_in, ffn_out,
@@ -1342,7 +1343,6 @@
     half, d = inputs.shape[2], inputs.shape[3]
     t = 2 * half
     chunks = d // TILE
-    mine = lambda a: lax.dynamic_index_in_dim(a, y, 0, keepdims=False)[0]
     rel = lambda a: jnp.concatenate(
         [lax.dynamic_slice_in_dim(a, (dp ^ r) * TILE, TILE, axis=a.ndim - 1) for r in range(chunks)], axis=-1)
 
@@ -1364,7 +1364,7 @@
     w_cq = lambda c: (cross_qkv, b_cq, c)
     out_rows = lambda T, r, n: [T(s, r, j) for s in range(2) for j in range(n)]
     ac, p_c, il_c, u1, inv1, qc, kc, vc, c_in, c_out, ad_all, cot_got = cross_forward(
-        src_n, x_full, a, mine(memory), mem_got, self_proj, b_so, cross_qkv, b_cq, ad_col, cotangent, ffn_in, ffn_out, gain[0])
+        src_n, x_full, a, memory, mem_got, self_proj, b_so, cross_qkv, b_cq, ad_col, cotangent, ffn_in, ffn_out, gain[0])
     fixed = lambda i: (0, 0)
     spec = lambda shape, index: pl.BlockSpec(shape, index)
     held = lambda *shape: pl.BlockSpec(shape, lambda i: (0,) * len(shape), pipeline_mode=pl.Buffered(1))
@@ -1375,8 +1375,15 @@
 
     def feed(W, need, rows, consts, outs, scr, put):
         dp, y = lax.axis_index("dp"), lax.axis_index("mp")
-        ac_ref, u1_ref, cot_a, cot_b = rows
-        act_ref, slope_ref, terms = scr
+        ac_ref, u1_ref, cot_hbm, cot_b = rows
+        act_ref, slope_ref, terms, cot_own, cot_sem = scr
+        cot_a = cot_own.at[pl.ds(pl.multiple_of(lax.rem(pl.program_id(0), half // tile) * tile, tile), tile)]
+        cot_load = pltpu.make_async_copy(cot_hbm.at[y, 0], cot_own, cot_sem.at[0])
+
+        @pl.when(pl.program_id(0) == 0)
+        def _():
+            cot_load.start()
+
         g1, g2, g3 = consts[:3]
         co, fi, fo = by_rows(W[0]), by_cols(W[1]), by_rows(W[2])
         down = lambda r, kk: (consts[3].at[kk] if r == 0 else consts[4].at[r, kk]).at[pl.ds(0, n_ad)]
@@ -1427,6 +1434,11 @@
         z3 = acc[...] + fall(len(spans) - 1) + 4.0 * dot_mm(act_a, up_m, 1, 0)
         u3, inv3 = normalize(z3)
         put(u3 * g3[...])
+
+        @pl.when(pl.program_id(0) == 0)
+        def _():
+            cot_load.wait()
+
         in_own = pl.program_id(0) // (half // tile) == y
         cot = jnp.where(in_own, place_cols(cot_a, dp), place_cols(cot_b, dp)).astype(F32)
         dz3 = norm_back(cot, u3, inv3, g3[...])
@@ -1469,14 +1481,15 @@
     part = lambda i: (i % (half // tile), 0)
     dz2, dac, keep, give, result = tiled(
         [w_co, (ffn_in, c_in, None), (ffn_out, c_out, None)],
-        [(ac, spec((tile, d), row)), (u1, spec((tile, d), row)), (mine(cotangent), spec((tile, d), part)),
+        [(ac, spec((tile, d), row)), (u1, spec((tile, d), row)), (cotangent, HBM),
          (cot_got, spec((tile, d), part))],
         gain + [ad_col, ad_all],
         [((t, d), F32, (tile, d), row), ((t, d), BF, (tile, d), row),
          ((2, 2, nz * n_ad, TILE), F32, (2, 2, nz * n_ad, TILE), lambda i: (0, 0, 0, 0)),
          ((2, 2, nz * n_ad, TILE), BF, (2, 2, nz * n_ad, TILE), lambda i: (0, 0, 0, 0))],
         feed, tile, t // tile, exchange=(2, half, d),
-        scratch=[pltpu.VMEM((tile, hid * TILE), BF)] * 2 + [pltpu.VMEM((2, nz * n_ad, d), F32)], flops=4 * 2 * t * d * hid * TILE)
+        scratch=[pltpu.VMEM((tile, hid * TILE), BF)] * 2 + [pltpu.VMEM((2, nz * n_ad, d), F32), pltpu.VMEM((half, d), BF), pltpu.SemaphoreType.DMA((1,))],
+        flops=4 * 2 * t * d * hid * TILE)
 
     dqc, dkc, dvc, down_grad, up_grad = attn_bwd(qc, kc, vc, ac, dac, il_c, p_c, keep=keep, give=give)
 

time: 404 us -> 401 us (level)
  no operation moved by 1% of the time
where the time goes in v4:
time: 401 us; the launch traced here: 394 us
  Pallas kernels  377 us (94%)
  local copies, waits for them, and re-layouts  11.9 us (3%)
  other arithmetic  4.14 us (1%)
    pallas_call x1, Pallas kernels, self_forward(): pl.pallas_call(kernel, grid=(pairs + 1,), in_specs=[HBM] * 8, out_specs=[...  90 us
    pallas_call x2, Pallas kernels, tiled(): pl.pallas_call(kernel, grid=(steps,), in_specs=[HBM] * (2 * nw) + [spec f...  89.9 us
    pallas_call x2, Pallas kernels, attn_bwd(): pl.pallas_call(functools.partial(attn_bwd_body, causal), grid=(pairs,), i...  80.6 us
    pallas_call x1, Pallas kernels, cross_forward(): pl.pallas_call(kernel, grid=(pairs + 1,), in_specs=[pl.BlockSpec(memory_s...  77.2 us
    pallas_call x1, Pallas kernels, last_gradient(): pl.pallas_call(kernel, in_specs=[HBM] * 6, out_specs=[HBM, pl.BlockSpec(m...  28.7 us
    pallas_call x1, Pallas kernels, whole_sequences(): pl.pallas_call(memory_back, grid_spec=pltpu.PrefetchScalarGridSpec(num_sc...  11 us
    unnamed x24, local copies, waits for them, and re-layouts  10.7 us

profile of v4, /device:TPU:0, one launch (start us, length us, event | category | flops | bytes accessed | tf_op | source)
XLA Modules:
  0.0 394.4 jit_solution(5674282683764899809)
XLA Ops:
  0.6 0.0 copy-start
  0.7 0.7 pad_add_fusion.sc
  1.3 0.0 copy-done
  1.3 0.6 constant_dynamic-slice_fusion.4
  1.9 0.7 convert_element_type.5
  2.6 0.6 pad_maximum_fusion.1
  3.2 0.8 copy.21
  4.1 0.6 pad.4.pre_ref
  4.7 0.9 copy.22
  5.7 1.5 pad_maximum_fusion.ad_ref
  7.2 0.0 copy-start.5
  7.2 90.0 %shard_map.181 = (bf16[1024,1024]{1,0:T(8,128)(2,1)}, bf16[16,1024,1024]{2,1,0:T(8,128)(2,1)}, bf16[16,32,1024]{2,1,0:T(8,128)(2,1)}, f32[8,2,1024]{2,1,0:T(2,12...) custom-call(bf16[2,1,512,1024]{3,2,1,0:T(8,128)(2,1)} %in_ref.1, ...), custom_call_target="tpu_custom_call" | custom-call | flops 99999997952 | bytes 100000000 | tf_op jit(solution)/shard_map/pallas_call | solution.py:1144
  97.2 0.0 copy-done.5
  97.2 0.7 bitcast_dynamic-update-slice_fusion.ad_ref.refs_13_
  97.8 77.2 %shard_map.182 = (bf16[1024,1024]{1,0:T(8,128)(2,1)}, bf16[16,1024,1024]{2,1,0:T(8,128)(2,1)}, f32[8,2,1024]{2,1,0:T(2,128)}, f32[1024,1024]{1,0:T(8,128)}, f32[...) custom-call(s32[1]{0:T(128)} %bitcast.1.n_ref, ...), custom_call_target="tpu_custom_call" | custom-call | flops 99999997952 | bytes 100000000 | tf_op jit(solution)/shard_map/pallas_call | solution.py:1319
  175.1 77.7 %shard_map.183 = (f32[1024,1024]{1,0:T(8,128)}, bf16[1024,1024]{1,0:T(8,128)(2,1)}, f32[2,2,512,256]{3,2,1,0:T(8,128)}, bf16[2,2,512,256]{3,2,1,0:T(8,128)(2,1)}, bf16[2,512,1024]{2,1,0:T(8,128)(2,1)}) custom-call(bf16[512,256]{1,0:T(8,128)(2,1)} %refs_0_.2, bf16[2,4,512,256]{3,2,1,0:T(8,128)(2,1)} %get-tuple-element.54.refs_1_, bf16[256,2048]{1,0:T(8,128)(2,1)} %refs_2_.2, ...), custom_call_target="tpu_custom_call" | custom-call | flops 34359738368 | bytes 16777216 | tf_op jit(solution)/shard_map/pallas_call | solution.py:777
  252.7 44.4 %shard_map.184 = (bf16[1024,1024]{1,0:T(8,128)(2,1)}, bf16[1024,1024]{1,0:T(8,128)(2,1)}, bf16[1024,1024]{1,0:T(8,128)(2,1)}, f32[128,128]{1,0:T(8,128)}, f32[128,128]{1,0:T(8,128)}) custom-call(bf16[1024,1024]{1,0:T(8,128)(2,1)} %get-tuple-element.70.q_ref, bf16[1024,1024]{1,0:T(8,128)(2,1)} %get-tuple-element.71.k_ref, ...), custom_call_target="tpu_custom_call" | custom-call | flops 42949672960 | bytes 33554432 | tf_op jit(solution)/shard_map/pallas_call | solution.py:597
  297.2 12.2 %shard_map.185 = (f32[1024,1024]{1,0:T(8,128)}, bf16[1024,1024]{1,0:T(8,128)(2,1)}) custom-call(bf16[3,256,512]{2,1,0:T(8,128)(2,1)} %own.1, bf16[2,4,3,256,512]{4,3,2,1,0:T(8,128)(2,1)} %get-tuple-element.59.bcq.refs_1_.far, bf16[512,256]{1,0:T(8,128)(2,1)} %refs_2_.3, bf16[2,4,512,256]{3,2,1,0:T(8,128)(2,1)} %get-tuple-element.58.bso.refs_3_, ...), custom_call_target="tpu_custom_call" | custom-call | flops 4294967296 | bytes 16777216 | tf_op jit(solution)/shard_map/pallas_call | solution.py:777
  309.4 11.0 %shard_map.186 = (bf16[2,512,1024]{2,1,0:T(8,128)(2,1)}, bf16[512,1024]{1,0:T(8,128)(2,1)}) custom-call(s32[2]{0:T(128)} %pad_add_fusion.sc, bf16[3,256,512]{2,1,0:T(8,128)(2,1)} %own.1, bf16[2,4,3,256,512]{4,3,2,1,0:T(8,128)(2,1)} %get-tuple-element.59.bcq.refs_1_.far, bf16[1024,1024]{1,0:T(8,128)(2,1)} %get-tuple-element.89.dk_ref, ...), custom_call_target="tpu_custom_call" | custom-call | flops 4294967296 | bytes 16777216 | tf_op jit(solution)/shard_map/pallas_call | solution.py:1525
  320.4 36.2 %shard_map.187 = (bf16[1024,1024]{1,0:T(8,128)(2,1)}, bf16[1024,1024]{1,0:T(8,128)(2,1)}, bf16[1024,1024]{1,0:T(8,128)(2,1)}, f32[2,32,1024]{2,1,0:T(8,128)}, bf16[2,512,1024]{2,1,0:T(8,128)(2,1)}) custom-call(bf16[1024,1024]{1,0:T(8,128)(2,1)} %get-tuple-element.81.q_ref, ...), custom_call_target="tpu_custom_call", output_to_operand_aliasing={{4}: (10, {})} | custom-call | flops 42949672960 | bytes 33554432 | tf_op jit(solution)/shard_map/pallas_call | solution.py:597
  356.6 0.0 copy-start.2
  356.6 28.7 %shard_map.188 = (bf16[2,512,1024]{2,1,0:T(8,128)(2,1)}, f32[2,32,512]{2,1,0:T(8,128)}) custom-call(bf16[2,4,3,256,512]{4,3,2,1,0:T(8,128)(2,1)} %get-tuple-element.68.wq_ref, f32[1024,1024]{1,0:T(8,128)} %get-tuple-element.80.dz_ref, bf16[1024,1024]{1,0:T(8,128)(2,1)} %get-tuple-element.93.dq_ref, bf16[1024,1024]{1,0:T(8,128)(2,1)} %get-tuple-element.94.dk_ref, ...), custom_call_target="tpu_custom_call" | custom-call | flops 6442450944 | bytes 16777216 | tf_op jit(solution)/shard_map/pallas_call | solution.py:885
  385.3 1.6 copy.26
  386.9 0.0 copy-done.2
  386.9 0.0 copy-start.4
  386.9 1.3 copy.34
  388.2 1.0 copy-done.4
  389.3 0.0 copy-start.3
  389.3 0.0 copy-start.1
  389.3 1.3 copy.35
  390.6 1.0 copy-done.3
  391.6 0.0 copy-start.7
  391.6 0.0 copy-start.6
  391.6 1.3 copy.36
  392.9 0.0 copy-done.7
  393.0 0.6 copy.37
  393.6 0.0 copy-done.6
  393.6 0.6 copy.38
  394.2 0.0 copy-done.1
  (1 shorter events, 0.0 us)
Async XLA Ops:
  0.6 0.7 copy-start
  7.2 90.0 %copy-start.5 = (bf16[128,256]{1,0:T(8,128)(2,1)S(1)}, bf16[128,256]{1,0:T(8,128)(2,1)}, u32[]{:S(2)}) copy-start(bf16[128,256]{1,0:T(8,128)(2,1)} %param.26) | copy-start | bytes 196612
  356.6 30.3 %copy-start.2 = (bf16[2,512,1024]{2,1,0:T(8,128)(2,1)S(1)}, bf16[2,512,1024]{2,1,0:T(8,128)(2,1)}, u32[]{:S(2)}) copy-start(bf16[2,512,1024]{2,1,0:T(8,128)(2,1)} %get-tuple-element.67) | copy-start | bytes 6291460
  386.9 2.3 copy-start.4
  389.3 2.3 copy-start.3
  389.3 4.9 %copy-start.1 = (s32[2,1,1]{0,2,1:T(1,128)S(1)}, s32[2,1,1]{0,2,1:T(1,128)}, u32[]{:S(2)}) copy-start(s32[2,1,1]{0,2,1:T(1,128)} %param.16) | copy-start | bytes 28
  391.6 1.3 copy-start.7
  391.6 2.0 copy-start.6
